TPU v7x, 512 devices: a whole 4x8x8 slice. The times are simulated.
512 devices in a mesh: ctx: 64 (over y, x, core), kvh: 8 (over z).
Axes of the slice: x: 4, y: 8, z: 8, core: 2. Of those that a mesh axis runs over, the one named last changes fastest.
Arguments:
- query_states: bfloat16 [65536, 8192], P('ctx', 'kvh')
- key_states: bfloat16 [65536, 1024], P('ctx', 'kvh')
- value_states: bfloat16 [65536, 1024], P('ctx', 'kvh'), may hold values from -6 to 6
- verticals: int32 [8, 4], P('kvh'), may hold values from 0 to 511, as said below
- slashes: int32 [8, 8], P('kvh'), may hold values from 1 to 24, as said below
Outputs:
- attended: bfloat16 [65536, 8192], P(('ctx', 'kvh'))
Inputs may be any that keep to these rules, and one draw needn't show every extreme that they name: `verticals`: some head's list holds block 0 and some head's list holds block 511. `slashes`: every head's list holds the offset 24.
All inputs are finite; a program needn't handle non-finite values.
Results may differ from a plain program's by a relative error of at most 0.0049.
Values may be sent and summed in bfloat16 or wider, within the bound.
No kernel may reach another device: no remote copies, remote signals or barrier semaphores. Data moves between devices by JAX's collectives and lax.ppermute only.
A program may use at most 64 MiB of HBM per device.

v0:
```python
import jax
import jax.numpy as jnp
from jax import lax
from jax.sharding import PartitionSpec as P

HD = 128
BLK = 128
REACH = 3


def from_behind(value, axis, steps):
    count = lax.axis_size(axis)
    leading, last = (max(0, -steps), min(count, count - steps))
    return lax.ppermute(value, axis, [(source, source + steps) for source in range(leading, last)])


def candidates(block_now, slash_row, vert_row):
    block_ids = jnp.concatenate([block_now[None], block_now - slash_row, vert_row])
    count = block_ids.shape[0]
    order = jnp.arange(count, dtype=jnp.int32)
    same_id = block_ids[:, None] == block_ids[None, :]
    earlier = order[None, :] < order[:, None]
    repeated = jnp.any(same_id & earlier, axis=1)
    live = (block_ids >= 0) & (block_ids <= block_now) & jnp.logical_not(repeated)
    return (block_ids, live)


def attend_block(query_block, key_cand, value_cand, live):
    scores = jnp.einsum(
        "tgd,kd->gtk", query_block, key_cand, preferred_element_type=jnp.float32
    ) * HD ** (-0.5)
    width = key_cand.shape[0]
    query_pos = lax.broadcasted_iota(jnp.int32, (BLK, width), 0)
    key_pos = lax.broadcasted_iota(jnp.int32, (BLK, width), 1)
    cand_index = key_pos // BLK
    within = key_pos % BLK
    allowed = live[cand_index] & ((cand_index > 0) | (within <= query_pos))
    masked = jnp.where(allowed[None], scores, -1e30)
    row_max = jnp.max(masked, axis=-1, keepdims=True)
    numerator = jnp.where(allowed[None], jnp.exp(masked - row_max), 0.0)
    row_total = jnp.sum(numerator, axis=-1, keepdims=True)
    weights = (numerator / row_total).astype(jnp.bfloat16)
    result = jnp.einsum("gtk,kd->tgd", weights, value_cand, preferred_element_type=jnp.float32)
    return result.astype(jnp.bfloat16)


def shards(query_states, key_states, value_states, verticals, slashes):
    stretch = key_states.shape[0]
    blocks = stretch // BLK
    rank_ctx = lax.axis_index("ctx")
    key_value = jnp.stack([key_states, value_states])
    vert_row = verticals[0]
    slash_row = slashes[0]
    owners = vert_row // blocks
    local_slot = jnp.clip(vert_row - rank_ctx * blocks, 0, blocks - 1)
    local_blocks = key_value.reshape(2, blocks, BLK, HD)
    picked = local_blocks[:, local_slot].astype(jnp.float32)
    picked = jnp.where((owners == rank_ctx)[None, :, None, None], picked, 0.0)
    columns = lax.psum(picked, "ctx").astype(jnp.bfloat16)
    window = [key_value]
    moving = key_value
    for hop_count in range(REACH):
        moving = from_behind(moving, "ctx", 1)
        window.insert(0, moving)
    pool = jnp.concatenate(window, axis=1).reshape(2, (REACH + 1) * blocks, BLK, HD)
    pool = jnp.concatenate([pool, columns], axis=1)
    pool_size = pool.shape[1]
    group = query_states.shape[1] // HD
    query_view = query_states.reshape(blocks, BLK, group, HD)
    own_start = REACH * blocks
    vert_slots = (REACH + 1) * blocks + jnp.arange(vert_row.shape[0], dtype=jnp.int32)

    def attend_one(local_block):
        block_now = rank_ctx * blocks + local_block
        block_ids, live = candidates(block_now, slash_row, vert_row)
        pool_slot = jnp.concatenate(
            [(own_start + local_block)[None], own_start + local_block - slash_row, vert_slots]
        )
        pool_slot = jnp.clip(pool_slot, 0, pool_size - 1)
        key_cand = pool[0][pool_slot].reshape(-1, HD)
        value_cand = pool[1][pool_slot].reshape(-1, HD)
        return attend_block(query_view[local_block], key_cand, value_cand, live)

    result = lax.map(attend_one, jnp.arange(blocks, dtype=jnp.int32))
    result = result.reshape(stretch, group * HD)
    return lax.all_to_all(result, "kvh", split_axis=0, concat_axis=1, tiled=True)


def solution(mesh):
    return jax.shard_map(
        shards,
        mesh=mesh,
        in_specs=(
            P("ctx", "kvh"),
            P("ctx", "kvh"),
            P("ctx", "kvh"),
            P("kvh", None),
            P("kvh", None),
        ),
        out_specs=P(("ctx", "kvh"), None),
        check_vma=False,
    )
```

profile of v0, /device:TPU:31, one launch (start us, length us, event | category | flops | bytes accessed | tf_op | source)
XLA Modules:
  0.0 646.7 jit_solution(4399918626762281824)
XLA Ops:
  1.2 4.9 collective-permute-start
  6.1 6.1 collective-permute-done
  12.2 7.7 %collective-permute-start.1 = (bf16[2,1024,128]{2,1,0:T(8,128)(2,1)S(1)}, bf16[2,1024,128]{2,1,0:T(8,128)(2,1)}, u32[]{:S(2)}, u32[]{:S(2)}) collective-permute-start(bf16[2,1024,128]{2,1,0:T(8,128)(2,1)S(1)} %collective-permute-done), channel_id=1, source_target_pairs={{0,8},{8,16},{16,24},{24,32},{32,40},{40,48},{48,56},{56,64},{64,7... | collective-permute-start | bytes 1572872 | tf_op jit(solution)/shard_map/ppermute | solution.py:14
  22.4 3.7 collective-permute-done.1
  26.0 7.8 %collective-permute-start.2 = (bf16[2,1024,128]{2,1,0:T(8,128)(2,1)}, bf16[2,1024,128]{2,1,0:T(8,128)(2,1)}, u32[]{:S(2)}, u32[]{:S(2)}) collective-permute-start(bf16[2,1024,128]{2,1,0:T(8,128)(2,1)} %collective-permute-done.1), channel_id=1, source_target_pairs={{0,8},{8,16},{16,24},{24,32},{32,40},{40,48},{48,56},{56,64},{64,7... | collective-permute-start | bytes 1572872 | tf_op jit(solution)/shard_map/ppermute | solution.py:14
  36.7 249.0 %all-reduce.1 = bf16[2,4,128,128]{3,2,0,1:T(8,128)(2,1)S(1)} all-reduce(f32[2,4,128,128]{3,2,0,1:T(8,128)S(1)} %select_bitcast_fusion), channel_id=1, replica_groups=mesh['ctx'=64,'kvh'=8] {'ctx'}, use_global_device_ids=true, to_apply=%region_0.1 | all-reduce | flops 131072 | bytes 786432 | tf_op jit(solution)/shard_map/psum | solution.py:59
  287.9 288.4 %while.13 = (s32[]{:T(128)}, bf16[8,128,8,128]{1,3,2,0:T(8,128)(2,1)}, bf16[2,36,128,128]{3,2,1,0:T(8,128)(2,1)S(1)}, s32[8]{0:T(128)S(1)}, s32[8]{0:T(128)S(1)}...) while((s32[]{:T(128)}, ...), condition=%wide.region_5.6_spmd.clone, body=%wide.region_1.5_spmd.clone.sunk | while | flops 891740800 | bytes 22454108 | solution.py:84
  291.0 12.0 %fusion.82 = pred[128,1664]{0,1:T(8,128)(4,1)} fusion(s32[1664]{0:T(1024)S(1)} %get-tuple-element.291, s32[1664]{0:T(1024)S(1)} %get-tuple-element.292, s32[1664]{0:T(1024)S(1)} %get-tuple-element.293, s32[1664]{0:T(1024)S(1)} %get-tuple-element.294, pred[1664]{0:T(1024)(128)(4,1)S(1)} %get-tuple-element.295, ...), kind=kLoop, calls=%fused_computation.53.clone.1 | loop fusion | flops 7241728 | bytes 242957 | tf_op jit(solution)/shard_map/while/body/eval_jaxpr/and | solution.py:37
  310.8 7.4 %fusion.83 = (f32[8,128]{1,0:T(8,128)}, f32[8,128,1664]{1,2,0:T(8,128)}) fusion(pred[128,1664]{0,1:T(8,128)(4,1)} %fusion.82, bf16[1664,128,1]{1,0,2:T(8,128)(2,1)} %bitcast.219, bf16[1,128,8,128]{3,2,1,0:T(8,128)(2,1)} %constant_dynamic-slice_fusion.2), kind=kOutput, calls=%fused_computation.96.clone.1 | convolution fusion | flops 444728960 | bytes 7720960 | tf_op jit(solution)/shard_map/while/body/eval_jaxpr/sub | solution.py:40
  319.6 4.3 fusion.84
  327.1 12.0 %fusion.82 = pred[128,1664]{0,1:T(8,128)(4,1)} fusion(s32[1664]{0:T(1024)S(1)} %get-tuple-element.291, s32[1664]{0:T(1024)S(1)} %get-tuple-element.292, s32[1664]{0:T(1024)S(1)} %get-tuple-element.293, s32[1664]{0:T(1024)S(1)} %get-tuple-element.294, pred[1664]{0:T(1024)(128)(4,1)S(1)} %get-tuple-element.295, ...), kind=kLoop, calls=%fused_computation.53.clone.1 | loop fusion | flops 7241728 | bytes 242957 | tf_op jit(solution)/shard_map/while/body/eval_jaxpr/and | solution.py:37
  346.9 7.4 %fusion.83 = (f32[8,128]{1,0:T(8,128)}, f32[8,128,1664]{1,2,0:T(8,128)}) fusion(pred[128,1664]{0,1:T(8,128)(4,1)} %fusion.82, bf16[1664,128,1]{1,0,2:T(8,128)(2,1)} %bitcast.219, bf16[1,128,8,128]{3,2,1,0:T(8,128)(2,1)} %constant_dynamic-slice_fusion.2), kind=kOutput, calls=%fused_computation.96.clone.1 | convolution fusion | flops 444728960 | bytes 7720960 | tf_op jit(solution)/shard_map/while/body/eval_jaxpr/sub | solution.py:40
  355.7 4.3 fusion.84
  363.1 12.0 %fusion.82 = pred[128,1664]{0,1:T(8,128)(4,1)} fusion(s32[1664]{0:T(1024)S(1)} %get-tuple-element.291, s32[1664]{0:T(1024)S(1)} %get-tuple-element.292, s32[1664]{0:T(1024)S(1)} %get-tuple-element.293, s32[1664]{0:T(1024)S(1)} %get-tuple-element.294, pred[1664]{0:T(1024)(128)(4,1)S(1)} %get-tuple-element.295, ...), kind=kLoop, calls=%fused_computation.53.clone.1 | loop fusion | flops 7241728 | bytes 242957 | tf_op jit(solution)/shard_map/while/body/eval_jaxpr/and | solution.py:37
  382.9 7.4 %fusion.83 = (f32[8,128]{1,0:T(8,128)}, f32[8,128,1664]{1,2,0:T(8,128)}) fusion(pred[128,1664]{0,1:T(8,128)(4,1)} %fusion.82, bf16[1664,128,1]{1,0,2:T(8,128)(2,1)} %bitcast.219, bf16[1,128,8,128]{3,2,1,0:T(8,128)(2,1)} %constant_dynamic-slice_fusion.2), kind=kOutput, calls=%fused_computation.96.clone.1 | convolution fusion | flops 444728960 | bytes 7720960 | tf_op jit(solution)/shard_map/while/body/eval_jaxpr/sub | solution.py:40
  391.7 4.3 fusion.84
  399.2 12.0 %fusion.82 = pred[128,1664]{0,1:T(8,128)(4,1)} fusion(s32[1664]{0:T(1024)S(1)} %get-tuple-element.291, s32[1664]{0:T(1024)S(1)} %get-tuple-element.292, s32[1664]{0:T(1024)S(1)} %get-tuple-element.293, s32[1664]{0:T(1024)S(1)} %get-tuple-element.294, pred[1664]{0:T(1024)(128)(4,1)S(1)} %get-tuple-element.295, ...), kind=kLoop, calls=%fused_computation.53.clone.1 | loop fusion | flops 7241728 | bytes 242957 | tf_op jit(solution)/shard_map/while/body/eval_jaxpr/and | solution.py:37
  419.0 7.4 %fusion.83 = (f32[8,128]{1,0:T(8,128)}, f32[8,128,1664]{1,2,0:T(8,128)}) fusion(pred[128,1664]{0,1:T(8,128)(4,1)} %fusion.82, bf16[1664,128,1]{1,0,2:T(8,128)(2,1)} %bitcast.219, bf16[1,128,8,128]{3,2,1,0:T(8,128)(2,1)} %constant_dynamic-slice_fusion.2), kind=kOutput, calls=%fused_computation.96.clone.1 | convolution fusion | flops 444728960 | bytes 7720960 | tf_op jit(solution)/shard_map/while/body/eval_jaxpr/sub | solution.py:40
  427.8 4.3 fusion.84
  435.2 12.0 %fusion.82 = pred[128,1664]{0,1:T(8,128)(4,1)} fusion(s32[1664]{0:T(1024)S(1)} %get-tuple-element.291, s32[1664]{0:T(1024)S(1)} %get-tuple-element.292, s32[1664]{0:T(1024)S(1)} %get-tuple-element.293, s32[1664]{0:T(1024)S(1)} %get-tuple-element.294, pred[1664]{0:T(1024)(128)(4,1)S(1)} %get-tuple-element.295, ...), kind=kLoop, calls=%fused_computation.53.clone.1 | loop fusion | flops 7241728 | bytes 242957 | tf_op jit(solution)/shard_map/while/body/eval_jaxpr/and | solution.py:37
  455.0 7.4 %fusion.83 = (f32[8,128]{1,0:T(8,128)}, f32[8,128,1664]{1,2,0:T(8,128)}) fusion(pred[128,1664]{0,1:T(8,128)(4,1)} %fusion.82, bf16[1664,128,1]{1,0,2:T(8,128)(2,1)} %bitcast.219, bf16[1,128,8,128]{3,2,1,0:T(8,128)(2,1)} %constant_dynamic-slice_fusion.2), kind=kOutput, calls=%fused_computation.96.clone.1 | convolution fusion | flops 444728960 | bytes 7720960 | tf_op jit(solution)/shard_map/while/body/eval_jaxpr/sub | solution.py:40
  463.8 4.3 fusion.84
  471.3 12.0 %fusion.82 = pred[128,1664]{0,1:T(8,128)(4,1)} fusion(s32[1664]{0:T(1024)S(1)} %get-tuple-element.291, s32[1664]{0:T(1024)S(1)} %get-tuple-element.292, s32[1664]{0:T(1024)S(1)} %get-tuple-element.293, s32[1664]{0:T(1024)S(1)} %get-tuple-element.294, pred[1664]{0:T(1024)(128)(4,1)S(1)} %get-tuple-element.295, ...), kind=kLoop, calls=%fused_computation.53.clone.1 | loop fusion | flops 7241728 | bytes 242957 | tf_op jit(solution)/shard_map/while/body/eval_jaxpr/and | solution.py:37
  491.1 7.4 %fusion.83 = (f32[8,128]{1,0:T(8,128)}, f32[8,128,1664]{1,2,0:T(8,128)}) fusion(pred[128,1664]{0,1:T(8,128)(4,1)} %fusion.82, bf16[1664,128,1]{1,0,2:T(8,128)(2,1)} %bitcast.219, bf16[1,128,8,128]{3,2,1,0:T(8,128)(2,1)} %constant_dynamic-slice_fusion.2), kind=kOutput, calls=%fused_computation.96.clone.1 | convolution fusion | flops 444728960 | bytes 7720960 | tf_op jit(solution)/shard_map/while/body/eval_jaxpr/sub | solution.py:40
  499.9 4.3 fusion.84
  507.3 12.0 %fusion.82 = pred[128,1664]{0,1:T(8,128)(4,1)} fusion(s32[1664]{0:T(1024)S(1)} %get-tuple-element.291, s32[1664]{0:T(1024)S(1)} %get-tuple-element.292, s32[1664]{0:T(1024)S(1)} %get-tuple-element.293, s32[1664]{0:T(1024)S(1)} %get-tuple-element.294, pred[1664]{0:T(1024)(128)(4,1)S(1)} %get-tuple-element.295, ...), kind=kLoop, calls=%fused_computation.53.clone.1 | loop fusion | flops 7241728 | bytes 242957 | tf_op jit(solution)/shard_map/while/body/eval_jaxpr/and | solution.py:37
  527.1 7.4 %fusion.83 = (f32[8,128]{1,0:T(8,128)}, f32[8,128,1664]{1,2,0:T(8,128)}) fusion(pred[128,1664]{0,1:T(8,128)(4,1)} %fusion.82, bf16[1664,128,1]{1,0,2:T(8,128)(2,1)} %bitcast.219, bf16[1,128,8,128]{3,2,1,0:T(8,128)(2,1)} %constant_dynamic-slice_fusion.2), kind=kOutput, calls=%fused_computation.96.clone.1 | convolution fusion | flops 444728960 | bytes 7720960 | tf_op jit(solution)/shard_map/while/body/eval_jaxpr/sub | solution.py:40
  535.9 4.3 fusion.84
  543.4 12.0 %fusion.82 = pred[128,1664]{0,1:T(8,128)(4,1)} fusion(s32[1664]{0:T(1024)S(1)} %get-tuple-element.291, s32[1664]{0:T(1024)S(1)} %get-tuple-element.292, s32[1664]{0:T(1024)S(1)} %get-tuple-element.293, s32[1664]{0:T(1024)S(1)} %get-tuple-element.294, pred[1664]{0:T(1024)(128)(4,1)S(1)} %get-tuple-element.295, ...), kind=kLoop, calls=%fused_computation.53.clone.1 | loop fusion | flops 7241728 | bytes 242957 | tf_op jit(solution)/shard_map/while/body/eval_jaxpr/and | solution.py:37
  563.2 7.4 %fusion.83 = (f32[8,128]{1,0:T(8,128)}, f32[8,128,1664]{1,2,0:T(8,128)}) fusion(pred[128,1664]{0,1:T(8,128)(4,1)} %fusion.82, bf16[1664,128,1]{1,0,2:T(8,128)(2,1)} %bitcast.219, bf16[1,128,8,128]{3,2,1,0:T(8,128)(2,1)} %constant_dynamic-slice_fusion.2), kind=kOutput, calls=%fused_computation.96.clone.1 | convolution fusion | flops 444728960 | bytes 7720960 | tf_op jit(solution)/shard_map/while/body/eval_jaxpr/sub | solution.py:40
  572.0 4.3 fusion.84
  579.2 61.7 %all_to_all.19 = bf16[8,128,1024]{2,1,0:T(8,128)(2,1)} all-to-all(bf16[8,128,1024]{2,1,0:T(8,128)(2,1)S(1)} %copy.35), channel_id=1, replica_groups=mesh['ctx'=64,'kvh'=8] {'kvh'}, dimensions={0} | all-to-all | bytes 4194304 | tf_op jit(solution)/shard_map/all_to_all | solution.py:86
  (156 shorter events, 88.1 us)
Async XLA Ops:
  0.0 34.6 %copy-start.2 = (bf16[1024,1024]{1,0:T(8,128)(2,1)S(1)}, bf16[1024,1024]{1,0:T(8,128)(2,1)}, u32[]{:S(2)}) copy-start(bf16[1024,1024]{1,0:T(8,128)(2,1)} %param.7) | copy-start | bytes 6291460
  1.2 11.0 %collective-permute-start = (bf16[2,1024,128]{2,1,0:T(8,128)(2,1)S(1)}, bf16[2,1024,128]{2,1,0:T(8,128)(2,1)S(1)}, u32[]{:S(2)}, u32[]{:S(2)}) collective-permute-start(bf16[2,1024,128]{2,1,0:T(8,128)(2,1)S(1)} %pad_maximum_fusion.1), channel_id=1, source_target_pairs={{0,8},{8,16},{16,24},{24,32},{32,40},{40,48},{48,56},{56,64},{64,7... | collective-permute-start | bytes 1572872 | tf_op jit(solution)/shard_map/ppermute | solution.py:14
  12.2 21.6 %copy-start.3 = (bf16[2,1024,128]{2,1,0:T(8,128)(2,1)}, bf16[2,1024,128]{2,1,0:T(8,128)(2,1)S(1)}, u32[]{:S(2)}) copy-start(bf16[2,1024,128]{2,1,0:T(8,128)(2,1)S(1)} %collective-permute-done) | copy-start | bytes 1572868
  12.2 13.8 %collective-permute-start.1 = (bf16[2,1024,128]{2,1,0:T(8,128)(2,1)S(1)}, bf16[2,1024,128]{2,1,0:T(8,128)(2,1)}, u32[]{:S(2)}, u32[]{:S(2)}) collective-permute-start(bf16[2,1024,128]{2,1,0:T(8,128)(2,1)S(1)} %collective-permute-done), channel_id=1, source_target_pairs={{0,8},{8,16},{16,24},{24,32},{32,40},{40,48},{48,56},{56,64},{64,7... | collective-permute-start | bytes 1572872 | tf_op jit(solution)/shard_map/ppermute | solution.py:14
  26.0 259.6 %collective-permute-start.2 = (bf16[2,1024,128]{2,1,0:T(8,128)(2,1)}, bf16[2,1024,128]{2,1,0:T(8,128)(2,1)}, u32[]{:S(2)}, u32[]{:S(2)}) collective-permute-start(bf16[2,1024,128]{2,1,0:T(8,128)(2,1)} %collective-permute-done.1), channel_id=1, source_target_pairs={{0,8},{8,16},{16,24},{24,32},{32,40},{40,48},{48,56},{56,64},{64,7... | collective-permute-start | bytes 1572872 | tf_op jit(solution)/shard_map/ppermute | solution.py:14
  34.6 251.1 %copy-start = (bf16[1024,128]{1,0:T(8,128)(2,1)S(1)}, bf16[1024,128]{1,0:T(8,128)(2,1)}, u32[]{:S(2)}) copy-start(bf16[1024,128]{1,0:T(8,128)(2,1)} %param.9) | copy-start | bytes 786436
  34.6 251.1 %copy-start.1 = (bf16[1024,128]{1,0:T(8,128)(2,1)S(1)}, bf16[1024,128]{1,0:T(8,128)(2,1)}, u32[]{:S(2)}) copy-start(bf16[1024,128]{1,0:T(8,128)(2,1)} %param.8) | copy-start | bytes 786436
  287.2 0.7 copy-start.4
  287.2 0.7 copy-start.5
where the time goes:
time: 649 us; the launch traced here: 647 us
  blocking collectives  311 us (48%)
  other arithmetic  105 us (16%)
  matrix products  93.7 us (14%)
  local copies, waits for them, and re-layouts  79 us (12%)
  loops' own time  27.8 us (4%)
  starting transfers between devices  20.4 us (3%)
  waiting for transfers between devices  9.79 us (2%)
    psum x1, blocking collectives, shards(): columns = lax.psum(picked, 'ctx').astype(jnp.bfloat16)  249 us
    and x8, other arithmetic, attend_block(): allowed = live[cand_index] & ((cand_index > 0) | (within <= query_pos))  96.2 us
    all_to_all x1, blocking collectives, shards(): lax.all_to_all(result, 'kvh', split_axis=0, concat_axis=1, tiled=True)  61.7 us
    sub x8, matrix products, attend_block(): numerator = jnp.where(allowed[None], jnp.exp(masked - row_max), 0.0)  59.1 us
    dot_general x8, matrix products, attend_block(): jnp.einsum('gtk,kd->tgd', weights, value_cand, preferred_element_type=jnp...  34.6 us
    another operation x1, loops' own time, shards(): result = lax.map(attend_one, jnp.arange(blocks, dtype=jnp.int32))  27.8 us
    gather x8, local copies, waits for them, and re-layouts, attend_one(): key_cand = pool[0][pool_slot].reshape(-1, HD)  21.5 us
    ppermute x3, starting transfers between devices, from_behind(): lax.ppermute(value, axis, [(source, source + steps) for source in range(l...  20.4 us
  transfers between devices with their start and end apart: 3, of which 2 were waited for; matrix products, arithmetic and copies ran while one was open for 1% of the time, Pallas kernels for 0%

commit v1 on v0

v1 whole, which is shorter than its diff:
```python
import functools

import jax
import jax.numpy as jnp
from jax import lax
from jax.experimental import pallas as pl
from jax.experimental.pallas import tpu as pltpu
from jax.sharding import PartitionSpec as P

HD = 128
BLK = 128
REACH = 3
FAR = -1e30
EXP2_SCALE = HD ** (-0.5) * 1.4426950408889634
CALLS = ((3,), (-3,), (4, 2), (-2, 1), (-1, 0))


def candidates(block_now, slash_row, vert_row):
    block_ids = jnp.concatenate([block_now[None], block_now - slash_row, vert_row])
    count = block_ids.shape[0]
    order = jnp.arange(count, dtype=jnp.int32)
    same_id = block_ids[:, None] == block_ids[None, :]
    earlier = order[None, :] < order[:, None]
    repeated = jnp.any(same_id & earlier, axis=1)
    live = (block_ids >= 0) & (block_ids <= block_now) & jnp.logical_not(repeated)
    return live


def attend_kernel(offsets, slash_count, vert_count, live_ref, place_ref, pick_ref, query_ref, *refs):
    sources = refs[:4]
    columns_ref = refs[4]
    count = len(offsets)
    outs = refs[6 : 6 + count]
    query_buf, kv_buf, live_buf, sems = refs[6 + count :]
    cand_count = 1 + slash_count + vert_count

    def fetch(at):
        block = pick_ref[offsets[at]]
        row = pl.multiple_of(block * BLK, BLK)
        pltpu.make_async_copy(query_ref.at[pl.ds(row, BLK), :], query_buf.at[at], sems.at[at, 0]).start()
        pltpu.make_async_copy(
            sources[0].at[:, pl.ds(row, BLK), :], kv_buf.at[at, :, pl.ds(0, BLK), :], sems.at[at, 1]
        ).start()
        for k in range(slash_count):
            place = place_ref[block, k]
            which = place // 8
            from_row = pl.multiple_of((place % 8) * BLK, BLK)
            for number in range(4):

                @pl.when(which == number)
                def _(number=number, k=k, from_row=from_row):
                    pltpu.make_async_copy(
                        sources[number].at[:, pl.ds(from_row, BLK), :],
                        kv_buf.at[at, :, pl.ds((1 + k) * BLK, BLK), :],
                        sems.at[at, 1],
                    ).start()

        pltpu.make_async_copy(
            columns_ref, kv_buf.at[at, :, pl.ds((1 + slash_count) * BLK, vert_count * BLK), :], sems.at[at, 1]
        ).start()

    def settle(at):
        block = pick_ref[offsets[at]]
        pltpu.make_async_copy(query_buf.at[at], query_buf.at[at], sems.at[at, 0]).wait()
        pltpu.make_async_copy(kv_buf.at[at], kv_buf.at[at], sems.at[at, 1]).wait()
        live_buf[at, pl.ds(0, BLK), :] = jnp.ones((BLK, HD), jnp.bfloat16)
        first_key = kv_buf[at, 0, pl.ds(0, 1), :]
        for c in range(1, cand_count):
            rows = pl.ds(c * BLK, BLK)
            alive = live_ref[block, c]

            @pl.when(alive != 0)
            def _(rows=rows):
                live_buf[at, rows, :] = jnp.ones((BLK, HD), jnp.bfloat16)

            @pl.when(alive == 0)
            def _(rows=rows):
                kv_buf[at, 0, rows, :] = jnp.broadcast_to(first_key, (BLK, HD))
                kv_buf[at, 1, rows, :] = jnp.zeros((BLK, HD), jnp.bfloat16)
                live_buf[at, rows, :] = jnp.zeros((BLK, HD), jnp.bfloat16)

    def attend(at):
        heads = query_buf.shape[2] // HD
        within = lax.broadcasted_iota(jnp.int32, (BLK, BLK), 0) >= lax.broadcasted_iota(jnp.int32, (BLK, BLK), 1)
        within = jnp.concatenate([within, within], axis=0)
        for h in range(0, heads, 2):
            left = query_buf[at, :, pl.ds(h * HD, HD)]
            right = query_buf[at, :, pl.ds((h + 1) * HD, HD)]
            both = jnp.concatenate([left, right], axis=0)
            scores = lax.dot_general(
                both, kv_buf[at, 0], (((1,), (1,)), ((), ())), preferred_element_type=jnp.float32
            )
            own = jnp.where(within, scores[:, :BLK], FAR)
            scores = jnp.concatenate([own, scores[:, BLK:]], axis=1)
            row_max = jnp.max(scores, axis=1, keepdims=True)
            weights = jnp.exp2((scores - row_max) * EXP2_SCALE).astype(jnp.bfloat16)
            widened = jnp.concatenate([kv_buf[at, 1], live_buf[at]], axis=1)
            total = jnp.dot(weights, widened, preferred_element_type=jnp.float32)
            result = (total[:, :HD] / total[:, HD:]).astype(jnp.bfloat16)
            outs[at][:, pl.ds(h * HD, HD)] = result[:BLK]
            outs[at][:, pl.ds((h + 1) * HD, HD)] = result[BLK:]

    for at in range(count):
        fetch(at)
    for at in range(count):
        settle(at)
        attend(at)


def attend_call(offsets, live, place, pick, query, sources, columns, previous):
    count = len(offsets)
    slash_count = place.shape[1]
    vert_count = columns.shape[1] // BLK
    width = (1 + slash_count + vert_count) * BLK
    columns_of_query = query.shape[1]
    rows = BLK * columns_of_query // HD
    anywhere = pl.BlockSpec(memory_space=pl.ANY)
    scalars = pl.BlockSpec(memory_space=pltpu.SMEM)
    return pl.pallas_call(
        functools.partial(attend_kernel, offsets, slash_count, vert_count),
        out_shape=[jax.ShapeDtypeStruct((BLK, columns_of_query), jnp.bfloat16)] * count,
        in_specs=[scalars] * 3 + [anywhere] * 7,
        out_specs=[pl.BlockSpec(memory_space=pltpu.VMEM)] * count,
        scratch_shapes=[
            pltpu.VMEM((count, BLK, columns_of_query), jnp.bfloat16),
            pltpu.VMEM((count, 2, width, HD), jnp.bfloat16),
            pltpu.VMEM((count, width, HD), jnp.bfloat16),
            pltpu.SemaphoreType.DMA((count, 2)),
        ],
        compiler_params=pltpu.CompilerParams(vmem_limit_bytes=40 * 2**20),
        cost_estimate=pl.CostEstimate(
            flops=count * 4 * rows * width * HD, bytes_accessed=count * 2**20, transcendentals=count * rows * width
        ),
    )(live, place, pick, query, *sources, columns, previous)


def assemble_kernel(count, start_ref, *refs):
    pieces, out_ref, sems = refs[:count], refs[count], refs[count + 1]
    width = pieces[0].shape[1]
    copies = []
    for n in range(count):
        at = pl.multiple_of(start_ref[n] * width, width)
        copies.append(pltpu.make_async_copy(pieces[n], out_ref.at[:, pl.ds(at, width)], sems.at[n]))
        copies[-1].start()
    for copy in copies:
        copy.wait()


def assemble(starts, pieces):
    count = len(pieces)
    rows, width = pieces[0].shape
    anywhere = pl.BlockSpec(memory_space=pl.ANY)
    return pl.pallas_call(
        functools.partial(assemble_kernel, count),
        out_shape=jax.ShapeDtypeStruct((rows, count * width), jnp.bfloat16),
        in_specs=[pl.BlockSpec(memory_space=pltpu.SMEM)] + [anywhere] * count,
        out_specs=anywhere,
        scratch_shapes=[pltpu.SemaphoreType.DMA((count,))],
        cost_estimate=pl.CostEstimate(flops=0, bytes_accessed=4 * rows * count * width, transcendentals=0),
    )(starts, *pieces)


def shards(query_states, key_states, value_states, verticals, slashes):
    stretch = key_states.shape[0]
    blocks = stretch // BLK
    stretches = lax.axis_size("ctx")
    planes = lax.axis_size("kvh")
    rank_ctx = lax.axis_index("ctx")
    rank_kvh = lax.axis_index("kvh")
    vert_row = verticals[0]
    slash_row = slashes[0]

    key_value = jnp.stack([key_states, value_states])
    owners = vert_row // blocks
    local_slot = jnp.clip(vert_row - rank_ctx * blocks, 0, blocks - 1)
    picked = key_value.reshape(2, blocks, BLK, HD)[:, local_slot]
    picked = jnp.where((owners == rank_ctx)[None, :, None, None], picked, jnp.zeros((), jnp.bfloat16))
    columns = lax.psum(picked, "ctx").reshape(2, -1, HD)

    ring = range(stretches)
    two_back = lax.ppermute(key_value, "ctx", [(s, (s + 2) % stretches) for s in ring])
    mixed = lax.ppermute(key_value, "ctx", [(s, (s + (1 if s % 2 == 0 else 3)) % stretches) for s in ring])
    swapped = lax.ppermute(two_back, "ctx", [(s, s ^ 1) for s in ring])
    sources = (key_value, swapped, two_back, mixed)

    local = jnp.arange(blocks, dtype=jnp.int32)
    live = jax.vmap(lambda block: candidates(block, slash_row, vert_row))(rank_ctx * blocks + local)
    live = live.astype(jnp.int32)
    relative = local[:, None] - slash_row[None, :]
    hops = (blocks - 1 - relative) // blocks
    odd = rank_ctx % 2 == 1
    which = jnp.where(odd & (hops > 0), REACH + 1 - hops, hops)
    place = which * blocks + (relative + REACH * blocks) % blocks
    pick = (rank_kvh + local) % planes

    pieces = []
    starts = []
    previous = key_value
    for offsets in CALLS:
        wanted = tuple(offset % planes for offset in offsets)
        results = attend_call(wanted, live, place, pick, query_states, sources, columns, previous)
        previous = results[0]
        for offset, result in zip(wanted, results):
            if offset:
                result = lax.ppermute(result, "kvh", [(s, (s + offset) % planes) for s in range(planes)])
            pieces.append(result)
            starts.append((rank_kvh - offset) % planes)
    return assemble(jnp.stack(starts).astype(jnp.int32), pieces)


def solution(mesh):
    return jax.shard_map(
        shards,
        mesh=mesh,
        in_specs=(
            P("ctx", "kvh"),
            P("ctx", "kvh"),
            P("ctx", "kvh"),
            P("kvh", None),
            P("kvh", None),
        ),
        out_specs=P(("ctx", "kvh"), None),
        check_vma=False,
    )
```

time: 649 us -> 359 us (0.55)
  the two profiles are of different devices: /device:TPU:31 before, /device:TPU:1 now
where the time goes in v1:
time: 359 us; the launch traced here: 357 us
  waiting for transfers between devices  194 us (54%)
  Pallas kernels  98 us (27%)
  starting transfers between devices  40.5 us (11%)
  between operations  13.8 us (4%)
  local copies, waits for them, and re-layouts  6.32 us (2%)
  other arithmetic  5.17 us (1%)
    psum x1, waiting for transfers between devices, shards(): columns = lax.psum(picked, 'ctx').reshape(2, -1, HD)  170 us
    pallas_call x1, Pallas kernels, assemble(): pl.pallas_call(functools.partial(assemble_kernel, count), out_shape=jax.S...  65.4 us
    pallas_call x5, Pallas kernels, attend_call(): pl.pallas_call(functools.partial(attend_kernel, offsets, slash_count, ver...  32.6 us
    ppermute x7, starting transfers between devices, shards(): lax.ppermute(result, 'kvh', [(s, (s + offset) % planes) for s in range(pl...  28.5 us
    ppermute x1, waiting for transfers between devices, shards(): lax.ppermute(key_value, 'ctx', [(s, (s + 2) % stretches) for s in ring])  16.2 us
    ppermute x7, waiting for transfers between devices, shards(): lax.ppermute(result, 'kvh', [(s, (s + offset) % planes) for s in range(pl...  7.66 us
  transfers between devices with their start and end apart: 11, of which 4 were waited for; matrix products, arithmetic and copies ran while one was open for 2% of the time, Pallas kernels for 8%

profile of v1, /device:TPU:1, one launch (start us, length us, event | category | flops | bytes accessed | tf_op | source)
XLA Modules:
  0.0 357.4 jit_solution(16839975698526951638)
XLA Ops:
  6.5 1.2 pad_maximum_fusion.refs_0_.refs_5_
  7.8 6.0 %collective-permute-start.2 = (bf16[2,1024,128]{2,1,0:T(8,128)(2,1)S(1)}, bf16[2,1024,128]{2,1,0:T(8,128)(2,1)S(1)}, u32[]{:S(2)}, u32[]{:S(2)}) collective-permute-start(bf16[2,1024,128]{2,1,0:T(8,128)(2,1)S(1)} %pad_maximum_fusion.refs_0_.refs_5_), channel_id=1, source_target_pairs={{0,8},{8,32},{16,24},{24,48},{32,40},{40,64},{48,56},{56,80},{64,7... | collective-permute-start | bytes 1572872 | tf_op jit(solution)/shard_map/ppermute | solution.py:182
  13.8 2.2 collective-permute-start
  16.1 0.7 fusion.9
  16.7 0.7 fusion.8
  17.4 1.9 pad_maximum_fusion.1
  19.3 1.6 gather_fusion
  21.0 0.7 copy.9
  22.1 16.2 %collective-permute-done.refs_2_ = bf16[2,1024,128]{2,1,0:T(8,128)(2,1)} collective-permute-done((bf16[2,1024,128]{2,1,0:T(8,128)(2,1)S(1)}, bf16[2,1024,128]{2,1,0:T(8,128)(2,1)}, u32[]{:S(2)}, u32[]{:S(2)}) %collective-permute-start) | collective-permute-done | bytes 524320 | tf_op jit(solution)/shard_map/ppermute | solution.py:181
  38.4 3.7 %collective-permute-start.1 = (bf16[2,1024,128]{2,1,0:T(8,128)(2,1)}, bf16[2,1024,128]{2,1,0:T(8,128)(2,1)}, u32[]{:S(2)}, u32[]{:S(2)}) collective-permute-start(bf16[2,1024,128]{2,1,0:T(8,128)(2,1)} %collective-permute-done.refs_2_), channel_id=1, source_target_pairs={{0,8},{8,0},{16,24},{24,16},{32,40},{40,32},{48,56},{56,48},{64,72... | collective-permute-start | bytes 1572872 | tf_op jit(solution)/shard_map/ppermute | solution.py:183
  42.1 0.4 and_reduce_fusion
  42.7 169.7 %all-reduce.2.cloned.1.call-done.refs_4_ = bf16[2,512,128]{2,1,0:T(8,128)(2,1)} async-done(((bf16[2,512,128]{2,1,0:T(8,128)(2,1)}), bf16[2,512,128]{2,1,0:T(8,128)(2,1)}) %all-reduce.2.cloned.1.call-update) | async-done | bytes 262160 | tf_op jit(solution)/shard_map/psum | solution.py:178
  212.4 0.9 copy-done.1
  213.4 4.6 %shard_map.55.refs_5_ = bf16[128,1024]{1,0:T(8,128)(2,1)S(1)} custom-call(s32[8,13]{1,0:T(8,128)S(1)} %and_convert_fusion.live_ref, s32[8,8]{1,0:T(8,128)S(1)} %get-tuple-element.17.place_ref, s32[8]{0:T(128)S(1)} %and_select_fusion.1.pick_ref, bf16[1024,1024]{1,0:T(8,128)(2,1)S(1)} %copy-done, bf16[2,1024,128]{2,1,0:T(8,128)(2,1)S(1)} %pad_maximum_fusion.refs_0_.refs_5_, ...), custom_call_target="tpu_custom_call" | custom-call | flops 872415232 | bytes 1048576 | tf_op jit(solution)/shard_map/pallas_call | solution.py:119
  218.0 5.4 %collective-permute-start.3 = (bf16[128,1024]{1,0:T(8,128)(2,1)S(1)}, bf16[128,1024]{1,0:T(8,128)(2,1)S(1)}, u32[]{:S(2)}, u32[]{:S(2)}) collective-permute-start(bf16[128,1024]{1,0:T(8,128)(2,1)S(1)} %shard_map.55.refs_5_), channel_id=1, source_target_pairs={{0,3},{1,4},{2,5},{3,6},{4,7},{5,0},{6,1},{7,2},{8,11},{9,12},{10,... | collective-permute-start | bytes 786440 | tf_op jit(solution)/shard_map/ppermute | solution.py:205
  223.4 4.6 %shard_map.56.refs_5_ = bf16[128,1024]{1,0:T(8,128)(2,1)S(1)} custom-call(s32[8,13]{1,0:T(8,128)S(1)} %and_convert_fusion.live_ref, s32[8,8]{1,0:T(8,128)S(1)} %get-tuple-element.17.place_ref, s32[8]{0:T(128)S(1)} %and_select_fusion.1.pick_ref, bf16[1024,1024]{1,0:T(8,128)(2,1)S(1)} %copy-done, bf16[2,1024,128]{2,1,0:T(8,128)(2,1)S(1)} %pad_maximum_fusion.refs_0_.refs_5_, ...), custom_call_target="tpu_custom_call" | custom-call | flops 872415232 | bytes 1048576 | tf_op jit(solution)/shard_map/pallas_call | solution.py:119
  227.9 3.3 collective-permute-start.4
  231.3 8.1 %shard_map.57 = (bf16[128,1024]{1,0:T(8,128)(2,1)S(1)}, bf16[128,1024]{1,0:T(8,128)(2,1)}) custom-call(s32[8,13]{1,0:T(8,128)S(1)} %and_convert_fusion.live_ref, s32[8,8]{1,0:T(8,128)S(1)} %get-tuple-element.17.place_ref, s32[8]{0:T(128)S(1)} %and_select_fusion.1.pick_ref, bf16[1024,1024]{1,0:T(8,128)(2,1)S(1)} %copy-done, ...), custom_call_target="tpu_custom_call" | custom-call | flops 1744830464 | bytes 2097152 | tf_op jit(solution)/shard_map/pallas_call | solution.py:119
  239.4 3.8 %collective-permute-start.6 = (bf16[128,1024]{1,0:T(8,128)(2,1)}, bf16[128,1024]{1,0:T(8,128)(2,1)}, u32[]{:S(2)}, u32[]{:S(2)}) collective-permute-start(bf16[128,1024]{1,0:T(8,128)(2,1)} %get-tuple-element.12), channel_id=1, source_target_pairs={{0,2},{1,3},{2,4},{3,5},{4,6},{5,7},{6,0},{7,1},{8,10},{9,11},{10,... | collective-permute-start | bytes 786440 | tf_op jit(solution)/shard_map/ppermute | solution.py:205
  243.2 5.9 %collective-permute-start.5 = (bf16[128,1024]{1,0:T(8,128)(2,1)S(1)}, bf16[128,1024]{1,0:T(8,128)(2,1)}, u32[]{:S(2)}, u32[]{:S(2)}) collective-permute-start(bf16[128,1024]{1,0:T(8,128)(2,1)S(1)} %get-tuple-element.11.refs_5_), channel_id=1, source_target_pairs={{0,4},{1,5},{2,6},{3,7},{4,0},{5,1},{6,2},{7,3},{8,12},{9,13},{10,... | collective-permute-start | bytes 786440 | tf_op jit(solution)/shard_map/ppermute | solution.py:205
  249.0 7.9 %shard_map.58 = (bf16[128,1024]{1,0:T(8,128)(2,1)}, bf16[128,1024]{1,0:T(8,128)(2,1)}) custom-call(s32[8,13]{1,0:T(8,128)S(1)} %and_convert_fusion.live_ref, s32[8,8]{1,0:T(8,128)S(1)} %get-tuple-element.17.place_ref, s32[8]{0:T(128)S(1)} %and_select_fusion.1.pick_ref, bf16[1024,1024]{1,0:T(8,128)(2,1)S(1)} %copy-done, ...), custom_call_target="tpu_custom_call" | custom-call | flops 1744830464 | bytes 2097152 | tf_op jit(solution)/shard_map/pallas_call | solution.py:119
  257.0 7.4 %shard_map.59 = (bf16[128,1024]{1,0:T(8,128)(2,1)}, bf16[128,1024]{1,0:T(8,128)(2,1)S(1)}) custom-call(s32[8,13]{1,0:T(8,128)S(1)} %and_convert_fusion.live_ref, s32[8,8]{1,0:T(8,128)S(1)} %get-tuple-element.17.place_ref, s32[8]{0:T(128)S(1)} %and_select_fusion.1.pick_ref, bf16[1024,1024]{1,0:T(8,128)(2,1)S(1)} %copy-done, ...), custom_call_target="tpu_custom_call" | custom-call | flops 1744830464 | bytes 2097152 | tf_op jit(solution)/shard_map/pallas_call | solution.py:119
  264.4 0.7 copy-done.2
  265.1 4.1 %collective-permute-start.9 = (bf16[128,1024]{1,0:T(8,128)(2,1)}, bf16[128,1024]{1,0:T(8,128)(2,1)S(1)}, u32[]{:S(2)}, u32[]{:S(2)}) collective-permute-start(bf16[128,1024]{1,0:T(8,128)(2,1)} %get-tuple-element.15), channel_id=1, source_target_pairs={{0,7},{1,0},{2,1},{3,2},{4,3},{5,4},{6,5},{7,6},{8,15},{9,8},{10,9... | collective-permute-start | bytes 786440 | tf_op jit(solution)/shard_map/ppermute | solution.py:205
  269.2 1.9 collective-permute-start.8
  271.2 0.7 copy-done.3
  271.8 4.1 %collective-permute-start.7 = (bf16[128,1024]{1,0:T(8,128)(2,1)}, bf16[128,1024]{1,0:T(8,128)(2,1)S(1)}, u32[]{:S(2)}, u32[]{:S(2)}) collective-permute-start(bf16[128,1024]{1,0:T(8,128)(2,1)} %get-tuple-element.13.refs_5_), channel_id=1, source_target_pairs={{0,6},{1,7},{2,0},{3,1},{4,2},{5,3},{6,4},{7,5},{8,14},{9,15},{10,... | collective-permute-start | bytes 786440 | tf_op jit(solution)/shard_map/ppermute | solution.py:205
  276.1 0.7 stack.50.start_ref
  276.8 2.9 collective-permute-done.8.refs_5_
  279.7 4.7 %collective-permute-done.7.refs_4_ = bf16[128,1024]{1,0:T(8,128)(2,1)S(1)} collective-permute-done((bf16[128,1024]{1,0:T(8,128)(2,1)}, bf16[128,1024]{1,0:T(8,128)(2,1)S(1)}, u32[]{:S(2)}, u32[]{:S(2)}) %collective-permute-start.7) | collective-permute-done | bytes 262176 | tf_op jit(solution)/shard_map/ppermute | solution.py:205
  284.5 0.7 copy-done.7
  285.1 65.4 %shard_map.60 = bf16[128,8192]{1,0:T(8,128)(2,1)} custom-call(s32[8]{0:T(128)} %stack.50.start_ref, bf16[128,1024]{1,0:T(8,128)(2,1)} %copy-done.3, bf16[128,1024]{1,0:T(8,128)(2,1)} %copy-done.4, bf16[128,1024]{1,0:T(8,128)(2,1)} %collective-permute-done.5.refs_2_, bf16[128,1024]{1,0:T(8,128)(2,1)} %collective-permute-done.6.refs_3_, ...), custom_call_target="tpu_custom_call" | custom-call | bytes 4194304 | tf_op jit(solution)/shard_map/pallas_call | solution.py:153
  (37 shorter events, 0.7 us)
Async XLA Ops:
  6.5 15.3 %copy-start.9 = (s32[1,4]{1,0:T(1,128)S(1)}, s32[1,4]{1,0:T(1,128)}, u32[]{:S(2)}) copy-start(s32[1,4]{1,0:T(1,128)} %param.8) | copy-start | bytes 52
  6.5 15.3 %copy-start.8 = (s32[1,8]{1,0:T(1,128)S(1)}, s32[1,8]{1,0:T(1,128)}, u32[]{:S(2)}) copy-start(s32[1,8]{1,0:T(1,128)} %param.9) | copy-start | bytes 100
  6.5 205.9 %copy-start = (bf16[1024,1024]{1,0:T(8,128)(2,1)S(1)}, bf16[1024,1024]{1,0:T(8,128)(2,1)}, u32[]{:S(2)}) copy-start(bf16[1024,1024]{1,0:T(8,128)(2,1)} %query_ref.9) | copy-start | bytes 6291460
  6.5 205.8 %all-reduce.2.cloned.1.call-start = ((), (), s32[]{:S(2)}) async-start(), calls=%async_computation | async-start | bytes 524288 | tf_op jit(solution)/shard_map/psum | solution.py:178
  7.8 204.6 %collective-permute-start.2 = (bf16[2,1024,128]{2,1,0:T(8,128)(2,1)S(1)}, bf16[2,1024,128]{2,1,0:T(8,128)(2,1)S(1)}, u32[]{:S(2)}, u32[]{:S(2)}) collective-permute-start(bf16[2,1024,128]{2,1,0:T(8,128)(2,1)S(1)} %pad_maximum_fusion.refs_0_.refs_5_), channel_id=1, source_target_pairs={{0,8},{8,32},{16,24},{24,48},{32,40},{40,64},{48,56},{56,80},{64,7... | collective-permute-start | bytes 1572872 | tf_op jit(solution)/shard_map/ppermute | solution.py:182
  13.8 24.5 %collective-permute-start = (bf16[2,1024,128]{2,1,0:T(8,128)(2,1)S(1)}, bf16[2,1024,128]{2,1,0:T(8,128)(2,1)}, u32[]{:S(2)}, u32[]{:S(2)}) collective-permute-start(bf16[2,1024,128]{2,1,0:T(8,128)(2,1)S(1)} %pad_maximum_fusion.refs_0_.refs_5_), channel_id=1, source_target_pairs={{0,16},{8,24},{16,32},{24,40},{32,48},{40,56},{48,64},{56,72},{64,... | collective-permute-start | bytes 1572872 | tf_op jit(solution)/shard_map/ppermute | solution.py:181
  38.4 174.0 %collective-permute-start.1 = (bf16[2,1024,128]{2,1,0:T(8,128)(2,1)}, bf16[2,1024,128]{2,1,0:T(8,128)(2,1)}, u32[]{:S(2)}, u32[]{:S(2)}) collective-permute-start(bf16[2,1024,128]{2,1,0:T(8,128)(2,1)} %collective-permute-done.refs_2_), channel_id=1, source_target_pairs={{0,8},{8,0},{16,24},{24,16},{32,40},{40,32},{48,56},{56,48},{64,72... | collective-permute-start | bytes 1572872 | tf_op jit(solution)/shard_map/ppermute | solution.py:183
  212.4 1.0 copy-start.1
  218.0 53.2 %collective-permute-start.3 = (bf16[128,1024]{1,0:T(8,128)(2,1)S(1)}, bf16[128,1024]{1,0:T(8,128)(2,1)S(1)}, u32[]{:S(2)}, u32[]{:S(2)}) collective-permute-start(bf16[128,1024]{1,0:T(8,128)(2,1)S(1)} %shard_map.55.refs_5_), channel_id=1, source_target_pairs={{0,3},{1,4},{2,5},{3,6},{4,7},{5,0},{6,1},{7,2},{8,11},{9,12},{10,... | collective-permute-start | bytes 786440 | tf_op jit(solution)/shard_map/ppermute | solution.py:205
  227.9 41.2 %collective-permute-start.4 = (bf16[128,1024]{1,0:T(8,128)(2,1)S(1)}, bf16[128,1024]{1,0:T(8,128)(2,1)S(1)}, u32[]{:S(2)}, u32[]{:S(2)}) collective-permute-start(bf16[128,1024]{1,0:T(8,128)(2,1)S(1)} %shard_map.56.refs_5_), channel_id=1, source_target_pairs={{0,5},{1,6},{2,7},{3,0},{4,1},{5,2},{6,3},{7,4},{8,13},{9,14},{10,... | collective-permute-start | bytes 786440 | tf_op jit(solution)/shard_map/ppermute | solution.py:205
  239.4 37.4 %collective-permute-start.6 = (bf16[128,1024]{1,0:T(8,128)(2,1)}, bf16[128,1024]{1,0:T(8,128)(2,1)}, u32[]{:S(2)}, u32[]{:S(2)}) collective-permute-start(bf16[128,1024]{1,0:T(8,128)(2,1)} %get-tuple-element.12), channel_id=1, source_target_pairs={{0,2},{1,3},{2,4},{3,5},{4,6},{5,7},{6,0},{7,1},{8,10},{9,11},{10,... | collective-permute-start | bytes 786440 | tf_op jit(solution)/shard_map/ppermute | solution.py:205
  243.2 33.6 %collective-permute-start.5 = (bf16[128,1024]{1,0:T(8,128)(2,1)S(1)}, bf16[128,1024]{1,0:T(8,128)(2,1)}, u32[]{:S(2)}, u32[]{:S(2)}) collective-permute-start(bf16[128,1024]{1,0:T(8,128)(2,1)S(1)} %get-tuple-element.11.refs_5_), channel_id=1, source_target_pairs={{0,4},{1,5},{2,6},{3,7},{4,0},{5,1},{6,2},{7,3},{8,12},{9,13},{10,... | collective-permute-start | bytes 786440 | tf_op jit(solution)/shard_map/ppermute | solution.py:205
  264.4 0.7 copy-start.2
  265.1 11.7 %collective-permute-start.9 = (bf16[128,1024]{1,0:T(8,128)(2,1)}, bf16[128,1024]{1,0:T(8,128)(2,1)S(1)}, u32[]{:S(2)}, u32[]{:S(2)}) collective-permute-start(bf16[128,1024]{1,0:T(8,128)(2,1)} %get-tuple-element.15), channel_id=1, source_target_pairs={{0,7},{1,0},{2,1},{3,2},{4,3},{5,4},{6,5},{7,6},{8,15},{9,8},{10,9... | collective-permute-start | bytes 786440 | tf_op jit(solution)/shard_map/ppermute | solution.py:205
  269.2 2.0 copy-start.4
  269.2 10.5 %collective-permute-start.8 = (bf16[128,1024]{1,0:T(8,128)(2,1)}, bf16[128,1024]{1,0:T(8,128)(2,1)S(1)}, u32[]{:S(2)}, u32[]{:S(2)}) collective-permute-start(bf16[128,1024]{1,0:T(8,128)(2,1)} %get-tuple-element.14), channel_id=1, source_target_pairs={{0,1},{1,2},{2,3},{3,4},{4,5},{5,6},{6,7},{7,0},{8,9},{9,10},{10,1... | collective-permute-start | bytes 786440 | tf_op jit(solution)/shard_map/ppermute | solution.py:205
  271.2 0.7 copy-start.3
  271.8 12.6 %collective-permute-start.7 = (bf16[128,1024]{1,0:T(8,128)(2,1)}, bf16[128,1024]{1,0:T(8,128)(2,1)S(1)}, u32[]{:S(2)}, u32[]{:S(2)}) collective-permute-start(bf16[128,1024]{1,0:T(8,128)(2,1)} %get-tuple-element.13.refs_5_), channel_id=1, source_target_pairs={{0,6},{1,7},{2,0},{3,1},{4,2},{5,3},{6,4},{7,5},{8,14},{9,15},{10,... | collective-permute-start | bytes 786440 | tf_op jit(solution)/shard_map/ppermute | solution.py:205
  276.8 7.7 %copy-start.5 = (bf16[128,1024]{1,0:T(8,128)(2,1)}, bf16[128,1024]{1,0:T(8,128)(2,1)S(1)}, u32[]{:S(2)}) copy-start(bf16[128,1024]{1,0:T(8,128)(2,1)S(1)} %collective-permute-done.9.refs_6_) | copy-start | bytes 786436
  279.7 4.7 %copy-start.6 = (bf16[128,1024]{1,0:T(8,128)(2,1)}, bf16[128,1024]{1,0:T(8,128)(2,1)S(1)}, u32[]{:S(2)}) copy-start(bf16[128,1024]{1,0:T(8,128)(2,1)S(1)} %collective-permute-done.8.refs_5_) | copy-start | bytes 786436
  284.4 0.7 copy-start.7
Sparse Core Ops, SparseCore 0:
  21.9 190.4 all-reduce.1

commit v2 on v1

v2 whole, which is shorter than its diff:
```python
import functools

import jax
import jax.numpy as jnp
from jax import lax
from jax.experimental import pallas as pl
from jax.experimental.pallas import tpu as pltpu
from jax.sharding import PartitionSpec as P

HD = 128
BLK = 128
REACH = 3
FAR = -1e30
EXP2_SCALE = HD ** (-0.5) * 1.4426950408889634
VMEM_BYTES = 62 * 2**20
KEY_TILE = 256
ROW_TILE = 16
CALLS = ((3,), (-3,), (2, 4), (1, -2), (-1, 0))

ANYWHERE = pl.BlockSpec(memory_space=pl.ANY)
SCALARS = pl.BlockSpec(memory_space=pltpu.SMEM)
IN_VMEM = pl.BlockSpec(memory_space=pltpu.VMEM)
LIMITS = pltpu.CompilerParams(vmem_limit_bytes=VMEM_BYTES)


def small_cost(bytes_accessed):
    return pl.CostEstimate(flops=0, bytes_accessed=bytes_accessed, transcendentals=0)


def prepare_kernel(where_ref, verticals_ref, keys_ref, values_ref, stacked_ref, picked_ref, sems):
    copies = [
        pltpu.make_async_copy(keys_ref, stacked_ref.at[0], sems.at[0]),
        pltpu.make_async_copy(values_ref, stacked_ref.at[1], sems.at[1]),
    ]
    for copy in copies:
        copy.start()
    for copy in copies:
        copy.wait()
    blocks = keys_ref.shape[0] // BLK
    for v in range(verticals_ref.shape[1]):
        block = verticals_ref[0, v]
        mine = block // blocks == where_ref[0]
        row = pl.multiple_of((block % blocks) * BLK, BLK)
        rows = pl.ds(v * BLK, BLK)

        @pl.when(mine)
        def _(row=row, rows=rows):
            picked_ref[:, rows, :] = stacked_ref[:, pl.ds(row, BLK), :]

        @pl.when(jnp.logical_not(mine))
        def _(rows=rows):
            picked_ref[:, rows, :] = jnp.zeros((2, BLK, HD), jnp.bfloat16)


def prepare(where, verticals, keys, values):
    stretch = keys.shape[0]
    return pl.pallas_call(
        prepare_kernel,
        out_shape=[
            jax.ShapeDtypeStruct((2, stretch, HD), jnp.bfloat16),
            jax.ShapeDtypeStruct((2, verticals.shape[1] * BLK, HD), jnp.bfloat16),
        ],
        in_specs=[SCALARS, SCALARS, ANYWHERE, ANYWHERE],
        out_specs=[IN_VMEM, IN_VMEM],
        scratch_shapes=[pltpu.SemaphoreType.DMA((2,))],
        compiler_params=LIMITS,
        cost_estimate=small_cost(2**20),
    )(where, verticals, keys, values)


def attend_kernel(offsets, blocks, where_ref, verticals_ref, slashes_ref, query_ref, *refs):
    sources = refs[:4]
    columns_ref = refs[4]
    count = len(offsets)
    outs, scratch = refs[-8 - count : -8], refs[-8:]
    query_buf, kv_buf, live_buf, scores_even, scores_odd, weights_even, weights_odd, sems = scratch
    slash_count = slashes_ref.shape[1]
    vert_count = verticals_ref.shape[1]
    cand_count = 1 + slash_count + vert_count
    width = cand_count * BLK
    heads = query_buf.shape[2] // HD
    score_bufs = (scores_even, scores_odd)
    weight_bufs = (weights_even, weights_odd)
    rank_ctx = where_ref[0]
    odd = rank_ctx % 2

    def local_block(at):
        return (where_ref[1] + offsets[at]) % blocks

    def fetch(at):
        block = local_block(at)
        row = pl.multiple_of(block * BLK, BLK)
        pltpu.make_async_copy(query_ref.at[pl.ds(row, BLK), :], query_buf.at[at], sems.at[at, 0]).start()
        pltpu.make_async_copy(
            sources[0].at[:, pl.ds(row, BLK), :], kv_buf.at[at, :, pl.ds(0, BLK), :], sems.at[at, 1]
        ).start()
        for k in range(slash_count):
            relative = block - slashes_ref[0, k] + REACH * blocks
            hops = REACH - relative // blocks
            which = jnp.where((odd == 1) & (hops > 0), REACH + 1 - hops, hops)
            from_row = pl.multiple_of((relative % blocks) * BLK, BLK)
            for number in range(4):

                @pl.when(which == number)
                def _(number=number, k=k, from_row=from_row):
                    pltpu.make_async_copy(
                        sources[number].at[:, pl.ds(from_row, BLK), :],
                        kv_buf.at[at, :, pl.ds((1 + k) * BLK, BLK), :],
                        sems.at[at, 1],
                    ).start()

        pltpu.make_async_copy(
            columns_ref, kv_buf.at[at, :, pl.ds((1 + slash_count) * BLK, vert_count * BLK), :], sems.at[at, 1]
        ).start()

    def settle(at):
        block_now = rank_ctx * blocks + local_block(at)
        ids = [block_now]
        ids += [block_now - slashes_ref[0, k] for k in range(slash_count)]
        ids += [verticals_ref[0, k] for k in range(vert_count)]
        pltpu.make_async_copy(query_buf.at[at], query_buf.at[at], sems.at[at, 0]).wait()
        pltpu.make_async_copy(kv_buf.at[at], kv_buf.at[at], sems.at[at, 1]).wait()
        live_buf[at, pl.ds(0, BLK), :] = jnp.ones((BLK, HD), jnp.bfloat16)
        for c in range(1, cand_count):
            alive = (ids[c] >= 0) & (ids[c] <= block_now)
            for earlier in range(c):
                alive = alive & (ids[c] != ids[earlier])
            rows = pl.ds(c * BLK, BLK)
            live_buf[at, rows, :] = jnp.broadcast_to(jnp.where(alive, 1.0, 0.0), (BLK, HD)).astype(jnp.bfloat16)

            @pl.when(jnp.logical_not(alive))
            def _(rows=rows):
                first_key = kv_buf[at, 0, pl.ds(0, 1), :]
                kv_buf[at, 0, rows, :] = jnp.broadcast_to(first_key, (BLK, HD))
                kv_buf[at, 1, rows, :] = jnp.zeros((BLK, HD), jnp.bfloat16)

    def score_steps(at, pair):
        def step(start):
            size = min(KEY_TILE, width - start)
            left = query_buf[at, :, pl.ds(2 * pair * HD, HD)]
            right = query_buf[at, :, pl.ds((2 * pair + 1) * HD, HD)]
            score_bufs[pair % 2][:, pl.ds(start, size)] = lax.dot_general(
                jnp.concatenate([left, right], axis=0),
                kv_buf[at, 0, pl.ds(start, size), :],
                (((1,), (1,)), ((), ())),
                preferred_element_type=jnp.float32,
            )

        return [functools.partial(step, start) for start in range(0, width, KEY_TILE)]

    def weight_steps(pair):
        def step(start):
            rows = pl.ds(start, ROW_TILE)
            scores = score_bufs[pair % 2][rows, :]
            position = lax.broadcasted_iota(jnp.int32, (ROW_TILE, BLK), 0) + start % BLK
            within = position >= lax.broadcasted_iota(jnp.int32, (ROW_TILE, BLK), 1)
            own = jnp.where(within, scores[:, :BLK], FAR)
            scores = jnp.concatenate([own, scores[:, BLK:]], axis=1)
            row_max = jnp.max(scores, axis=1, keepdims=True)
            weights = jnp.exp2((scores - row_max) * EXP2_SCALE)
            weight_bufs[pair % 2][rows, :] = weights.astype(jnp.bfloat16)

        return [functools.partial(step, start) for start in range(0, 2 * BLK, ROW_TILE)]

    def value_step(at, pair):
        widened = jnp.concatenate([kv_buf[at, 1], live_buf[at]], axis=1)
        total = jnp.dot(weight_bufs[pair % 2][...], widened, preferred_element_type=jnp.float32)
        result = (total[:, :HD] / total[:, HD:]).astype(jnp.bfloat16)
        outs[at][:, pl.ds(2 * pair * HD, HD)] = result[:BLK]
        outs[at][:, pl.ds((2 * pair + 1) * HD, HD)] = result[BLK:]

    def attend(at):
        pairs = heads // 2
        for step in score_steps(at, 0):
            step()
        for pair in range(pairs):
            products = [functools.partial(value_step, at, pair - 1)] if pair else []
            products += score_steps(at, pair + 1) if pair + 1 < pairs else []
            weights = weight_steps(pair)
            every = max(1, len(weights) // max(1, len(products)))
            for n, step in enumerate(weights):
                if n % every == 0 and products:
                    products.pop(0)()
                step()
            for step in products:
                step()
        value_step(at, pairs - 1)

    for at in range(count):
        fetch(at)
    for at in range(count):
        settle(at)
        attend(at)


def attend_call(offsets, blocks, where, verticals, slashes, query, sources, columns, after):
    count = len(offsets)
    width = (1 + slashes.shape[1] + verticals.shape[1]) * BLK
    query_width = query.shape[1]
    return pl.pallas_call(
        functools.partial(attend_kernel, offsets, blocks),
        out_shape=[jax.ShapeDtypeStruct((BLK, query_width), jnp.bfloat16)] * count,
        in_specs=[SCALARS] * 3 + [ANYWHERE] * (6 + len(after)),
        out_specs=[IN_VMEM] * count,
        scratch_shapes=[
            pltpu.VMEM((count, BLK, query_width), jnp.bfloat16),
            pltpu.VMEM((count, 2, width, HD), jnp.bfloat16),
            pltpu.VMEM((count, width, HD), jnp.bfloat16),
            pltpu.VMEM((2 * BLK, width), jnp.float32),
            pltpu.VMEM((2 * BLK, width), jnp.float32),
            pltpu.VMEM((2 * BLK, width), jnp.bfloat16),
            pltpu.VMEM((2 * BLK, width), jnp.bfloat16),
            pltpu.SemaphoreType.DMA((count, 2)),
        ],
        compiler_params=LIMITS,
        cost_estimate=pl.CostEstimate(
            flops=4 * count * BLK * query_width * width,
            bytes_accessed=count * 2**20,
            transcendentals=count * BLK * query_width // HD * width,
        ),
    )(where, verticals, slashes, query, *sources, columns, *after)


def assemble_kernel(offsets, where_ref, *refs):
    count = len(offsets)
    pieces, out_ref, sems = refs[:count], refs[count], refs[count + 1]
    width = pieces[0].shape[1]
    copies = []
    for n, offset in enumerate(offsets):
        source = (where_ref[1] + count - offset) % count
        at = pl.multiple_of(source * width, width)
        copies.append(pltpu.make_async_copy(pieces[n], out_ref.at[:, pl.ds(at, width)], sems.at[n]))
        copies[-1].start()
    for copy in copies:
        copy.wait()


def assemble(offsets, where, pieces):
    count = len(pieces)
    rows, width = pieces[0].shape
    return pl.pallas_call(
        functools.partial(assemble_kernel, offsets),
        out_shape=jax.ShapeDtypeStruct((rows, count * width), jnp.bfloat16),
        in_specs=[SCALARS] + [ANYWHERE] * count,
        out_specs=IN_VMEM,
        scratch_shapes=[pltpu.SemaphoreType.DMA((count,))],
        compiler_params=LIMITS,
        cost_estimate=small_cost(4 * rows * count * width),
    )(where, *pieces)


def window_routes(stretches):
    chips = stretches // 2
    first, mixed, last = [], [], []
    for chip in range(chips):
        y, x = divmod(chip, 4)
        for core in range(2):
            first.append((2 * chip + core, (2 * chip + core + 2) % stretches))
        mixed.append((2 * chip, 2 * chip + 1))
        half_y = y + 1 if x == 2 else y
        half = (half_y * 4 + (x - 1) % 4) % chips
        target = (chip + 2) % chips
        mixed.append((2 * chip + 1, 2 * half))
        last.append((2 * half, 2 * target))
    return first, mixed, last


def shards(query_states, key_states, value_states, verticals, slashes):
    stretch = key_states.shape[0]
    blocks = stretch // BLK
    stretches = lax.axis_size("ctx")
    planes = lax.axis_size("kvh")
    where = jnp.stack([lax.axis_index("ctx"), lax.axis_index("kvh")]).astype(jnp.int32)
    key_value, picked = prepare(where, verticals, key_states, value_states)

    first, mixed, last = window_routes(stretches)
    two_back = lax.ppermute(key_value, "ctx", first)
    halfway = lax.ppermute(key_value, "ctx", mixed)

    shares = picked.reshape(stretches, -1, HD)
    shares = lax.all_to_all(shares, "ctx", split_axis=0, concat_axis=0, tiled=True)
    share = jnp.sum(shares.astype(jnp.float32), axis=0).astype(jnp.bfloat16)
    share, two_back = lax.optimization_barrier((share, two_back))
    swapped = lax.ppermute(two_back, "ctx", [(s, s ^ 1) for s in range(stretches)])
    onward = lax.ppermute(halfway, "ctx", last)
    shares = jnp.broadcast_to(share[None], (stretches,) + share.shape)
    columns = lax.all_to_all(shares, "ctx", split_axis=0, concat_axis=0, tiled=True).reshape(2, -1, HD)
    near = jnp.where(where[0] % 2 == 1, halfway, onward)
    sources = (key_value, swapped, two_back, near)

    pieces = []
    came = []
    after = []
    for number, offsets in enumerate(CALLS):
        wanted = tuple(offset % planes for offset in offsets)
        if number == len(CALLS) - 1:
            after = after + pieces[:2]
        results = attend_call(wanted, blocks, where, verticals, slashes, query_states, sources, columns, after)
        after = [results[0]]
        for offset, result in zip(wanted, results):
            if offset:
                result = lax.ppermute(result, "kvh", [(s, (s + offset) % planes) for s in range(planes)])
            pieces.append(result)
            came.append(offset)
    return assemble(tuple(came), where, pieces)


def solution(mesh):
    return jax.shard_map(
        shards,
        mesh=mesh,
        in_specs=(
            P("ctx", "kvh"),
            P("ctx", "kvh"),
            P("ctx", "kvh"),
            P("kvh", None),
            P("kvh", None),
        ),
        out_specs=P(("ctx", "kvh"), None),
        check_vma=False,
    )
```

time: 359 us -> 141 us (0.39)
  waiting for transfers between devices: 194 us -> 29.1 us
  Pallas kernels: 98 us -> 45.4 us
  starting transfers between devices: 40.5 us -> 60.2 us
  between operations: 13.8 us -> 0.5 us
  other arithmetic: 5.17 us -> 1.58 us
    psum x1 -> x0, waiting for transfers between devices: 170 us -> none  [shards(): columns = lax.psum(picked, 'ctx').reshape(2, -1, HD)]
    pallas_call x6 -> x7, Pallas kernels: 98 us -> 45.4 us  [the longest x5 39.1 us: attend_call(): pl.pallas_call(functools.partial(attend_kernel, offsets, blocks), out_sha...]
    all_to_all x0 -> x2, waiting for transfers between devices: none -> 24.7 us  [shards(): lax.all_to_all(shares, 'ctx', split_axis=0, concat_axis=0, tiled=True)]
    ppermute x3 -> x4, waiting for transfers between devices: 16.2 us -> 0.01 us  [the longest x1 0.01 us: shards(): halfway = lax.ppermute(key_value, 'ctx', mixed)]
    all_to_all x0 -> x2, starting transfers between devices: none -> 12.4 us  [shards(): lax.all_to_all(shares, 'ctx', split_axis=0, concat_axis=0, tiled=True)]
    ppermute x7, starting transfers between devices: 28.5 us -> 32.9 us  [shards(): lax.ppermute(result, 'kvh', [(s, (s + offset) % planes) for s in range(pl...]
    ppermute x3 -> x4, starting transfers between devices: 12 us -> 14.9 us  [the longest x1 6.27 us: shards(): two_back = lax.ppermute(key_value, 'ctx', first)]
  transfers between devices with their start and end apart: 11 -> 13, of which waited for: 4 -> 3; matrix products, arithmetic and copies ran while one was open for 2% -> 1% of each run, Pallas kernels for 8% -> 24%
where the time goes in v2:
time: 141 us; the launch traced here: 140 us
  starting transfers between devices  60.2 us (43%)
  Pallas kernels  45.4 us (32%)
  waiting for transfers between devices  29.1 us (21%)
  local copies, waits for them, and re-layouts  3.05 us (2%)
  other arithmetic  1.58 us (1%)
    pallas_call x5, Pallas kernels, attend_call(): pl.pallas_call(functools.partial(attend_kernel, offsets, blocks), out_sha...  39.1 us
    ppermute x7, starting transfers between devices, shards(): lax.ppermute(result, 'kvh', [(s, (s + offset) % planes) for s in range(pl...  32.9 us
    all_to_all x2, waiting for transfers between devices, shards(): lax.all_to_all(shares, 'ctx', split_axis=0, concat_axis=0, tiled=True)  24.7 us
    all_to_all x2, starting transfers between devices, shards(): lax.all_to_all(shares, 'ctx', split_axis=0, concat_axis=0, tiled=True)  12.4 us
    ppermute x1, starting transfers between devices, shards(): two_back = lax.ppermute(key_value, 'ctx', first)  6.27 us
    ppermute x1, starting transfers between devices, shards(): halfway = lax.ppermute(key_value, 'ctx', mixed)  5.78 us
    ppermute x7, waiting for transfers between devices, shards(): lax.ppermute(result, 'kvh', [(s, (s + offset) % planes) for s in range(pl...  4.39 us
    pallas_call x1, Pallas kernels, assemble(): pl.pallas_call(functools.partial(assemble_kernel, offsets), out_shape=jax...  3.57 us
  transfers between devices with their start and end apart: 13, of which 3 were waited for; matrix products, arithmetic and copies ran while one was open for 1% of the time, Pallas kernels for 24%

profile of v2, /device:TPU:1, one launch (start us, length us, event | category | flops | bytes accessed | tf_op | source)
XLA Modules:
  0.0 139.8 jit_solution(6699382897171683938)
XLA Ops:
  0.0 0.6 pad_add_fusion.where_ref
  0.6 2.7 %shard_map.55 = (bf16[2,1024,128]{2,1,0:T(8,128)(2,1)}, bf16[2,512,128]{2,1,0:T(8,128)(2,1)}) custom-call(s32[2]{0:T(128)} %pad_add_fusion.where_ref, s32[1,4]{1,0:T(1,128)} %verticals_ref.11, bf16[1024,128]{1,0:T(8,128)(2,1)} %keys_ref.1, bf16[1024,128]{1,0:T(8,128)(2,1)} %values_ref.1), custom_call_target="tpu_custom_call" | custom-call | bytes 1048576 | tf_op jit(solution)/shard_map/pallas_call | solution.py:57
  3.3 5.8 %collective-permute-start.2 = (bf16[2,1024,128]{2,1,0:T(8,128)(2,1)}, bf16[2,1024,128]{2,1,0:T(8,128)(2,1)S(1)}, u32[]{:S(2)}, u32[]{:S(2)}) collective-permute-start(bf16[2,1024,128]{2,1,0:T(8,128)(2,1)} %get-tuple-element.15.refs_0_), channel_id=1, source_target_pairs={{0,8},{8,48},{16,24},{24,0},{32,40},{40,80},{48,56},{56,32},{64,72... | collective-permute-start | bytes 1572872 | tf_op jit(solution)/shard_map/ppermute | solution.py:278
  9.1 6.3 %collective-permute-start = (bf16[2,1024,128]{2,1,0:T(8,128)(2,1)}, bf16[2,1024,128]{2,1,0:T(8,128)(2,1)S(1)}, u32[]{:S(2)}, u32[]{:S(2)}) collective-permute-start(bf16[2,1024,128]{2,1,0:T(8,128)(2,1)} %get-tuple-element.15.refs_0_), channel_id=1, source_target_pairs={{0,16},{8,24},{16,32},{24,40},{32,48},{40,56},{48,64},{56,72},{64,... | collective-permute-start | bytes 1572872 | tf_op jit(solution)/shard_map/ppermute | solution.py:277
  15.4 5.9 %all-to-all-start = ((bf16[64,16,128]{2,1,0:T(8,128)(2,1)}), bf16[64,16,128]{2,1,0:T(8,128)(2,1)S(1)}, u32[]{:S(2)}, u32[]{:S(2)}) async-start(bf16[64,16,128]{2,1,0:T(8,128)(2,1)} %bitcast.9), calls=%async_computation | async-start | bytes 524288 | tf_op jit(solution)/shard_map/all_to_all | solution.py:281
  21.3 0.0 collective-permute-done.2
  21.3 0.7 collective-permute-start.3
  22.0 12.5 %all-to-all-done = bf16[64,16,128]{2,1,0:T(8,128)(2,1)S(1)} async-done(((bf16[64,16,128]{2,1,0:T(8,128)(2,1)}), bf16[64,16,128]{2,1,0:T(8,128)(2,1)S(1)}, u32[]{:S(2)}, u32[]{:S(2)}) %all-to-all-start) | async-done | bytes 262176 | tf_op jit(solution)/shard_map/all_to_all | solution.py:281
  34.5 0.1 reduce_sum.12
  34.6 2.2 %collective-permute-start.1 = (bf16[2,1024,128]{2,1,0:T(8,128)(2,1)S(1)}, bf16[2,1024,128]{2,1,0:T(8,128)(2,1)S(1)}, u32[]{:S(2)}, u32[]{:S(2)}) collective-permute-start(bf16[2,1024,128]{2,1,0:T(8,128)(2,1)S(1)} %collective-permute-done.refs_2_), channel_id=1, source_target_pairs={{0,8},{8,0},{16,24},{24,16},{32,40},{40,32},{48,56},{56,48},{64,72... | collective-permute-start | bytes 1572872 | tf_op jit(solution)/shard_map/ppermute | solution.py:284
  36.7 0.7 broadcast_in_dim.2
  37.5 6.4 %all-to-all-start.1 = ((bf16[64,16,128]{2,1,0:T(8,128)(2,1)}), bf16[64,16,128]{2,1,0:T(8,128)(2,1)S(1)}, u32[]{:S(2)}, u32[]{:S(2)}) async-start(bf16[64,16,128]{2,1,0:T(8,128)(2,1)} %broadcast_in_dim.2), calls=%async_computation.1 | async-start | bytes 524288 | tf_op jit(solution)/shard_map/all_to_all | solution.py:287
  43.9 0.9 broadcast_select_fusion.refs_3_
  44.8 12.3 %all-to-all-done.1 = bf16[64,16,128]{2,1,0:T(8,128)(2,1)S(1)} async-done(((bf16[64,16,128]{2,1,0:T(8,128)(2,1)}), bf16[64,16,128]{2,1,0:T(8,128)(2,1)S(1)}, u32[]{:S(2)}, u32[]{:S(2)}) %all-to-all-start.1) | async-done | bytes 262176 | tf_op jit(solution)/shard_map/all_to_all | solution.py:287
  57.1 0.7 copy-done
  57.8 0.2 copy-done.2
  58.0 5.7 %shard_map.56.refs_5_ = bf16[128,1024]{1,0:T(8,128)(2,1)} custom-call(s32[2]{0:T(128)} %pad_add_fusion.where_ref, s32[1,4]{1,0:T(1,128)} %verticals_ref.11, s32[1,8]{1,0:T(1,128)} %slashes_ref.9, bf16[1024,1024]{1,0:T(8,128)(2,1)} %query_ref.9, bf16[2,1024,128]{2,1,0:T(8,128)(2,1)} %get-tuple-element.15.refs_0_, bf16[2,1024,128]{2,1,0:T(8,128)(2,1)} %copy-done.2, ...), custom_call_target="tpu_custom_call" | custom-call | flops 872415232 | bytes 1048576 | tf_op jit(solution)/shard_map/pallas_call | solution.py:200
  63.7 7.6 %collective-permute-start.4 = (bf16[128,1024]{1,0:T(8,128)(2,1)}, bf16[128,1024]{1,0:T(8,128)(2,1)S(1)}, u32[]{:S(2)}, u32[]{:S(2)}) collective-permute-start(bf16[128,1024]{1,0:T(8,128)(2,1)} %shard_map.56.refs_5_), channel_id=1, source_target_pairs={{0,3},{1,4},{2,5},{3,6},{4,7},{5,0},{6,1},{7,2},{8,11},{9,12},{10,... | collective-permute-start | bytes 786440 | tf_op jit(solution)/shard_map/ppermute | solution.py:302
  71.4 5.8 %shard_map.57.refs_5_ = bf16[128,1024]{1,0:T(8,128)(2,1)} custom-call(s32[2]{0:T(128)} %pad_add_fusion.where_ref, s32[1,4]{1,0:T(1,128)} %verticals_ref.11, s32[1,8]{1,0:T(1,128)} %slashes_ref.9, bf16[1024,1024]{1,0:T(8,128)(2,1)} %query_ref.9, bf16[2,1024,128]{2,1,0:T(8,128)(2,1)} %get-tuple-element.15.refs_0_, bf16[2,1024,128]{2,1,0:T(8,128)(2,1)} %copy-done.2, ...), custom_call_target="tpu_custom_call" | custom-call | flops 872415232 | bytes 1048576 | tf_op jit(solution)/shard_map/pallas_call | solution.py:200
  77.1 5.0 %collective-permute-start.5 = (bf16[128,1024]{1,0:T(8,128)(2,1)}, bf16[128,1024]{1,0:T(8,128)(2,1)S(1)}, u32[]{:S(2)}, u32[]{:S(2)}) collective-permute-start(bf16[128,1024]{1,0:T(8,128)(2,1)} %shard_map.57.refs_5_), channel_id=1, source_target_pairs={{0,5},{1,6},{2,7},{3,0},{4,1},{5,2},{6,3},{7,4},{8,13},{9,14},{10,... | collective-permute-start | bytes 786440 | tf_op jit(solution)/shard_map/ppermute | solution.py:302
  82.1 9.3 %shard_map.58 = (bf16[128,1024]{1,0:T(8,128)(2,1)}, bf16[128,1024]{1,0:T(8,128)(2,1)}) custom-call(s32[2]{0:T(128)} %pad_add_fusion.where_ref, s32[1,4]{1,0:T(1,128)} %verticals_ref.11, s32[1,8]{1,0:T(1,128)} %slashes_ref.9, bf16[1024,1024]{1,0:T(8,128)(2,1)} %query_ref.9, bf16[2,1024,128]{2,1,0:T(8,128)(2,1)} %get-tuple-element.15.refs_0_, ...), custom_call_target="tpu_custom_call" | custom-call | flops 1744830464 | bytes 2097152 | tf_op jit(solution)/shard_map/pallas_call | solution.py:200
  91.4 6.4 %collective-permute-start.7 = (bf16[128,1024]{1,0:T(8,128)(2,1)}, bf16[128,1024]{1,0:T(8,128)(2,1)S(1)}, u32[]{:S(2)}, u32[]{:S(2)}) collective-permute-start(bf16[128,1024]{1,0:T(8,128)(2,1)} %get-tuple-element.20), channel_id=1, source_target_pairs={{0,4},{1,5},{2,6},{3,7},{4,0},{5,1},{6,2},{7,3},{8,12},{9,13},{10,... | collective-permute-start | bytes 786440 | tf_op jit(solution)/shard_map/ppermute | solution.py:302
  97.8 4.0 %collective-permute-start.6 = (bf16[128,1024]{1,0:T(8,128)(2,1)}, bf16[128,1024]{1,0:T(8,128)(2,1)S(1)}, u32[]{:S(2)}, u32[]{:S(2)}) collective-permute-start(bf16[128,1024]{1,0:T(8,128)(2,1)} %get-tuple-element.19.refs_5_), channel_id=1, source_target_pairs={{0,2},{1,3},{2,4},{3,5},{4,6},{5,7},{6,0},{7,1},{8,10},{9,11},{10,... | collective-permute-start | bytes 786440 | tf_op jit(solution)/shard_map/ppermute | solution.py:302
  101.9 9.3 %shard_map.59 = (bf16[128,1024]{1,0:T(8,128)(2,1)}, bf16[128,1024]{1,0:T(8,128)(2,1)}) custom-call(s32[2]{0:T(128)} %pad_add_fusion.where_ref, s32[1,4]{1,0:T(1,128)} %verticals_ref.11, s32[1,8]{1,0:T(1,128)} %slashes_ref.9, bf16[1024,1024]{1,0:T(8,128)(2,1)} %query_ref.9, bf16[2,1024,128]{2,1,0:T(8,128)(2,1)} %get-tuple-element.15.refs_0_, ...), custom_call_target="tpu_custom_call" | custom-call | flops 1744830464 | bytes 2097152 | tf_op jit(solution)/shard_map/pallas_call | solution.py:200
  111.2 3.4 %collective-permute-start.9 = (bf16[128,1024]{1,0:T(8,128)(2,1)}, bf16[128,1024]{1,0:T(8,128)(2,1)S(1)}, u32[]{:S(2)}, u32[]{:S(2)}) collective-permute-start(bf16[128,1024]{1,0:T(8,128)(2,1)} %get-tuple-element.22), channel_id=1, source_target_pairs={{0,6},{1,7},{2,0},{3,1},{4,2},{5,3},{6,4},{7,5},{8,14},{9,15},{10,... | collective-permute-start | bytes 786440 | tf_op jit(solution)/shard_map/ppermute | solution.py:302
  114.6 3.1 %collective-permute-start.8 = (bf16[128,1024]{1,0:T(8,128)(2,1)}, bf16[128,1024]{1,0:T(8,128)(2,1)S(1)}, u32[]{:S(2)}, u32[]{:S(2)}) collective-permute-start(bf16[128,1024]{1,0:T(8,128)(2,1)} %get-tuple-element.21.refs_5_), channel_id=1, source_target_pairs={{0,1},{1,2},{2,3},{3,4},{4,5},{5,6},{6,7},{7,0},{8,9},{9,10},{10,1... | collective-permute-start | bytes 786440 | tf_op jit(solution)/shard_map/ppermute | solution.py:302
  117.7 0.7 copy-done.3
  118.4 9.1 %shard_map.60 = (bf16[128,1024]{1,0:T(8,128)(2,1)}, bf16[128,1024]{1,0:T(8,128)(2,1)}) custom-call(s32[2]{0:T(128)} %pad_add_fusion.where_ref, s32[1,4]{1,0:T(1,128)} %verticals_ref.11, s32[1,8]{1,0:T(1,128)} %slashes_ref.9, bf16[1024,1024]{1,0:T(8,128)(2,1)} %query_ref.9, bf16[2,1024,128]{2,1,0:T(8,128)(2,1)} %get-tuple-element.15.refs_0_, ...), custom_call_target="tpu_custom_call" | custom-call | flops 1744830464 | bytes 2097152 | tf_op jit(solution)/shard_map/pallas_call | solution.py:200
  127.5 3.4 %collective-permute-start.10 = (bf16[128,1024]{1,0:T(8,128)(2,1)}, bf16[128,1024]{1,0:T(8,128)(2,1)S(1)}, u32[]{:S(2)}, u32[]{:S(2)}) collective-permute-start(bf16[128,1024]{1,0:T(8,128)(2,1)} %get-tuple-element.23), channel_id=1, source_target_pairs={{0,7},{1,0},{2,1},{3,2},{4,3},{5,4},{6,5},{7,6},{8,15},{9,8},{10,9... | collective-permute-start | bytes 786440 | tf_op jit(solution)/shard_map/ppermute | solution.py:302
  131.0 4.4 %collective-permute-done.10.refs_6_ = bf16[128,1024]{1,0:T(8,128)(2,1)S(1)} collective-permute-done((bf16[128,1024]{1,0:T(8,128)(2,1)}, bf16[128,1024]{1,0:T(8,128)(2,1)S(1)}, u32[]{:S(2)}, u32[]{:S(2)}) %collective-permute-start.10) | collective-permute-done | bytes 262176 | tf_op jit(solution)/shard_map/ppermute | solution.py:302
  135.4 0.7 copy-done.9
  136.1 3.6 %shard_map.61 = bf16[128,8192]{1,0:T(8,128)(2,1)} custom-call(s32[2]{0:T(128)} %pad_add_fusion.where_ref, bf16[128,1024]{1,0:T(8,128)(2,1)} %copy-done.3, bf16[128,1024]{1,0:T(8,128)(2,1)} %copy-done.4, bf16[128,1024]{1,0:T(8,128)(2,1)} %copy-done.6, bf16[128,1024]{1,0:T(8,128)(2,1)} %copy-done.5, bf16[128,1024]{1,0:T(8,128)(2,1)} %copy-done.8, ...), custom_call_target="tpu_custom_call" | custom-call | bytes 4194304 | tf_op jit(solution)/shard_map/pallas_call | solution.py:241
  (25 shorter events, 0.1 us)
Async XLA Ops:
  3.3 18.0 %collective-permute-start.2 = (bf16[2,1024,128]{2,1,0:T(8,128)(2,1)}, bf16[2,1024,128]{2,1,0:T(8,128)(2,1)S(1)}, u32[]{:S(2)}, u32[]{:S(2)}) collective-permute-start(bf16[2,1024,128]{2,1,0:T(8,128)(2,1)} %get-tuple-element.15.refs_0_), channel_id=1, source_target_pairs={{0,8},{8,48},{16,24},{24,0},{32,40},{40,80},{48,56},{56,32},{64,72... | collective-permute-start | bytes 1572872 | tf_op jit(solution)/shard_map/ppermute | solution.py:278
  9.1 25.5 %collective-permute-start = (bf16[2,1024,128]{2,1,0:T(8,128)(2,1)}, bf16[2,1024,128]{2,1,0:T(8,128)(2,1)S(1)}, u32[]{:S(2)}, u32[]{:S(2)}) collective-permute-start(bf16[2,1024,128]{2,1,0:T(8,128)(2,1)} %get-tuple-element.15.refs_0_), channel_id=1, source_target_pairs={{0,16},{8,24},{16,32},{24,40},{32,48},{40,56},{48,64},{56,72},{64,... | collective-permute-start | bytes 1572872 | tf_op jit(solution)/shard_map/ppermute | solution.py:277
  15.4 19.1 %all-to-all-start = ((bf16[64,16,128]{2,1,0:T(8,128)(2,1)}), bf16[64,16,128]{2,1,0:T(8,128)(2,1)S(1)}, u32[]{:S(2)}, u32[]{:S(2)}) async-start(bf16[64,16,128]{2,1,0:T(8,128)(2,1)} %bitcast.9), calls=%async_computation | async-start | bytes 524288 | tf_op jit(solution)/shard_map/all_to_all | solution.py:281
  21.3 22.6 %collective-permute-start.3 = (bf16[2,1024,128]{2,1,0:T(8,128)(2,1)S(1)}, bf16[2,1024,128]{2,1,0:T(8,128)(2,1)S(1)}, u32[]{:S(2)}, u32[]{:S(2)}) collective-permute-start(bf16[2,1024,128]{2,1,0:T(8,128)(2,1)S(1)} %collective-permute-done.2), channel_id=1, source_target_pairs={{48,32},{0,48},{80,64},{32,80},{112,96},{64,112},{144,128},{96,144... | collective-permute-start | bytes 1572872 | tf_op jit(solution)/shard_map/ppermute | solution.py:285
  34.6 22.5 %copy-start.1 = (bf16[2,1024,128]{2,1,0:T(8,128)(2,1)}, bf16[2,1024,128]{2,1,0:T(8,128)(2,1)S(1)}, u32[]{:S(2)}) copy-start(bf16[2,1024,128]{2,1,0:T(8,128)(2,1)S(1)} %collective-permute-done.refs_2_) | copy-start | bytes 1572868
  34.6 22.5 %collective-permute-start.1 = (bf16[2,1024,128]{2,1,0:T(8,128)(2,1)S(1)}, bf16[2,1024,128]{2,1,0:T(8,128)(2,1)S(1)}, u32[]{:S(2)}, u32[]{:S(2)}) collective-permute-start(bf16[2,1024,128]{2,1,0:T(8,128)(2,1)S(1)} %collective-permute-done.refs_2_), channel_id=1, source_target_pairs={{0,8},{8,0},{16,24},{24,16},{32,40},{40,32},{48,56},{56,48},{64,72... | collective-permute-start | bytes 1572872 | tf_op jit(solution)/shard_map/ppermute | solution.py:284
  37.5 19.6 %all-to-all-start.1 = ((bf16[64,16,128]{2,1,0:T(8,128)(2,1)}), bf16[64,16,128]{2,1,0:T(8,128)(2,1)S(1)}, u32[]{:S(2)}, u32[]{:S(2)}) async-start(bf16[64,16,128]{2,1,0:T(8,128)(2,1)} %broadcast_in_dim.2), calls=%async_computation.1 | async-start | bytes 524288 | tf_op jit(solution)/shard_map/all_to_all | solution.py:287
  57.1 0.7 copy-start
  57.1 0.9 copy-start.2
  63.7 54.0 %collective-permute-start.4 = (bf16[128,1024]{1,0:T(8,128)(2,1)}, bf16[128,1024]{1,0:T(8,128)(2,1)S(1)}, u32[]{:S(2)}, u32[]{:S(2)}) collective-permute-start(bf16[128,1024]{1,0:T(8,128)(2,1)} %shard_map.56.refs_5_), channel_id=1, source_target_pairs={{0,3},{1,4},{2,5},{3,6},{4,7},{5,0},{6,1},{7,2},{8,11},{9,12},{10,... | collective-permute-start | bytes 786440 | tf_op jit(solution)/shard_map/ppermute | solution.py:302
  77.1 37.4 %collective-permute-start.5 = (bf16[128,1024]{1,0:T(8,128)(2,1)}, bf16[128,1024]{1,0:T(8,128)(2,1)S(1)}, u32[]{:S(2)}, u32[]{:S(2)}) collective-permute-start(bf16[128,1024]{1,0:T(8,128)(2,1)} %shard_map.57.refs_5_), channel_id=1, source_target_pairs={{0,5},{1,6},{2,7},{3,0},{4,1},{5,2},{6,3},{7,4},{8,13},{9,14},{10,... | collective-permute-start | bytes 786440 | tf_op jit(solution)/shard_map/ppermute | solution.py:302
  91.4 39.5 %collective-permute-start.7 = (bf16[128,1024]{1,0:T(8,128)(2,1)}, bf16[128,1024]{1,0:T(8,128)(2,1)S(1)}, u32[]{:S(2)}, u32[]{:S(2)}) collective-permute-start(bf16[128,1024]{1,0:T(8,128)(2,1)} %get-tuple-element.20), channel_id=1, source_target_pairs={{0,4},{1,5},{2,6},{3,7},{4,0},{5,1},{6,2},{7,3},{8,12},{9,13},{10,... | collective-permute-start | bytes 786440 | tf_op jit(solution)/shard_map/ppermute | solution.py:302
  97.8 33.1 %collective-permute-start.6 = (bf16[128,1024]{1,0:T(8,128)(2,1)}, bf16[128,1024]{1,0:T(8,128)(2,1)S(1)}, u32[]{:S(2)}, u32[]{:S(2)}) collective-permute-start(bf16[128,1024]{1,0:T(8,128)(2,1)} %get-tuple-element.19.refs_5_), channel_id=1, source_target_pairs={{0,2},{1,3},{2,4},{3,5},{4,6},{5,7},{6,0},{7,1},{8,10},{9,11},{10,... | collective-permute-start | bytes 786440 | tf_op jit(solution)/shard_map/ppermute | solution.py:302
  111.2 19.8 %collective-permute-start.9 = (bf16[128,1024]{1,0:T(8,128)(2,1)}, bf16[128,1024]{1,0:T(8,128)(2,1)S(1)}, u32[]{:S(2)}, u32[]{:S(2)}) collective-permute-start(bf16[128,1024]{1,0:T(8,128)(2,1)} %get-tuple-element.22), channel_id=1, source_target_pairs={{0,6},{1,7},{2,0},{3,1},{4,2},{5,3},{6,4},{7,5},{8,14},{9,15},{10,... | collective-permute-start | bytes 786440 | tf_op jit(solution)/shard_map/ppermute | solution.py:302
  114.6 3.1 %copy-start.4 = (bf16[128,1024]{1,0:T(8,128)(2,1)}, bf16[128,1024]{1,0:T(8,128)(2,1)S(1)}, u32[]{:S(2)}) copy-start(bf16[128,1024]{1,0:T(8,128)(2,1)S(1)} %collective-permute-done.5.refs_7_.refs_1_) | copy-start | bytes 786436
  114.6 16.4 %collective-permute-start.8 = (bf16[128,1024]{1,0:T(8,128)(2,1)}, bf16[128,1024]{1,0:T(8,128)(2,1)S(1)}, u32[]{:S(2)}, u32[]{:S(2)}) collective-permute-start(bf16[128,1024]{1,0:T(8,128)(2,1)} %get-tuple-element.21.refs_5_), channel_id=1, source_target_pairs={{0,1},{1,2},{2,3},{3,4},{4,5},{5,6},{6,7},{7,0},{8,9},{9,10},{10,1... | collective-permute-start | bytes 786440 | tf_op jit(solution)/shard_map/ppermute | solution.py:302
  117.7 0.7 copy-start.3
  127.5 7.9 %collective-permute-start.10 = (bf16[128,1024]{1,0:T(8,128)(2,1)}, bf16[128,1024]{1,0:T(8,128)(2,1)S(1)}, u32[]{:S(2)}, u32[]{:S(2)}) collective-permute-start(bf16[128,1024]{1,0:T(8,128)(2,1)} %get-tuple-element.23), channel_id=1, source_target_pairs={{0,7},{1,0},{2,1},{3,2},{4,3},{5,4},{6,5},{7,6},{8,15},{9,8},{10,9... | collective-permute-start | bytes 786440 | tf_op jit(solution)/shard_map/ppermute | solution.py:302
  130.9 4.5 %copy-start.5 = (bf16[128,1024]{1,0:T(8,128)(2,1)}, bf16[128,1024]{1,0:T(8,128)(2,1)S(1)}, u32[]{:S(2)}) copy-start(bf16[128,1024]{1,0:T(8,128)(2,1)S(1)} %collective-permute-done.7.refs_3_) | copy-start | bytes 786436
  130.9 4.4 %copy-start.6 = (bf16[128,1024]{1,0:T(8,128)(2,1)}, bf16[128,1024]{1,0:T(8,128)(2,1)S(1)}, u32[]{:S(2)}) copy-start(bf16[128,1024]{1,0:T(8,128)(2,1)S(1)} %collective-permute-done.6.refs_2_) | copy-start | bytes 786436
  131.0 4.4 %copy-start.7 = (bf16[128,1024]{1,0:T(8,128)(2,1)}, bf16[128,1024]{1,0:T(8,128)(2,1)S(1)}, u32[]{:S(2)}) copy-start(bf16[128,1024]{1,0:T(8,128)(2,1)S(1)} %collective-permute-done.9.refs_5_) | copy-start | bytes 786436
  131.0 4.4 %copy-start.8 = (bf16[128,1024]{1,0:T(8,128)(2,1)}, bf16[128,1024]{1,0:T(8,128)(2,1)S(1)}, u32[]{:S(2)}) copy-start(bf16[128,1024]{1,0:T(8,128)(2,1)S(1)} %collective-permute-done.8.refs_4_) | copy-start | bytes 786436
  135.4 0.7 copy-start.9

commit v3 on v0

v3 whole, which is shorter than its diff:
```python
import functools

import jax
import jax.numpy as jnp
from jax import lax
from jax.experimental import pallas as pl
from jax.experimental.pallas import tpu as pltpu
from jax.sharding import PartitionSpec as P

HD = 128
BLK = 128
REACH = 3
ONES = 16
FAR = -1e30
EXP2_SCALE = HD ** (-0.5) * 1.4426950408889634
VMEM_BYTES = 32 * 2**20
PAIR = 2
CALLS = ((3,), (-3,), (4,), (2,), (-2,), (1,), (-1,), (0,))
ARRIVED = {5: (0,), 6: (1,), 7: (2,)}
ROW = 8

ANYWHERE = pl.BlockSpec(memory_space=pl.ANY)
SCALARS = pl.BlockSpec(memory_space=pltpu.SMEM)
IN_VMEM = pl.BlockSpec(memory_space=pltpu.VMEM)
LIMITS = pltpu.CompilerParams(vmem_limit_bytes=VMEM_BYTES)
SMALL = pltpu.CompilerParams(vmem_limit_bytes=8 * 2**20)
MOST_VMEM = pltpu.CompilerParams(vmem_limit_bytes=60 * 2**20)


def small_cost(bytes_accessed):
    return pl.CostEstimate(flops=0, bytes_accessed=bytes_accessed, transcendentals=0)


def prepare_kernel(verticals_ref, keys_ref, values_ref, stacked_ref, picked_ref, verticals_buf, values_buf, sems):
    verticals_in = pltpu.make_async_copy(verticals_ref, verticals_buf, sems.at[0])
    values_in = pltpu.make_async_copy(values_ref, values_buf, sems.at[1])
    keys_in = pltpu.make_async_copy(keys_ref, stacked_ref.at[0], sems.at[2])
    values_in.start()
    keys_in.start()
    verticals_in.start()
    blocks = keys_ref.shape[0] // BLK
    values_in.wait()
    for j in range(blocks):
        rows = pl.ds(j * BLK, BLK)
        stacked_ref[1, rows, :] = values_buf[rows, :].T
    keys_in.wait()
    verticals_in.wait()
    for v in range(verticals_ref.shape[1]):
        block = verticals_buf[0, v]
        mine = lax.div(block, blocks) == lax.axis_index("ctx")
        row = pl.multiple_of(lax.rem(block, blocks) * BLK, BLK)
        rows = pl.ds(v * BLK, BLK)

        @pl.when(mine)
        def _(row=row, rows=rows):
            picked_ref[:, rows, :] = stacked_ref[:, pl.ds(row, BLK), :]

        @pl.when(jnp.logical_not(mine))
        def _(rows=rows):
            picked_ref[:, rows, :] = jnp.zeros((2, BLK, HD), jnp.bfloat16)


def prepare(verticals, keys, values):
    stretch = keys.shape[0]
    return pl.pallas_call(
        prepare_kernel,
        out_shape=[
            jax.ShapeDtypeStruct((2, stretch, HD), jnp.bfloat16),
            jax.ShapeDtypeStruct((2, verticals.shape[1] * BLK, HD), jnp.bfloat16),
        ],
        in_specs=[ANYWHERE] * 3,
        out_specs=[IN_VMEM, IN_VMEM],
        scratch_shapes=[
            pltpu.SMEM(verticals.shape, jnp.int32),
            pltpu.VMEM((stretch, HD), jnp.bfloat16),
            pltpu.SemaphoreType.DMA((3,)),
        ],
        compiler_params=MOST_VMEM,
        cost_estimate=small_cost(2**20),
    )(verticals, keys, values)


def plan_kernel(blocks, verticals_ref, slashes_ref, slots_ref):
    slash_count = slashes_ref.shape[1]
    vert_count = verticals_ref.shape[1]
    count = 1 + slash_count + vert_count
    rank_ctx = lax.axis_index("ctx")

    def one(local, _):
        block_now = rank_ctx * blocks + local
        ids = [block_now]
        ids += [block_now - slashes_ref[0, k] for k in range(slash_count)]
        ids += [verticals_ref[0, k] for k in range(vert_count)]
        base = REACH * blocks
        slots = [base + local]
        slots += [base + local - slashes_ref[0, k] for k in range(slash_count)]
        slots += [base + blocks + k for k in range(vert_count)]
        dead = base + blocks + vert_count + local
        slots_ref[local * count] = slots[0]
        for c in range(1, count):
            alive = (ids[c] >= 0) & (ids[c] <= block_now)
            for earlier in range(c):
                alive = alive & (ids[c] != ids[earlier])
            slots_ref[local * count + c] = jnp.where(alive, slots[c], dead)
        return 0

    lax.fori_loop(0, blocks, one, 0)


def plan(blocks, verticals, slashes):
    count = 1 + slashes.shape[1] + verticals.shape[1]
    return pl.pallas_call(
        functools.partial(plan_kernel, blocks),
        out_shape=jax.ShapeDtypeStruct((blocks * count,), jnp.int32),
        in_specs=[SCALARS] * 2,
        out_specs=SCALARS,
        compiler_params=SMALL,
        cost_estimate=small_cost(2**20),
    )(verticals, slashes)


def pool_kernel(blocks, own_ref, swapped_ref, two_ref, halfway_ref, onward_ref, columns_ref, pool_ref, sems):
    odd = lax.rem(lax.axis_index("ctx"), 2)
    rows = blocks * BLK

    def copy(source, stretch_at, number):
        return pltpu.make_async_copy(
            source, pool_ref.at[:, pl.ds(stretch_at * rows, source.shape[1]), :], sems.at[number]
        )

    always = [copy(two_ref, 1, 0), copy(own_ref, REACH, 1), copy(columns_ref, REACH + 1, 2)]
    on_odd = [copy(halfway_ref, 2, 3), copy(swapped_ref, 0, 4)]
    on_even = [copy(swapped_ref, 2, 3), copy(onward_ref, 0, 4)]

    @pl.when(odd == 1)
    def _():
        for item in on_odd:
            item.start()

    @pl.when(odd == 0)
    def _():
        for item in on_even:
            item.start()

    for item in always:
        item.start()
    for item in always + on_odd:
        item.wait()
    dead_at = (REACH + 1) * rows + columns_ref.shape[1]
    for local in range(blocks):
        first_key = pool_ref[0, pl.ds(REACH * rows + local * BLK, 1), :]
        at = pl.ds(dead_at + local * BLK, BLK)
        pool_ref[0, at, :] = jnp.broadcast_to(first_key, (BLK, HD))
        pool_ref[1, at, :] = jnp.zeros((BLK, HD), jnp.bfloat16)


def make_pool(blocks, own, swapped, two_back, halfway, onward, columns):
    rows = (REACH + 2) * blocks * BLK + columns.shape[1]
    return pl.pallas_call(
        functools.partial(pool_kernel, blocks),
        out_shape=jax.ShapeDtypeStruct((2, rows, HD), jnp.bfloat16),
        in_specs=[ANYWHERE] * 6,
        out_specs=IN_VMEM,
        scratch_shapes=[pltpu.SemaphoreType.DMA((5,))],
        compiler_params=SMALL,
        cost_estimate=small_cost(2**22),
    )(own, swapped, two_back, halfway, onward, columns)


def attend_kernel(offsets, blocks, slots_ref, pool_ref, query_ref, *refs):
    number = len(offsets)
    outs, (live_buf, scores_buf, weights_buf) = refs[-3 - number : -3], refs[-3:]
    count = slots_ref.shape[0] // blocks
    alive_slots = pool_ref.shape[1] // BLK - blocks
    columns = PAIR * BLK
    pairs = query_ref.shape[1] // (PAIR * HD)
    live_buf[0] = jnp.zeros((ONES, BLK), jnp.bfloat16)
    live_buf[1] = jnp.ones((ONES, BLK), jnp.bfloat16)
    rank_kvh = lax.axis_index("kvh")

    def head_columns(pair, h):
        return pl.ds(pl.multiple_of((pair * PAIR + h) * HD, HD), HD)

    def products(local, slots, pair, buf):
        rows = pl.ds(pl.multiple_of(local * BLK, BLK), BLK)
        queries = jnp.concatenate([query_ref[rows, head_columns(pair, h)].T for h in range(PAIR)], axis=1)
        keys = jnp.concatenate([pool_ref[0, rows, :] for rows in slots], axis=0)
        scores = jnp.dot(keys, queries, preferred_element_type=jnp.float32)
        key_at = lax.broadcasted_iota(jnp.int32, (BLK, columns), 0)
        query_at = lax.rem(lax.broadcasted_iota(jnp.int32, (BLK, columns), 1), BLK)
        own = jnp.where(key_at <= query_at, scores[:BLK], FAR)
        scores_buf[buf, pl.ds(0, BLK), :] = own
        scores_buf[buf, pl.ds(BLK, (count - 1) * BLK), :] = scores[BLK:]
        best = jnp.maximum(jnp.max(own, axis=0, keepdims=True), jnp.max(scores[BLK:], axis=0, keepdims=True))
        return best

    def soften(buf, best):
        for c in range(count):
            rows = pl.ds(c * BLK, BLK)
            weights = jnp.exp2((scores_buf[buf, rows, :] - best) * EXP2_SCALE)
            weights_buf[buf, rows, :] = weights.astype(jnp.bfloat16)

    def finish(at, slots, live, pair, buf):
        values = jnp.concatenate([pool_ref[1, rows, :] for rows in slots], axis=1)
        left = jnp.concatenate([values, jnp.concatenate([live_buf[n] for n in live], axis=1)], axis=0)
        total = jnp.dot(left, weights_buf[buf], preferred_element_type=jnp.float32)
        result = total[:HD] / total[HD : HD + 1]
        for h in range(PAIR):
            outs[at][:, head_columns(pair, h)] = result[:, h * BLK : (h + 1) * BLK].T.astype(jnp.bfloat16)

    for at, offset in enumerate(offsets):
        local = lax.rem(rank_kvh + offset, blocks)
        places = [slots_ref[local * count + c] for c in range(count)]
        slots = [pl.ds(pl.multiple_of(place * BLK, BLK), BLK) for place in places]
        live = [jnp.where(place < alive_slots, 1, 0) for place in places]

        def two(step, _, at=at, local=local, slots=slots, live=live):
            pair = 2 * step
            best = products(local, slots, pair, 0)
            best_next = products(local, slots, pair + 1, 1)
            soften(0, best)
            finish(at, slots, live, pair, 0)
            soften(1, best_next)
            finish(at, slots, live, pair + 1, 1)
            return 0

        if pairs > 1:
            lax.fori_loop(0, pairs // 2, two, 0)
        else:
            soften(0, products(local, slots, 0, 0))
            finish(at, slots, live, 0, 0)


def attend_call(offsets, blocks, slots, pool, query, after):
    count = slots.shape[0] // blocks
    width = count * BLK
    columns = PAIR * BLK
    query_width = query.shape[1]
    number = len(offsets)
    return pl.pallas_call(
        functools.partial(attend_kernel, offsets, blocks),
        out_shape=[jax.ShapeDtypeStruct((BLK, query_width), jnp.bfloat16)] * number,
        in_specs=[SCALARS, IN_VMEM, IN_VMEM] + [ANYWHERE] * len(after),
        out_specs=[IN_VMEM] * number,
        scratch_shapes=[
            pltpu.VMEM((2, ONES, BLK), jnp.bfloat16),
            pltpu.VMEM((2, width, columns), jnp.float32),
            pltpu.VMEM((2, width, columns), jnp.bfloat16),
        ],
        compiler_params=LIMITS,
        cost_estimate=pl.CostEstimate(
            flops=4 * number * BLK * query_width * width,
            bytes_accessed=number * 2**20,
            transcendentals=number * BLK * query_width // HD * width,
        ),
    )(slots, pool, query, *after)


def assemble_kernel(offsets, *refs):
    pieces, out_ref, sems = refs[:-2], refs[-2], refs[-1]
    count = len(offsets)
    width = pieces[0].shape[1]
    copies = []
    for n, offset in enumerate(offsets):
        source = lax.rem(lax.axis_index("kvh") + count - offset, count)
        at = pl.multiple_of(source * width, width)
        copies.append(pltpu.make_async_copy(pieces[n], out_ref.at[:, pl.ds(at, width)], sems.at[n]))
        copies[-1].start()
    for copy in copies:
        copy.wait()


def assemble(offsets, pieces):
    rows, width = pieces[0].shape
    return pl.pallas_call(
        functools.partial(assemble_kernel, offsets),
        out_shape=jax.ShapeDtypeStruct((rows, width * len(pieces)), jnp.bfloat16),
        in_specs=[IN_VMEM] * len(pieces),
        out_specs=ANYWHERE,
        scratch_shapes=[pltpu.SemaphoreType.DMA((len(pieces),))],
        compiler_params=SMALL,
        cost_estimate=small_cost(2**23),
    )(*pieces)


def window_routes(stretches):
    chips = stretches // 2
    first, mixed, last = [], [], []
    for chip in range(chips):
        y, x = divmod(chip, 4)
        for core in range(2):
            first.append((2 * chip + core, (2 * chip + core + 2) % stretches))
        mixed.append((2 * chip, 2 * chip + 1))
        half_y = y + 1 if x == 2 else y
        half = (half_y * 4 + (x - 1) % 4) % chips
        target = (chip + 2) % chips
        mixed.append((2 * chip + 1, 2 * half))
        last.append((2 * half, 2 * target))
    return first, mixed, last


def exchange(parts, groups):
    return lax.all_to_all(parts, "ctx", split_axis=0, concat_axis=0, axis_index_groups=groups, tiled=True)


def add_up(parts):
    return jnp.sum(parts.astype(jnp.float32), axis=0).astype(jnp.bfloat16)


def spread(part, copies):
    return jnp.broadcast_to(part[None], (copies,) + part.shape)


def shards(query_states, key_states, value_states, verticals, slashes):
    blocks = key_states.shape[0] // BLK
    stretches = lax.axis_size("ctx")
    planes = lax.axis_size("kvh")
    key_value, picked = prepare(verticals, key_states, value_states)

    lines = stretches // ROW
    rows = [[y * ROW + g for g in range(ROW)] for y in range(lines)]
    columns_of = [[y * ROW + g for y in range(lines)] for g in range(ROW)]
    share = add_up(exchange(picked.reshape(ROW, -1, HD), rows))

    share, key_value = lax.optimization_barrier((share, key_value))
    first, mixed, last = window_routes(stretches)
    two_back = lax.ppermute(key_value, "ctx", first)
    halfway = lax.ppermute(key_value, "ctx", mixed)
    swapped = lax.ppermute(two_back, "ctx", [(s, s ^ 1) for s in range(stretches)])
    onward = lax.ppermute(halfway, "ctx", last)

    share = add_up(exchange(spread(share, lines), columns_of))
    columns = exchange(spread(share, ROW), rows).reshape(2, -1, HD)

    slots = plan(blocks, verticals, slashes)
    pool = make_pool(blocks, key_value, swapped, two_back, halfway, onward, columns)
    pieces = []
    came = []
    after = []
    for number, offsets in enumerate(CALLS):
        wanted = tuple(offset % planes for offset in offsets)
        after = after + [pieces[n] for n in ARRIVED.get(number, ())]
        results = attend_call(wanted, blocks, slots, pool, query_states, after)
        after = [results[0]]
        for offset, result in zip(wanted, results):
            if offset:
                result = lax.ppermute(result, "kvh", [(s, (s + offset) % planes) for s in range(planes)])
            pieces.append(result)
            came.append(offset)
    return assemble(tuple(came), pieces)


def solution(mesh):
    return jax.shard_map(
        shards,
        mesh=mesh,
        in_specs=(
            P("ctx", "kvh"),
            P("ctx", "kvh"),
            P("ctx", "kvh"),
            P("kvh", None),
            P("kvh", None),
        ),
        out_specs=P(("ctx", "kvh"), None),
        check_vma=False,
    )
```

time: 649 us -> 132 us (0.20)
  the two profiles are of different devices: /device:TPU:31 before, /device:TPU:38 now
where the time goes in v3:
time: 132 us; the launch traced here: 131 us
  starting transfers between devices  67.3 us (51%)
  Pallas kernels  36.8 us (28%)
  waiting for transfers between devices  13.4 us (10%)
  blocking collectives  10.4 us (8%)
  local copies, waits for them, and re-layouts  2.77 us (2%)
    ppermute x7, starting transfers between devices, shards(): lax.ppermute(result, 'kvh', [(s, (s + offset) % planes) for s in range(pl...  40 us
    pallas_call x8, Pallas kernels, attend_call(): pl.pallas_call(functools.partial(attend_kernel, offsets, blocks), out_sha...  31.1 us
    all_to_all x2, starting transfers between devices, exchange(): lax.all_to_all(parts, 'ctx', split_axis=0, concat_axis=0, axis_index_grou...  17.2 us
    all_to_all x1, blocking collectives, exchange(): lax.all_to_all(parts, 'ctx', split_axis=0, concat_axis=0, axis_index_grou...  10.4 us
    all_to_all x2, waiting for transfers between devices, exchange(): lax.all_to_all(parts, 'ctx', split_axis=0, concat_axis=0, axis_index_grou...  9.48 us
    ppermute x1, starting transfers between devices, shards(): two_back = lax.ppermute(key_value, 'ctx', first)  4.09 us
    ppermute x7, waiting for transfers between devices, shards(): lax.ppermute(result, 'kvh', [(s, (s + offset) % planes) for s in range(pl...  3.62 us
  transfers between devices with their start and end apart: 13, of which 4 were waited for; matrix products, arithmetic and copies ran while one was open for 1% of the time, Pallas kernels for 22%

profile of v3, /device:TPU:38, one launch (start us, length us, event | category | flops | bytes accessed | tf_op | source)
XLA Modules:
  0.0 131.2 jit_solution(17620260683807488200)
XLA Ops:
  0.0 2.1 %shard_map.56 = (bf16[2,1024,128]{2,1,0:T(8,128)(2,1)}, bf16[2,512,128]{2,1,0:T(8,128)(2,1)}) custom-call(s32[1,4]{1,0:T(1,128)} %verticals_ref.3, bf16[1024,128]{1,0:T(8,128)(2,1)} %keys_ref.1, bf16[1024,128]{1,0:T(8,128)(2,1)} %values_ref.1), custom_call_target="tpu_custom_call" | custom-call | bytes 1048576 | tf_op jit(solution)/shard_map/pallas_call | solution.py:65
  2.1 10.4 %all_to_all.15 = bf16[8,128,128]{2,1,0:T(8,128)(2,1)S(1)} all-to-all(bf16[8,128,128]{2,1,0:T(8,128)(2,1)} %bitcast.3), channel_id=1, replica_groups={{0,8,16,24,32,40,48,56},{64,72,80,88,96,104,112,120},{128,136,144,152,1..., dimensions={0} | all-to-all | bytes 524288 | tf_op jit(solution)/shard_map/all_to_all | solution.py:303
  12.6 4.1 %collective-permute-start = (bf16[2,1024,128]{2,1,0:T(8,128)(2,1)}, bf16[2,1024,128]{2,1,0:T(8,128)(2,1)S(1)}, u32[]{:S(2)}, u32[]{:S(2)}) collective-permute-start(bf16[2,1024,128]{2,1,0:T(8,128)(2,1)} %get-tuple-element.11.own_ref), channel_id=1, source_target_pairs={{0,16},{8,24},{16,32},{24,40},{32,48},{40,56},{48,64},{56,72},{64,... | collective-permute-start | bytes 1572872 | tf_op jit(solution)/shard_map/ppermute | solution.py:327
  16.6 1.9 %collective-permute-start.2 = (bf16[2,1024,128]{2,1,0:T(8,128)(2,1)}, bf16[2,1024,128]{2,1,0:T(8,128)(2,1)S(1)}, u32[]{:S(2)}, u32[]{:S(2)}) collective-permute-start(bf16[2,1024,128]{2,1,0:T(8,128)(2,1)} %get-tuple-element.11.own_ref), channel_id=1, source_target_pairs={{0,8},{8,48},{16,24},{24,0},{32,40},{40,80},{48,56},{56,32},{64,72... | collective-permute-start | bytes 1572872 | tf_op jit(solution)/shard_map/ppermute | solution.py:328
  18.6 0.7 broadcast_in_dim.4
  19.3 8.3 %all-to-all-start.1 = ((bf16[8,128,128]{2,1,0:T(8,128)(2,1)}), bf16[8,128,128]{2,1,0:T(8,128)(2,1)S(1)}, u32[]{:S(2)}, u32[]{:S(2)}) async-start(bf16[8,128,128]{2,1,0:T(8,128)(2,1)} %broadcast_in_dim.4), calls=%async_computation.1 | async-start | bytes 524288 | tf_op jit(solution)/shard_map/all_to_all | solution.py:303
  27.6 0.3 collective-permute-done.two_ref
  28.0 1.9 %collective-permute-start.1 = (bf16[2,1024,128]{2,1,0:T(8,128)(2,1)S(1)}, bf16[2,1024,128]{2,1,0:T(8,128)(2,1)S(1)}, u32[]{:S(2)}, u32[]{:S(2)}) collective-permute-start(bf16[2,1024,128]{2,1,0:T(8,128)(2,1)S(1)} %collective-permute-done.two_ref), channel_id=1, source_target_pairs={{0,8},{8,0},{16,24},{24,16},{32,40},{40,32},{48,56},{56,48},{64,72... | collective-permute-start | bytes 1572872 | tf_op jit(solution)/shard_map/ppermute | solution.py:329
  29.9 2.2 %collective-permute-start.3 = (bf16[2,1024,128]{2,1,0:T(8,128)(2,1)S(1)}, bf16[2,1024,128]{2,1,0:T(8,128)(2,1)S(1)}, u32[]{:S(2)}, u32[]{:S(2)}) collective-permute-start(bf16[2,1024,128]{2,1,0:T(8,128)(2,1)S(1)} %collective-permute-done.2.halfway_ref), channel_id=1, source_target_pairs={{48,32},{0,48},{80,64},{32,80},{112,96},{64,112},{144,128},{96,144... | collective-permute-start | bytes 1572872 | tf_op jit(solution)/shard_map/ppermute | solution.py:330
  32.1 4.2 %all-to-all-done.1 = bf16[8,128,128]{2,1,0:T(8,128)(2,1)S(1)} async-done(((bf16[8,128,128]{2,1,0:T(8,128)(2,1)}), bf16[8,128,128]{2,1,0:T(8,128)(2,1)S(1)}, u32[]{:S(2)}, u32[]{:S(2)}) %all-to-all-start.1) | async-done | bytes 262176 | tf_op jit(solution)/shard_map/all_to_all | solution.py:303
  36.3 0.7 broadcast_in_dim.5
  37.1 8.8 %all-to-all-start.2 = ((bf16[8,128,128]{2,1,0:T(8,128)(2,1)}), bf16[8,128,128]{2,1,0:T(8,128)(2,1)S(1)}, u32[]{:S(2)}, u32[]{:S(2)}) async-start(bf16[8,128,128]{2,1,0:T(8,128)(2,1)} %broadcast_in_dim.5), calls=%async_computation.2 | async-start | bytes 524288 | tf_op jit(solution)/shard_map/all_to_all | solution.py:303
  45.9 1.9 %shard_map.55.slots_ref = s32[104]{0:T(128)S(1)} custom-call(s32[1,4]{1,0:T(1,128)S(1)} %copy-done.2, s32[1,8]{1,0:T(1,128)S(1)} %copy-done.3), custom_call_target="tpu_custom_call" | custom-call | bytes 1048576 | tf_op jit(solution)/shard_map/pallas_call | solution.py:112
  47.9 5.3 %all-to-all-done.2 = bf16[8,128,128]{2,1,0:T(8,128)(2,1)S(1)} async-done(((bf16[8,128,128]{2,1,0:T(8,128)(2,1)}), bf16[8,128,128]{2,1,0:T(8,128)(2,1)S(1)}, u32[]{:S(2)}, u32[]{:S(2)}) %all-to-all-start.2) | async-done | bytes 262176 | tf_op jit(solution)/shard_map/all_to_all | solution.py:303
  53.5 1.3 copy-done
  54.8 3.9 %shard_map.58.refs_0_ = bf16[128,1024]{1,0:T(8,128)(2,1)S(1)} custom-call(s32[104]{0:T(128)S(1)} %shard_map.55.slots_ref, bf16[2,5632,128]{2,1,0:T(8,128)(2,1)S(1)} %shard_map.57.pool_ref, bf16[1024,1024]{1,0:T(8,128)(2,1)S(1)} %copy-done), custom_call_target="tpu_custom_call" | custom-call | flops 872415232 | bytes 1048576 | tf_op jit(solution)/shard_map/pallas_call | solution.py:240
  58.7 7.9 %collective-permute-start.4 = (bf16[128,1024]{1,0:T(8,128)(2,1)S(1)}, bf16[128,1024]{1,0:T(8,128)(2,1)S(1)}, u32[]{:S(2)}, u32[]{:S(2)}) collective-permute-start(bf16[128,1024]{1,0:T(8,128)(2,1)S(1)} %shard_map.58.refs_0_), channel_id=1, source_target_pairs={{0,3},{1,4},{2,5},{3,6},{4,7},{5,0},{6,1},{7,2},{8,11},{9,12},{10,... | collective-permute-start | bytes 786440 | tf_op jit(solution)/shard_map/ppermute | solution.py:347
  66.6 3.9 %shard_map.59.refs_0_ = bf16[128,1024]{1,0:T(8,128)(2,1)S(1)} custom-call(s32[104]{0:T(128)S(1)} %shard_map.55.slots_ref, bf16[2,5632,128]{2,1,0:T(8,128)(2,1)S(1)} %shard_map.57.pool_ref, bf16[1024,1024]{1,0:T(8,128)(2,1)S(1)} %copy-done, bf16[128,1024]{1,0:T(8,128)(2,1)S(1)} %shard_map.58.refs_0_), custom_call_target="tpu_custom_call" | custom-call | flops 872415232 | bytes 1048576 | tf_op jit(solution)/shard_map/pallas_call | solution.py:240
  70.5 5.0 %collective-permute-start.5 = (bf16[128,1024]{1,0:T(8,128)(2,1)S(1)}, bf16[128,1024]{1,0:T(8,128)(2,1)S(1)}, u32[]{:S(2)}, u32[]{:S(2)}) collective-permute-start(bf16[128,1024]{1,0:T(8,128)(2,1)S(1)} %shard_map.59.refs_0_), channel_id=1, source_target_pairs={{0,5},{1,6},{2,7},{3,0},{4,1},{5,2},{6,3},{7,4},{8,13},{9,14},{10,... | collective-permute-start | bytes 786440 | tf_op jit(solution)/shard_map/ppermute | solution.py:347
  75.4 3.9 %shard_map.60.refs_0_ = bf16[128,1024]{1,0:T(8,128)(2,1)S(1)} custom-call(s32[104]{0:T(128)S(1)} %shard_map.55.slots_ref, bf16[2,5632,128]{2,1,0:T(8,128)(2,1)S(1)} %shard_map.57.pool_ref, bf16[1024,1024]{1,0:T(8,128)(2,1)S(1)} %copy-done, bf16[128,1024]{1,0:T(8,128)(2,1)S(1)} %shard_map.59.refs_0_), custom_call_target="tpu_custom_call" | custom-call | flops 872415232 | bytes 1048576 | tf_op jit(solution)/shard_map/pallas_call | solution.py:240
  79.3 6.9 %collective-permute-start.6 = (bf16[128,1024]{1,0:T(8,128)(2,1)S(1)}, bf16[128,1024]{1,0:T(8,128)(2,1)S(1)}, u32[]{:S(2)}, u32[]{:S(2)}) collective-permute-start(bf16[128,1024]{1,0:T(8,128)(2,1)S(1)} %shard_map.60.refs_0_), channel_id=1, source_target_pairs={{0,4},{1,5},{2,6},{3,7},{4,0},{5,1},{6,2},{7,3},{8,12},{9,13},{10,... | collective-permute-start | bytes 786440 | tf_op jit(solution)/shard_map/ppermute | solution.py:347
  86.2 3.9 %shard_map.61.refs_0_ = bf16[128,1024]{1,0:T(8,128)(2,1)S(1)} custom-call(s32[104]{0:T(128)S(1)} %shard_map.55.slots_ref, bf16[2,5632,128]{2,1,0:T(8,128)(2,1)S(1)} %shard_map.57.pool_ref, bf16[1024,1024]{1,0:T(8,128)(2,1)S(1)} %copy-done, bf16[128,1024]{1,0:T(8,128)(2,1)S(1)} %shard_map.60.refs_0_), custom_call_target="tpu_custom_call" | custom-call | flops 872415232 | bytes 1048576 | tf_op jit(solution)/shard_map/pallas_call | solution.py:240
  90.1 4.3 %collective-permute-start.7 = (bf16[128,1024]{1,0:T(8,128)(2,1)S(1)}, bf16[128,1024]{1,0:T(8,128)(2,1)S(1)}, u32[]{:S(2)}, u32[]{:S(2)}) collective-permute-start(bf16[128,1024]{1,0:T(8,128)(2,1)S(1)} %shard_map.61.refs_0_), channel_id=1, source_target_pairs={{0,2},{1,3},{2,4},{3,5},{4,6},{5,7},{6,0},{7,1},{8,10},{9,11},{10,... | collective-permute-start | bytes 786440 | tf_op jit(solution)/shard_map/ppermute | solution.py:347
  94.4 3.9 %shard_map.62.refs_0_ = bf16[128,1024]{1,0:T(8,128)(2,1)S(1)} custom-call(s32[104]{0:T(128)S(1)} %shard_map.55.slots_ref, bf16[2,5632,128]{2,1,0:T(8,128)(2,1)S(1)} %shard_map.57.pool_ref, bf16[1024,1024]{1,0:T(8,128)(2,1)S(1)} %copy-done, bf16[128,1024]{1,0:T(8,128)(2,1)S(1)} %shard_map.61.refs_0_), custom_call_target="tpu_custom_call" | custom-call | flops 872415232 | bytes 1048576 | tf_op jit(solution)/shard_map/pallas_call | solution.py:240
  98.3 3.8 %collective-permute-start.8 = (bf16[128,1024]{1,0:T(8,128)(2,1)S(1)}, bf16[128,1024]{1,0:T(8,128)(2,1)S(1)}, u32[]{:S(2)}, u32[]{:S(2)}) collective-permute-start(bf16[128,1024]{1,0:T(8,128)(2,1)S(1)} %shard_map.62.refs_0_), channel_id=1, source_target_pairs={{0,6},{1,7},{2,0},{3,1},{4,2},{5,3},{6,4},{7,5},{8,14},{9,15},{10,... | collective-permute-start | bytes 786440 | tf_op jit(solution)/shard_map/ppermute | solution.py:347
  102.2 3.9 %shard_map.63.refs_0_ = bf16[128,1024]{1,0:T(8,128)(2,1)S(1)} custom-call(s32[104]{0:T(128)S(1)} %shard_map.55.slots_ref, bf16[2,5632,128]{2,1,0:T(8,128)(2,1)S(1)} %shard_map.57.pool_ref, bf16[1024,1024]{1,0:T(8,128)(2,1)S(1)} %copy-done, bf16[128,1024]{1,0:T(8,128)(2,1)S(1)} %shard_map.62.refs_0_, bf16[128,1024]{1,0:T(8,128)(2,1)S(1)} %collective-permute-done.4.refs_1_.refs_0_), custom_call_target="tpu_custom_call" | custom-call | flops 872415232 | bytes 1048576 | tf_op jit(solution)/shard_map/pallas_call | solution.py:240
  106.1 3.9 %shard_map.64.refs_0_ = bf16[128,1024]{1,0:T(8,128)(2,1)S(1)} custom-call(s32[104]{0:T(128)S(1)} %shard_map.55.slots_ref, bf16[2,5632,128]{2,1,0:T(8,128)(2,1)S(1)} %shard_map.57.pool_ref, bf16[1024,1024]{1,0:T(8,128)(2,1)S(1)} %copy-done, bf16[128,1024]{1,0:T(8,128)(2,1)S(1)} %shard_map.63.refs_0_, bf16[128,1024]{1,0:T(8,128)(2,1)S(1)} %collective-permute-done.5.refs_1_), custom_call_target="tpu_custom_call" | custom-call | flops 872415232 | bytes 1048576 | tf_op jit(solution)/shard_map/pallas_call | solution.py:240
  110.0 10.2 %collective-permute-start.10 = (bf16[128,1024]{1,0:T(8,128)(2,1)S(1)}, bf16[128,1024]{1,0:T(8,128)(2,1)S(1)}, u32[]{:S(2)}, u32[]{:S(2)}) collective-permute-start(bf16[128,1024]{1,0:T(8,128)(2,1)S(1)} %shard_map.64.refs_0_), channel_id=1, source_target_pairs={{0,7},{1,0},{2,1},{3,2},{4,3},{5,4},{6,5},{7,6},{8,15},{9,8},{10,9... | collective-permute-start | bytes 786440 | tf_op jit(solution)/shard_map/ppermute | solution.py:347
  120.2 1.9 %collective-permute-start.9 = (bf16[128,1024]{1,0:T(8,128)(2,1)S(1)}, bf16[128,1024]{1,0:T(8,128)(2,1)S(1)}, u32[]{:S(2)}, u32[]{:S(2)}) collective-permute-start(bf16[128,1024]{1,0:T(8,128)(2,1)S(1)} %shard_map.63.refs_0_), channel_id=1, source_target_pairs={{0,1},{1,2},{2,3},{3,4},{4,5},{5,6},{6,7},{7,0},{8,9},{9,10},{10,1... | collective-permute-start | bytes 786440 | tf_op jit(solution)/shard_map/ppermute | solution.py:347
  122.1 3.9 %shard_map.65.refs_7_ = bf16[128,1024]{1,0:T(8,128)(2,1)S(1)} custom-call(s32[104]{0:T(128)S(1)} %shard_map.55.slots_ref, bf16[2,5632,128]{2,1,0:T(8,128)(2,1)S(1)} %shard_map.57.pool_ref, bf16[1024,1024]{1,0:T(8,128)(2,1)S(1)} %copy-done, bf16[128,1024]{1,0:T(8,128)(2,1)S(1)} %shard_map.64.refs_0_, bf16[128,1024]{1,0:T(8,128)(2,1)S(1)} %collective-permute-done.6.refs_1_.refs_2_), custom_call_target="tpu_custom_call" | custom-call | flops 872415232 | bytes 1048576 | tf_op jit(solution)/shard_map/pallas_call | solution.py:240
  126.0 3.6 %collective-permute-done.9.refs_5_ = bf16[128,1024]{1,0:T(8,128)(2,1)S(1)} collective-permute-done((bf16[128,1024]{1,0:T(8,128)(2,1)S(1)}, bf16[128,1024]{1,0:T(8,128)(2,1)S(1)}, u32[]{:S(2)}, u32[]{:S(2)}) %collective-permute-start.9) | collective-permute-done | bytes 262176 | tf_op jit(solution)/shard_map/ppermute | solution.py:347
  129.7 1.4 %shard_map.66 = bf16[128,8192]{1,0:T(8,128)(2,1)} custom-call(bf16[128,1024]{1,0:T(8,128)(2,1)S(1)} %collective-permute-done.4.refs_1_.refs_0_, bf16[128,1024]{1,0:T(8,128)(2,1)S(1)} %collective-permute-done.5.refs_1_, bf16[128,1024]{1,0:T(8,128)(2,1)S(1)} %collective-permute-done.6.refs_1_.refs_2_, bf16[128,1024]{1,0:T(8,128)(2,1)S(1)} %collective-permute-done.7.refs_3_, ...), custom_call_target="tpu_custom_call" | custom-call | bytes 8388608 | tf_op jit(solution)/shard_map/pallas_call | solution.py:275
  (19 shorter events, 0.4 us)
Async XLA Ops:
  0.0 45.9 %copy-start.2 = (s32[1,4]{1,0:T(1,128)S(1)}, s32[1,4]{1,0:T(1,128)}, u32[]{:S(2)}) copy-start(s32[1,4]{1,0:T(1,128)} %verticals_ref.3) | copy-start | bytes 52
  0.0 45.9 %copy-start.3 = (s32[1,8]{1,0:T(1,128)S(1)}, s32[1,8]{1,0:T(1,128)}, u32[]{:S(2)}) copy-start(s32[1,8]{1,0:T(1,128)} %slashes_ref.1) | copy-start | bytes 100
  2.1 51.1 %copy-start.1 = (bf16[2,1024,128]{2,1,0:T(8,128)(2,1)S(1)}, bf16[2,1024,128]{2,1,0:T(8,128)(2,1)}, u32[]{:S(2)}) copy-start(bf16[2,1024,128]{2,1,0:T(8,128)(2,1)} %get-tuple-element.11.own_ref) | copy-start | bytes 1572868
  12.6 15.4 %collective-permute-start = (bf16[2,1024,128]{2,1,0:T(8,128)(2,1)}, bf16[2,1024,128]{2,1,0:T(8,128)(2,1)S(1)}, u32[]{:S(2)}, u32[]{:S(2)}) collective-permute-start(bf16[2,1024,128]{2,1,0:T(8,128)(2,1)} %get-tuple-element.11.own_ref), channel_id=1, source_target_pairs={{0,16},{8,24},{16,32},{24,40},{32,48},{40,56},{48,64},{56,72},{64,... | collective-permute-start | bytes 1572872 | tf_op jit(solution)/shard_map/ppermute | solution.py:327
  16.6 13.2 %collective-permute-start.2 = (bf16[2,1024,128]{2,1,0:T(8,128)(2,1)}, bf16[2,1024,128]{2,1,0:T(8,128)(2,1)S(1)}, u32[]{:S(2)}, u32[]{:S(2)}) collective-permute-start(bf16[2,1024,128]{2,1,0:T(8,128)(2,1)} %get-tuple-element.11.own_ref), channel_id=1, source_target_pairs={{0,8},{8,48},{16,24},{24,0},{32,40},{40,80},{48,56},{56,32},{64,72... | collective-permute-start | bytes 1572872 | tf_op jit(solution)/shard_map/ppermute | solution.py:328
  19.3 17.0 %all-to-all-start.1 = ((bf16[8,128,128]{2,1,0:T(8,128)(2,1)}), bf16[8,128,128]{2,1,0:T(8,128)(2,1)S(1)}, u32[]{:S(2)}, u32[]{:S(2)}) async-start(bf16[8,128,128]{2,1,0:T(8,128)(2,1)} %broadcast_in_dim.4), calls=%async_computation.1 | async-start | bytes 524288 | tf_op jit(solution)/shard_map/all_to_all | solution.py:303
  28.0 25.2 %collective-permute-start.1 = (bf16[2,1024,128]{2,1,0:T(8,128)(2,1)S(1)}, bf16[2,1024,128]{2,1,0:T(8,128)(2,1)S(1)}, u32[]{:S(2)}, u32[]{:S(2)}) collective-permute-start(bf16[2,1024,128]{2,1,0:T(8,128)(2,1)S(1)} %collective-permute-done.two_ref), channel_id=1, source_target_pairs={{0,8},{8,0},{16,24},{24,16},{32,40},{40,32},{48,56},{56,48},{64,72... | collective-permute-start | bytes 1572872 | tf_op jit(solution)/shard_map/ppermute | solution.py:329
  29.9 23.3 %collective-permute-start.3 = (bf16[2,1024,128]{2,1,0:T(8,128)(2,1)S(1)}, bf16[2,1024,128]{2,1,0:T(8,128)(2,1)S(1)}, u32[]{:S(2)}, u32[]{:S(2)}) collective-permute-start(bf16[2,1024,128]{2,1,0:T(8,128)(2,1)S(1)} %collective-permute-done.2.halfway_ref), channel_id=1, source_target_pairs={{48,32},{0,48},{80,64},{32,80},{112,96},{64,112},{144,128},{96,144... | collective-permute-start | bytes 1572872 | tf_op jit(solution)/shard_map/ppermute | solution.py:330
  37.1 16.1 %all-to-all-start.2 = ((bf16[8,128,128]{2,1,0:T(8,128)(2,1)}), bf16[8,128,128]{2,1,0:T(8,128)(2,1)S(1)}, u32[]{:S(2)}, u32[]{:S(2)}) async-start(bf16[8,128,128]{2,1,0:T(8,128)(2,1)} %broadcast_in_dim.5), calls=%async_computation.2 | async-start | bytes 524288 | tf_op jit(solution)/shard_map/all_to_all | solution.py:303
  53.2 1.6 %copy-start = (bf16[1024,1024]{1,0:T(8,128)(2,1)S(1)}, bf16[1024,1024]{1,0:T(8,128)(2,1)}, u32[]{:S(2)}) copy-start(bf16[1024,1024]{1,0:T(8,128)(2,1)} %query_ref.15) | copy-start | bytes 6291460
  58.7 43.5 %collective-permute-start.4 = (bf16[128,1024]{1,0:T(8,128)(2,1)S(1)}, bf16[128,1024]{1,0:T(8,128)(2,1)S(1)}, u32[]{:S(2)}, u32[]{:S(2)}) collective-permute-start(bf16[128,1024]{1,0:T(8,128)(2,1)S(1)} %shard_map.58.refs_0_), channel_id=1, source_target_pairs={{0,3},{1,4},{2,5},{3,6},{4,7},{5,0},{6,1},{7,2},{8,11},{9,12},{10,... | collective-permute-start | bytes 786440 | tf_op jit(solution)/shard_map/ppermute | solution.py:347
  70.5 35.6 %collective-permute-start.5 = (bf16[128,1024]{1,0:T(8,128)(2,1)S(1)}, bf16[128,1024]{1,0:T(8,128)(2,1)S(1)}, u32[]{:S(2)}, u32[]{:S(2)}) collective-permute-start(bf16[128,1024]{1,0:T(8,128)(2,1)S(1)} %shard_map.59.refs_0_), channel_id=1, source_target_pairs={{0,5},{1,6},{2,7},{3,0},{4,1},{5,2},{6,3},{7,4},{8,13},{9,14},{10,... | collective-permute-start | bytes 786440 | tf_op jit(solution)/shard_map/ppermute | solution.py:347
  79.3 42.8 %collective-permute-start.6 = (bf16[128,1024]{1,0:T(8,128)(2,1)S(1)}, bf16[128,1024]{1,0:T(8,128)(2,1)S(1)}, u32[]{:S(2)}, u32[]{:S(2)}) collective-permute-start(bf16[128,1024]{1,0:T(8,128)(2,1)S(1)} %shard_map.60.refs_0_), channel_id=1, source_target_pairs={{0,4},{1,5},{2,6},{3,7},{4,0},{5,1},{6,2},{7,3},{8,12},{9,13},{10,... | collective-permute-start | bytes 786440 | tf_op jit(solution)/shard_map/ppermute | solution.py:347
  90.1 35.9 %collective-permute-start.7 = (bf16[128,1024]{1,0:T(8,128)(2,1)S(1)}, bf16[128,1024]{1,0:T(8,128)(2,1)S(1)}, u32[]{:S(2)}, u32[]{:S(2)}) collective-permute-start(bf16[128,1024]{1,0:T(8,128)(2,1)S(1)} %shard_map.61.refs_0_), channel_id=1, source_target_pairs={{0,2},{1,3},{2,4},{3,5},{4,6},{5,7},{6,0},{7,1},{8,10},{9,11},{10,... | collective-permute-start | bytes 786440 | tf_op jit(solution)/shard_map/ppermute | solution.py:347
  98.3 27.7 %collective-permute-start.8 = (bf16[128,1024]{1,0:T(8,128)(2,1)S(1)}, bf16[128,1024]{1,0:T(8,128)(2,1)S(1)}, u32[]{:S(2)}, u32[]{:S(2)}) collective-permute-start(bf16[128,1024]{1,0:T(8,128)(2,1)S(1)} %shard_map.62.refs_0_), channel_id=1, source_target_pairs={{0,6},{1,7},{2,0},{3,1},{4,2},{5,3},{6,4},{7,5},{8,14},{9,15},{10,... | collective-permute-start | bytes 786440 | tf_op jit(solution)/shard_map/ppermute | solution.py:347
  110.0 16.0 %collective-permute-start.10 = (bf16[128,1024]{1,0:T(8,128)(2,1)S(1)}, bf16[128,1024]{1,0:T(8,128)(2,1)S(1)}, u32[]{:S(2)}, u32[]{:S(2)}) collective-permute-start(bf16[128,1024]{1,0:T(8,128)(2,1)S(1)} %shard_map.64.refs_0_), channel_id=1, source_target_pairs={{0,7},{1,0},{2,1},{3,2},{4,3},{5,4},{6,5},{7,6},{8,15},{9,8},{10,9... | collective-permute-start | bytes 786440 | tf_op jit(solution)/shard_map/ppermute | solution.py:347
  120.2 9.5 %collective-permute-start.9 = (bf16[128,1024]{1,0:T(8,128)(2,1)S(1)}, bf16[128,1024]{1,0:T(8,128)(2,1)S(1)}, u32[]{:S(2)}, u32[]{:S(2)}) collective-permute-start(bf16[128,1024]{1,0:T(8,128)(2,1)S(1)} %shard_map.63.refs_0_), channel_id=1, source_target_pairs={{0,1},{1,2},{2,3},{3,4},{4,5},{5,6},{6,7},{7,0},{8,9},{9,10},{10,1... | collective-permute-start | bytes 786440 | tf_op jit(solution)/shard_map/ppermute | solution.py:347

commit v4 on v3

--- a/solution.py
+++ b/solution.py
@@ -14,9 +14,12 @@
 FAR = -1e30
 EXP2_SCALE = HD ** (-0.5) * 1.4426950408889634
 VMEM_BYTES = 32 * 2**20
-PAIR = 2
-CALLS = ((3,), (-3,), (4,), (2,), (-2,), (1,), (-1,), (0,))
-ARRIVED = {5: (0,), 6: (1,), 7: (2,)}
+PAIR = 4
+FAR_SIDE = 4
+BY_STEPS = -2
+OFFSETS = (3, -3, 2, 1, -1, 0)
+HALF = BLK // 2
+
 ROW = 8
 
 ANYWHERE = pl.BlockSpec(memory_space=pl.ANY)
@@ -173,17 +176,17 @@
     count = slots_ref.shape[0] // blocks
     alive_slots = pool_ref.shape[1] // BLK - blocks
     columns = PAIR * BLK
-    pairs = query_ref.shape[1] // (PAIR * HD)
+    sets = query_ref.shape[1] // (PAIR * HD)
     live_buf[0] = jnp.zeros((ONES, BLK), jnp.bfloat16)
     live_buf[1] = jnp.ones((ONES, BLK), jnp.bfloat16)
     rank_kvh = lax.axis_index("kvh")
 
-    def head_columns(pair, h):
-        return pl.ds(pl.multiple_of((pair * PAIR + h) * HD, HD), HD)
-
-    def products(local, slots, pair, buf):
+    def head_columns(which, h):
+        return pl.ds((which * PAIR + h) * HD, HD)
+
+    def products(local, slots, which, buf):
         rows = pl.ds(pl.multiple_of(local * BLK, BLK), BLK)
-        queries = jnp.concatenate([query_ref[rows, head_columns(pair, h)].T for h in range(PAIR)], axis=1)
+        queries = jnp.concatenate([query_ref[rows, head_columns(which, h)].T for h in range(PAIR)], axis=1)
         keys = jnp.concatenate([pool_ref[0, rows, :] for rows in slots], axis=0)
         scores = jnp.dot(keys, queries, preferred_element_type=jnp.float32)
         key_at = lax.broadcasted_iota(jnp.int32, (BLK, columns), 0)
@@ -191,8 +194,7 @@
         own = jnp.where(key_at <= query_at, scores[:BLK], FAR)
         scores_buf[buf, pl.ds(0, BLK), :] = own
         scores_buf[buf, pl.ds(BLK, (count - 1) * BLK), :] = scores[BLK:]
-        best = jnp.maximum(jnp.max(own, axis=0, keepdims=True), jnp.max(scores[BLK:], axis=0, keepdims=True))
-        return best
+        return jnp.maximum(jnp.max(own, axis=0, keepdims=True), jnp.max(scores[BLK:], axis=0, keepdims=True))
 
     def soften(buf, best):
         for c in range(count):
@@ -200,35 +202,35 @@
             weights = jnp.exp2((scores_buf[buf, rows, :] - best) * EXP2_SCALE)
             weights_buf[buf, rows, :] = weights.astype(jnp.bfloat16)
 
-    def finish(at, slots, live, pair, buf):
+    def store(at, which, h, result):
+        where = head_columns(which, h)
+        if number == 1:
+            outs[0][:, where] = result
+        elif at == 0:
+            outs[0][:, where] = result[:HALF]
+            outs[1][pl.ds(BLK, HALF), where] = result[HALF:]
+        else:
+            outs[1][pl.ds(0, BLK), where] = result
+
+    def finish(at, slots, live, which, buf):
         values = jnp.concatenate([pool_ref[1, rows, :] for rows in slots], axis=1)
         left = jnp.concatenate([values, jnp.concatenate([live_buf[n] for n in live], axis=1)], axis=0)
         total = jnp.dot(left, weights_buf[buf], preferred_element_type=jnp.float32)
         result = total[:HD] / total[HD : HD + 1]
         for h in range(PAIR):
-            outs[at][:, head_columns(pair, h)] = result[:, h * BLK : (h + 1) * BLK].T.astype(jnp.bfloat16)
+            store(at, which, h, result[:, h * BLK : (h + 1) * BLK].T.astype(jnp.bfloat16))
 
     for at, offset in enumerate(offsets):
         local = lax.rem(rank_kvh + offset, blocks)
         places = [slots_ref[local * count + c] for c in range(count)]
         slots = [pl.ds(pl.multiple_of(place * BLK, BLK), BLK) for place in places]
         live = [jnp.where(place < alive_slots, 1, 0) for place in places]
-
-        def two(step, _, at=at, local=local, slots=slots, live=live):
-            pair = 2 * step
-            best = products(local, slots, pair, 0)
-            best_next = products(local, slots, pair + 1, 1)
-            soften(0, best)
-            finish(at, slots, live, pair, 0)
-            soften(1, best_next)
-            finish(at, slots, live, pair + 1, 1)
-            return 0
-
-        if pairs > 1:
-            lax.fori_loop(0, pairs // 2, two, 0)
-        else:
-            soften(0, products(local, slots, 0, 0))
-            finish(at, slots, live, 0, 0)
+        best = [products(local, slots, which, which % 2) for which in range(min(2, sets))]
+        for which in range(sets):
+            soften(which % 2, best[which])
+            finish(at, slots, live, which, which % 2)
+            if which + 2 < sets:
+                best.append(products(local, slots, which + 2, which % 2))
 
 
 def attend_call(offsets, blocks, slots, pool, query, after):
@@ -237,9 +239,10 @@
     columns = PAIR * BLK
     query_width = query.shape[1]
     number = len(offsets)
+    rows = (BLK,) if number == 1 else (HALF, BLK + HALF)
     return pl.pallas_call(
         functools.partial(attend_kernel, offsets, blocks),
-        out_shape=[jax.ShapeDtypeStruct((BLK, query_width), jnp.bfloat16)] * number,
+        out_shape=[jax.ShapeDtypeStruct((n, query_width), jnp.bfloat16) for n in rows],
         in_specs=[SCALARS, IN_VMEM, IN_VMEM] + [ANYWHERE] * len(after),
         out_specs=[IN_VMEM] * number,
         scratch_shapes=[
@@ -256,25 +259,25 @@
     )(slots, pool, query, *after)
 
 
-def assemble_kernel(offsets, *refs):
+def assemble_kernel(places, planes, *refs):
     pieces, out_ref, sems = refs[:-2], refs[-2], refs[-1]
-    count = len(offsets)
     width = pieces[0].shape[1]
     copies = []
-    for n, offset in enumerate(offsets):
-        source = lax.rem(lax.axis_index("kvh") + count - offset, count)
+    for n, (offset, row, rows) in enumerate(places):
+        source = lax.rem(lax.axis_index("kvh") + planes - offset, planes)
         at = pl.multiple_of(source * width, width)
-        copies.append(pltpu.make_async_copy(pieces[n], out_ref.at[:, pl.ds(at, width)], sems.at[n]))
+        target = out_ref.at[pl.ds(row, rows), pl.ds(at, width)]
+        copies.append(pltpu.make_async_copy(pieces[n].at[pl.ds(0, rows), :], target, sems.at[n]))
         copies[-1].start()
     for copy in copies:
         copy.wait()
 
 
-def assemble(offsets, pieces):
-    rows, width = pieces[0].shape
-    return pl.pallas_call(
-        functools.partial(assemble_kernel, offsets),
-        out_shape=jax.ShapeDtypeStruct((rows, width * len(pieces)), jnp.bfloat16),
+def assemble(places, planes, pieces):
+    width = pieces[0].shape[1]
+    return pl.pallas_call(
+        functools.partial(assemble_kernel, places, planes),
+        out_shape=jax.ShapeDtypeStruct((BLK, width * planes), jnp.bfloat16),
         in_specs=[IN_VMEM] * len(pieces),
         out_specs=ANYWHERE,
         scratch_shapes=[pltpu.SemaphoreType.DMA((len(pieces),))],
@@ -321,33 +324,42 @@
     rows = [[y * ROW + g for g in range(ROW)] for y in range(lines)]
     columns_of = [[y * ROW + g for y in range(lines)] for g in range(ROW)]
     share = add_up(exchange(picked.reshape(ROW, -1, HD), rows))
-
-    share, key_value = lax.optimization_barrier((share, key_value))
+    share = add_up(exchange(spread(share, lines), columns_of))
+    columns = exchange(spread(share, ROW), rows).reshape(2, -1, HD)
+
     first, mixed, last = window_routes(stretches)
     two_back = lax.ppermute(key_value, "ctx", first)
     halfway = lax.ppermute(key_value, "ctx", mixed)
     swapped = lax.ppermute(two_back, "ctx", [(s, s ^ 1) for s in range(stretches)])
     onward = lax.ppermute(halfway, "ctx", last)
 
-    share = add_up(exchange(spread(share, lines), columns_of))
-    columns = exchange(spread(share, ROW), rows).reshape(2, -1, HD)
-
     slots = plan(blocks, verticals, slashes)
     pool = make_pool(blocks, key_value, swapped, two_back, halfway, onward, columns)
-    pieces = []
-    came = []
-    after = []
-    for number, offsets in enumerate(CALLS):
-        wanted = tuple(offset % planes for offset in offsets)
-        after = after + [pieces[n] for n in ARRIVED.get(number, ())]
-        results = attend_call(wanted, blocks, slots, pool, query_states, after)
-        after = [results[0]]
-        for offset, result in zip(wanted, results):
-            if offset:
-                result = lax.ppermute(result, "kvh", [(s, (s + offset) % planes) for s in range(planes)])
-            pieces.append(result)
-            came.append(offset)
-    return assemble(tuple(came), pieces)
+
+    def attend(offsets, after):
+        return attend_call(tuple(n % planes for n in offsets), blocks, slots, pool, query_states, after)
+
+    def send(block, offset):
+        return lax.ppermute(block, "kvh", [(s, (s + offset) % planes) for s in range(planes)])
+
+    upper, bundle = attend((FAR_SIDE, BY_STEPS), [])
+    after = [upper]
+    upper = send(upper, FAR_SIDE)
+    bundle = send(bundle, BY_STEPS)
+    lower = send(bundle[BLK:], BY_STEPS)
+    pieces = [upper, lower, bundle]
+    places = [(FAR_SIDE, 0, HALF), (FAR_SIDE, HALF, HALF), (BY_STEPS % planes, 0, BLK)]
+    arrived = {3: [bundle], 4: [upper]}
+    for number, offset in enumerate(OFFSETS):
+        (result,) = attend((offset,), after + arrived.get(number, []))
+        after = [result]
+        if offset:
+            result = send(result, offset)
+        if number == 0:
+            arrived[5] = [result]
+        pieces.append(result)
+        places.append((offset % planes, 0, BLK))
+    return assemble(tuple(places), planes, pieces)
 
 
 def solution(mesh):

time: 132 us -> 126 us (0.955)
  the two profiles are of different devices: /device:TPU:38 before, /device:TPU:1 now
where the time goes in v4:
time: 126 us; the launch traced here: 125 us
  starting transfers between devices  59.8 us (47%)
  Pallas kernels  30.5 us (24%)
  waiting for transfers between devices  17.1 us (14%)
  blocking collectives  14 us (11%)
  local copies, waits for them, and re-layouts  2.76 us (2%)
    ppermute x8, starting transfers between devices, send(): lax.ppermute(block, 'kvh', [(s, (s + offset) % planes) for s in range(pla...  34.6 us
    pallas_call x7, Pallas kernels, attend_call(): pl.pallas_call(functools.partial(attend_kernel, offsets, blocks), out_sha...  24.8 us
    all_to_all x1, blocking collectives, exchange(): lax.all_to_all(parts, 'ctx', split_axis=0, concat_axis=0, axis_index_grou...  14 us
    all_to_all x2, starting transfers between devices, exchange(): lax.all_to_all(parts, 'ctx', split_axis=0, concat_axis=0, axis_index_grou...  12 us
    all_to_all x2, waiting for transfers between devices, exchange(): lax.all_to_all(parts, 'ctx', split_axis=0, concat_axis=0, axis_index_grou...  10.7 us
    ppermute x8, waiting for transfers between devices, send(): lax.ppermute(block, 'kvh', [(s, (s + offset) % planes) for s in range(pla...  6.4 us
    ppermute x1, starting transfers between devices, shards(): halfway = lax.ppermute(key_value, 'ctx', mixed)  5.23 us
    ppermute x1, starting transfers between devices, shards(): two_back = lax.ppermute(key_value, 'ctx', first)  4.08 us
  transfers between devices with their start and end apart: 14, of which 3 were waited for; matrix products, arithmetic and copies ran while one was open for 1% of the time, Pallas kernels for 17%

profile of v4, /device:TPU:1, one launch (start us, length us, event | category | flops | bytes accessed | tf_op | source)
XLA Modules:
  0.0 124.7 jit_solution(12198034549221700720)
XLA Ops:
  0.0 2.1 %shard_map.56 = (bf16[2,1024,128]{2,1,0:T(8,128)(2,1)}, bf16[2,512,128]{2,1,0:T(8,128)(2,1)}) custom-call(s32[1,4]{1,0:T(1,128)} %verticals_ref.3, bf16[1024,128]{1,0:T(8,128)(2,1)} %keys_ref.1, bf16[1024,128]{1,0:T(8,128)(2,1)} %values_ref.1), custom_call_target="tpu_custom_call" | custom-call | bytes 1048576 | tf_op jit(solution)/shard_map/pallas_call | solution.py:68
  2.1 4.1 %collective-permute-start = (bf16[2,1024,128]{2,1,0:T(8,128)(2,1)}, bf16[2,1024,128]{2,1,0:T(8,128)(2,1)S(1)}, u32[]{:S(2)}, u32[]{:S(2)}) collective-permute-start(bf16[2,1024,128]{2,1,0:T(8,128)(2,1)} %get-tuple-element.9.own_ref), channel_id=1, source_target_pairs={{0,16},{8,24},{16,32},{24,40},{32,48},{40,56},{48,64},{56,72},{64,... | collective-permute-start | bytes 1572872 | tf_op jit(solution)/shard_map/ppermute | solution.py:331
  6.2 5.2 %collective-permute-start.2 = (bf16[2,1024,128]{2,1,0:T(8,128)(2,1)}, bf16[2,1024,128]{2,1,0:T(8,128)(2,1)S(1)}, u32[]{:S(2)}, u32[]{:S(2)}) collective-permute-start(bf16[2,1024,128]{2,1,0:T(8,128)(2,1)} %get-tuple-element.9.own_ref), channel_id=1, source_target_pairs={{0,8},{8,48},{16,24},{24,0},{32,40},{40,80},{48,56},{56,32},{64,72... | collective-permute-start | bytes 1572872 | tf_op jit(solution)/shard_map/ppermute | solution.py:332
  11.4 14.0 %all_to_all.15 = bf16[8,128,128]{2,1,0:T(8,128)(2,1)S(1)} all-to-all(bf16[8,128,128]{2,1,0:T(8,128)(2,1)} %bitcast.3), channel_id=1, replica_groups={{0,8,16,24,32,40,48,56},{64,72,80,88,96,104,112,120},{128,136,144,152,1..., dimensions={0} | all-to-all | bytes 524288 | tf_op jit(solution)/shard_map/all_to_all | solution.py:306
  25.5 0.7 broadcast_in_dim.4
  26.3 5.9 %all-to-all-start.1 = ((bf16[8,128,128]{2,1,0:T(8,128)(2,1)}), bf16[8,128,128]{2,1,0:T(8,128)(2,1)S(1)}, u32[]{:S(2)}, u32[]{:S(2)}) async-start(bf16[8,128,128]{2,1,0:T(8,128)(2,1)} %broadcast_in_dim.4), calls=%async_computation.1 | async-start | bytes 524288 | tf_op jit(solution)/shard_map/all_to_all | solution.py:306
  32.2 3.2 %collective-permute-start.1 = (bf16[2,1024,128]{2,1,0:T(8,128)(2,1)S(1)}, bf16[2,1024,128]{2,1,0:T(8,128)(2,1)S(1)}, u32[]{:S(2)}, u32[]{:S(2)}) collective-permute-start(bf16[2,1024,128]{2,1,0:T(8,128)(2,1)S(1)} %collective-permute-done.two_ref), channel_id=1, source_target_pairs={{0,8},{8,0},{16,24},{24,16},{32,40},{40,32},{48,56},{56,48},{64,72... | collective-permute-start | bytes 1572872 | tf_op jit(solution)/shard_map/ppermute | solution.py:333
  35.5 0.7 collective-permute-start.3
  36.2 6.1 %all-to-all-done.1 = bf16[8,128,128]{2,1,0:T(8,128)(2,1)S(1)} async-done(((bf16[8,128,128]{2,1,0:T(8,128)(2,1)}), bf16[8,128,128]{2,1,0:T(8,128)(2,1)S(1)}, u32[]{:S(2)}, u32[]{:S(2)}) %all-to-all-start.1) | async-done | bytes 262176 | tf_op jit(solution)/shard_map/all_to_all | solution.py:306
  42.3 0.7 broadcast_in_dim.5
  43.0 6.1 %all-to-all-start.2 = ((bf16[8,128,128]{2,1,0:T(8,128)(2,1)}), bf16[8,128,128]{2,1,0:T(8,128)(2,1)S(1)}, u32[]{:S(2)}, u32[]{:S(2)}) async-start(bf16[8,128,128]{2,1,0:T(8,128)(2,1)} %broadcast_in_dim.5), calls=%async_computation.2 | async-start | bytes 524288 | tf_op jit(solution)/shard_map/all_to_all | solution.py:306
  49.1 1.9 %shard_map.55.slots_ref = s32[104]{0:T(128)S(1)} custom-call(s32[1,4]{1,0:T(1,128)S(1)} %copy-done.2, s32[1,8]{1,0:T(1,128)S(1)} %copy-done.3), custom_call_target="tpu_custom_call" | custom-call | bytes 1048576 | tf_op jit(solution)/shard_map/pallas_call | solution.py:115
  51.1 4.6 %all-to-all-done.2 = bf16[8,128,128]{2,1,0:T(8,128)(2,1)S(1)} async-done(((bf16[8,128,128]{2,1,0:T(8,128)(2,1)}), bf16[8,128,128]{2,1,0:T(8,128)(2,1)S(1)}, u32[]{:S(2)}, u32[]{:S(2)}) %all-to-all-start.2) | async-done | bytes 262176 | tf_op jit(solution)/shard_map/all_to_all | solution.py:306
  55.7 0.3 shard_map.57.pool_ref
  56.0 1.3 %copy-done = bf16[1024,1024]{1,0:T(8,128)(2,1)S(1)} copy-done((bf16[1024,1024]{1,0:T(8,128)(2,1)S(1)}, bf16[1024,1024]{1,0:T(8,128)(2,1)}, u32[]{:S(2)}) %copy-start) | copy-done | bytes 2097176
  57.2 5.5 %shard_map.58 = (bf16[64,1024]{1,0:T(8,128)(2,1)S(1)}, bf16[192,1024]{1,0:T(8,128)(2,1)S(1)}) custom-call(s32[104]{0:T(128)S(1)} %shard_map.55.slots_ref, bf16[2,5632,128]{2,1,0:T(8,128)(2,1)S(1)} %shard_map.57.pool_ref, bf16[1024,1024]{1,0:T(8,128)(2,1)S(1)} %copy-done), custom_call_target="tpu_custom_call" | custom-call | flops 1744830464 | bytes 2097152 | tf_op jit(solution)/shard_map/pallas_call | solution.py:243
  62.7 10.7 %collective-permute-start.5 = (bf16[192,1024]{1,0:T(8,128)(2,1)S(1)}, bf16[192,1024]{1,0:T(8,128)(2,1)S(1)}, u32[]{:S(2)}, u32[]{:S(2)}) collective-permute-start(bf16[192,1024]{1,0:T(8,128)(2,1)S(1)} %get-tuple-element.12), channel_id=1, source_target_pairs={{0,6},{1,7},{2,0},{3,1},{4,2},{5,3},{6,4},{7,5},{8,14},{9,15},{10,... | collective-permute-start | bytes 1179656 | tf_op jit(solution)/shard_map/ppermute | solution.py:343
  73.4 1.9 %collective-permute-start.4 = (bf16[64,1024]{1,0:T(8,128)(2,1)S(1)}, bf16[64,1024]{1,0:T(8,128)(2,1)S(1)}, u32[]{:S(2)}, u32[]{:S(2)}) collective-permute-start(bf16[64,1024]{1,0:T(8,128)(2,1)S(1)} %get-tuple-element.11.refs_0_), channel_id=1, source_target_pairs={{0,4},{1,5},{2,6},{3,7},{4,0},{5,1},{6,2},{7,3},{8,12},{9,13},{10,... | collective-permute-start | bytes 393224 | tf_op jit(solution)/shard_map/ppermute | solution.py:343
  75.3 3.2 %shard_map.59.refs_0_ = bf16[128,1024]{1,0:T(8,128)(2,1)S(1)} custom-call(s32[104]{0:T(128)S(1)} %shard_map.55.slots_ref, bf16[2,5632,128]{2,1,0:T(8,128)(2,1)S(1)} %shard_map.57.pool_ref, bf16[1024,1024]{1,0:T(8,128)(2,1)S(1)} %copy-done, bf16[64,1024]{1,0:T(8,128)(2,1)S(1)} %get-tuple-element.11.refs_0_), custom_call_target="tpu_custom_call" | custom-call | flops 872415232 | bytes 1048576 | tf_op jit(solution)/shard_map/pallas_call | solution.py:243
  78.5 5.2 %collective-permute-start.7 = (bf16[128,1024]{1,0:T(8,128)(2,1)S(1)}, bf16[128,1024]{1,0:T(8,128)(2,1)S(1)}, u32[]{:S(2)}, u32[]{:S(2)}) collective-permute-start(bf16[128,1024]{1,0:T(8,128)(2,1)S(1)} %shard_map.59.refs_0_), channel_id=1, source_target_pairs={{0,3},{1,4},{2,5},{3,6},{4,7},{5,0},{6,1},{7,2},{8,11},{9,12},{10,... | collective-permute-start | bytes 786440 | tf_op jit(solution)/shard_map/ppermute | solution.py:343
  83.7 3.2 %shard_map.60.refs_0_ = bf16[128,1024]{1,0:T(8,128)(2,1)S(1)} custom-call(s32[104]{0:T(128)S(1)} %shard_map.55.slots_ref, bf16[2,5632,128]{2,1,0:T(8,128)(2,1)S(1)} %shard_map.57.pool_ref, bf16[1024,1024]{1,0:T(8,128)(2,1)S(1)} %copy-done, bf16[128,1024]{1,0:T(8,128)(2,1)S(1)} %shard_map.59.refs_0_), custom_call_target="tpu_custom_call" | custom-call | flops 872415232 | bytes 1048576 | tf_op jit(solution)/shard_map/pallas_call | solution.py:243
  86.9 4.2 %collective-permute-start.8 = (bf16[128,1024]{1,0:T(8,128)(2,1)S(1)}, bf16[128,1024]{1,0:T(8,128)(2,1)S(1)}, u32[]{:S(2)}, u32[]{:S(2)}) collective-permute-start(bf16[128,1024]{1,0:T(8,128)(2,1)S(1)} %shard_map.60.refs_0_), channel_id=1, source_target_pairs={{0,5},{1,6},{2,7},{3,0},{4,1},{5,2},{6,3},{7,4},{8,13},{9,14},{10,... | collective-permute-start | bytes 786440 | tf_op jit(solution)/shard_map/ppermute | solution.py:343
  91.1 3.2 %shard_map.61.refs_0_ = bf16[128,1024]{1,0:T(8,128)(2,1)S(1)} custom-call(s32[104]{0:T(128)S(1)} %shard_map.55.slots_ref, bf16[2,5632,128]{2,1,0:T(8,128)(2,1)S(1)} %shard_map.57.pool_ref, bf16[1024,1024]{1,0:T(8,128)(2,1)S(1)} %copy-done, bf16[128,1024]{1,0:T(8,128)(2,1)S(1)} %shard_map.60.refs_0_), custom_call_target="tpu_custom_call" | custom-call | flops 872415232 | bytes 1048576 | tf_op jit(solution)/shard_map/pallas_call | solution.py:243
  94.4 3.3 %collective-permute-start.9 = (bf16[128,1024]{1,0:T(8,128)(2,1)S(1)}, bf16[128,1024]{1,0:T(8,128)(2,1)S(1)}, u32[]{:S(2)}, u32[]{:S(2)}) collective-permute-start(bf16[128,1024]{1,0:T(8,128)(2,1)S(1)} %shard_map.61.refs_0_), channel_id=1, source_target_pairs={{0,2},{1,3},{2,4},{3,5},{4,6},{5,7},{6,0},{7,1},{8,10},{9,11},{10,... | collective-permute-start | bytes 786440 | tf_op jit(solution)/shard_map/ppermute | solution.py:343
  97.7 3.2 %shard_map.62.refs_0_ = bf16[128,1024]{1,0:T(8,128)(2,1)S(1)} custom-call(s32[104]{0:T(128)S(1)} %shard_map.55.slots_ref, bf16[2,5632,128]{2,1,0:T(8,128)(2,1)S(1)} %shard_map.57.pool_ref, bf16[1024,1024]{1,0:T(8,128)(2,1)S(1)} %copy-done, bf16[128,1024]{1,0:T(8,128)(2,1)S(1)} %shard_map.61.refs_0_, bf16[192,1024]{1,0:T(8,128)(2,1)S(1)} %collective-permute-done.5.refs_1_.refs_2_), custom_call_target="tpu_custom_call" | custom-call | flops 872415232 | bytes 1048576 | tf_op jit(solution)/shard_map/pallas_call | solution.py:243
  101.0 3.2 %shard_map.63.refs_0_ = bf16[128,1024]{1,0:T(8,128)(2,1)S(1)} custom-call(s32[104]{0:T(128)S(1)} %shard_map.55.slots_ref, bf16[2,5632,128]{2,1,0:T(8,128)(2,1)S(1)} %shard_map.57.pool_ref, bf16[1024,1024]{1,0:T(8,128)(2,1)S(1)} %copy-done, bf16[128,1024]{1,0:T(8,128)(2,1)S(1)} %shard_map.62.refs_0_, bf16[64,1024]{1,0:T(8,128)(2,1)S(1)} %collective-permute-done.4.refs_1_.refs_0_), custom_call_target="tpu_custom_call" | custom-call | flops 872415232 | bytes 1048576 | tf_op jit(solution)/shard_map/pallas_call | solution.py:243
  104.2 3.2 %collective-permute-start.11 = (bf16[128,1024]{1,0:T(8,128)(2,1)S(1)}, bf16[128,1024]{1,0:T(8,128)(2,1)S(1)}, u32[]{:S(2)}, u32[]{:S(2)}) collective-permute-start(bf16[128,1024]{1,0:T(8,128)(2,1)S(1)} %shard_map.63.refs_0_), channel_id=1, source_target_pairs={{0,7},{1,0},{2,1},{3,2},{4,3},{5,4},{6,5},{7,6},{8,15},{9,8},{10,9... | collective-permute-start | bytes 786440 | tf_op jit(solution)/shard_map/ppermute | solution.py:343
  107.4 2.1 %collective-permute-start.10 = (bf16[128,1024]{1,0:T(8,128)(2,1)S(1)}, bf16[128,1024]{1,0:T(8,128)(2,1)S(1)}, u32[]{:S(2)}, u32[]{:S(2)}) collective-permute-start(bf16[128,1024]{1,0:T(8,128)(2,1)S(1)} %shard_map.62.refs_0_), channel_id=1, source_target_pairs={{0,1},{1,2},{2,3},{3,4},{4,5},{5,6},{6,7},{7,0},{8,9},{9,10},{10,1... | collective-permute-start | bytes 786440 | tf_op jit(solution)/shard_map/ppermute | solution.py:343
  109.5 4.0 %collective-permute-start.6 = (bf16[64,1024]{1,0:T(8,128)(2,1)S(1)}, bf16[64,1024]{1,0:T(8,128)(2,1)S(1)}, u32[]{:S(2)}, u32[]{:S(2)}) collective-permute-start(bf16[64,1024]{1,0:T(8,128)(2,1)S(1)} %slice.4), channel_id=1, source_target_pairs={{0,6},{1,7},{2,0},{3,1},{4,2},{5,3},{6,4},{7,5},{8,14},{9,15},{10,... | collective-permute-start | bytes 393224 | tf_op jit(solution)/shard_map/ppermute | solution.py:343
  113.6 3.2 %shard_map.64.refs_8_ = bf16[128,1024]{1,0:T(8,128)(2,1)S(1)} custom-call(s32[104]{0:T(128)S(1)} %shard_map.55.slots_ref, bf16[2,5632,128]{2,1,0:T(8,128)(2,1)S(1)} %shard_map.57.pool_ref, bf16[1024,1024]{1,0:T(8,128)(2,1)S(1)} %copy-done, bf16[128,1024]{1,0:T(8,128)(2,1)S(1)} %shard_map.63.refs_0_, bf16[128,1024]{1,0:T(8,128)(2,1)S(1)} %collective-permute-done.7.refs_1_.refs_3_), custom_call_target="tpu_custom_call" | custom-call | flops 872415232 | bytes 1048576 | tf_op jit(solution)/shard_map/pallas_call | solution.py:243
  116.8 6.4 %collective-permute-done.6.refs_1_ = bf16[64,1024]{1,0:T(8,128)(2,1)S(1)} collective-permute-done((bf16[64,1024]{1,0:T(8,128)(2,1)S(1)}, bf16[64,1024]{1,0:T(8,128)(2,1)S(1)}, u32[]{:S(2)}, u32[]{:S(2)}) %collective-permute-start.6) | collective-permute-done | bytes 131104 | tf_op jit(solution)/shard_map/ppermute | solution.py:343
  123.2 1.4 %shard_map.65 = bf16[128,8192]{1,0:T(8,128)(2,1)} custom-call(bf16[64,1024]{1,0:T(8,128)(2,1)S(1)} %collective-permute-done.4.refs_1_.refs_0_, bf16[64,1024]{1,0:T(8,128)(2,1)S(1)} %collective-permute-done.6.refs_1_, bf16[192,1024]{1,0:T(8,128)(2,1)S(1)} %collective-permute-done.5.refs_1_.refs_2_, ...), custom_call_target="tpu_custom_call" | custom-call | bytes 8388608 | tf_op jit(solution)/shard_map/pallas_call | solution.py:278
  (21 shorter events, 0.1 us)
Async XLA Ops:
  0.0 49.1 %copy-start.2 = (s32[1,4]{1,0:T(1,128)S(1)}, s32[1,4]{1,0:T(1,128)}, u32[]{:S(2)}) copy-start(s32[1,4]{1,0:T(1,128)} %verticals_ref.3) | copy-start | bytes 52
  0.0 49.1 %copy-start.3 = (s32[1,8]{1,0:T(1,128)S(1)}, s32[1,8]{1,0:T(1,128)}, u32[]{:S(2)}) copy-start(s32[1,8]{1,0:T(1,128)} %slashes_ref.1) | copy-start | bytes 100
  2.1 53.5 %copy-start.1 = (bf16[2,1024,128]{2,1,0:T(8,128)(2,1)S(1)}, bf16[2,1024,128]{2,1,0:T(8,128)(2,1)}, u32[]{:S(2)}) copy-start(bf16[2,1024,128]{2,1,0:T(8,128)(2,1)} %get-tuple-element.9.own_ref) | copy-start | bytes 1572868
  2.1 30.1 %collective-permute-start = (bf16[2,1024,128]{2,1,0:T(8,128)(2,1)}, bf16[2,1024,128]{2,1,0:T(8,128)(2,1)S(1)}, u32[]{:S(2)}, u32[]{:S(2)}) collective-permute-start(bf16[2,1024,128]{2,1,0:T(8,128)(2,1)} %get-tuple-element.9.own_ref), channel_id=1, source_target_pairs={{0,16},{8,24},{16,32},{24,40},{32,48},{40,56},{48,64},{56,72},{64,... | collective-permute-start | bytes 1572872 | tf_op jit(solution)/shard_map/ppermute | solution.py:331
  6.2 29.2 %collective-permute-start.2 = (bf16[2,1024,128]{2,1,0:T(8,128)(2,1)}, bf16[2,1024,128]{2,1,0:T(8,128)(2,1)S(1)}, u32[]{:S(2)}, u32[]{:S(2)}) collective-permute-start(bf16[2,1024,128]{2,1,0:T(8,128)(2,1)} %get-tuple-element.9.own_ref), channel_id=1, source_target_pairs={{0,8},{8,48},{16,24},{24,0},{32,40},{40,80},{48,56},{56,32},{64,72... | collective-permute-start | bytes 1572872 | tf_op jit(solution)/shard_map/ppermute | solution.py:332
  26.3 16.0 %all-to-all-start.1 = ((bf16[8,128,128]{2,1,0:T(8,128)(2,1)}), bf16[8,128,128]{2,1,0:T(8,128)(2,1)S(1)}, u32[]{:S(2)}, u32[]{:S(2)}) async-start(bf16[8,128,128]{2,1,0:T(8,128)(2,1)} %broadcast_in_dim.4), calls=%async_computation.1 | async-start | bytes 524288 | tf_op jit(solution)/shard_map/all_to_all | solution.py:306
  32.2 23.4 %collective-permute-start.1 = (bf16[2,1024,128]{2,1,0:T(8,128)(2,1)S(1)}, bf16[2,1024,128]{2,1,0:T(8,128)(2,1)S(1)}, u32[]{:S(2)}, u32[]{:S(2)}) collective-permute-start(bf16[2,1024,128]{2,1,0:T(8,128)(2,1)S(1)} %collective-permute-done.two_ref), channel_id=1, source_target_pairs={{0,8},{8,0},{16,24},{24,16},{32,40},{40,32},{48,56},{56,48},{64,72... | collective-permute-start | bytes 1572872 | tf_op jit(solution)/shard_map/ppermute | solution.py:333
  35.5 20.2 %collective-permute-start.3 = (bf16[2,1024,128]{2,1,0:T(8,128)(2,1)S(1)}, bf16[2,1024,128]{2,1,0:T(8,128)(2,1)S(1)}, u32[]{:S(2)}, u32[]{:S(2)}) collective-permute-start(bf16[2,1024,128]{2,1,0:T(8,128)(2,1)S(1)} %collective-permute-done.2.halfway_ref), channel_id=1, source_target_pairs={{48,32},{0,48},{80,64},{32,80},{112,96},{64,112},{144,128},{96,144... | collective-permute-start | bytes 1572872 | tf_op jit(solution)/shard_map/ppermute | solution.py:334
  43.0 12.6 %all-to-all-start.2 = ((bf16[8,128,128]{2,1,0:T(8,128)(2,1)}), bf16[8,128,128]{2,1,0:T(8,128)(2,1)S(1)}, u32[]{:S(2)}, u32[]{:S(2)}) async-start(bf16[8,128,128]{2,1,0:T(8,128)(2,1)} %broadcast_in_dim.5), calls=%async_computation.2 | async-start | bytes 524288 | tf_op jit(solution)/shard_map/all_to_all | solution.py:306
  55.6 1.6 %copy-start = (bf16[1024,1024]{1,0:T(8,128)(2,1)S(1)}, bf16[1024,1024]{1,0:T(8,128)(2,1)}, u32[]{:S(2)}) copy-start(bf16[1024,1024]{1,0:T(8,128)(2,1)} %query_ref.13) | copy-start | bytes 6291460
  62.7 35.0 %collective-permute-start.5 = (bf16[192,1024]{1,0:T(8,128)(2,1)S(1)}, bf16[192,1024]{1,0:T(8,128)(2,1)S(1)}, u32[]{:S(2)}, u32[]{:S(2)}) collective-permute-start(bf16[192,1024]{1,0:T(8,128)(2,1)S(1)} %get-tuple-element.12), channel_id=1, source_target_pairs={{0,6},{1,7},{2,0},{3,1},{4,2},{5,3},{6,4},{7,5},{8,14},{9,15},{10,... | collective-permute-start | bytes 1179656 | tf_op jit(solution)/shard_map/ppermute | solution.py:343
  73.4 27.6 %collective-permute-start.4 = (bf16[64,1024]{1,0:T(8,128)(2,1)S(1)}, bf16[64,1024]{1,0:T(8,128)(2,1)S(1)}, u32[]{:S(2)}, u32[]{:S(2)}) collective-permute-start(bf16[64,1024]{1,0:T(8,128)(2,1)S(1)} %get-tuple-element.11.refs_0_), channel_id=1, source_target_pairs={{0,4},{1,5},{2,6},{3,7},{4,0},{5,1},{6,2},{7,3},{8,12},{9,13},{10,... | collective-permute-start | bytes 393224 | tf_op jit(solution)/shard_map/ppermute | solution.py:343
  78.5 31.0 %collective-permute-start.7 = (bf16[128,1024]{1,0:T(8,128)(2,1)S(1)}, bf16[128,1024]{1,0:T(8,128)(2,1)S(1)}, u32[]{:S(2)}, u32[]{:S(2)}) collective-permute-start(bf16[128,1024]{1,0:T(8,128)(2,1)S(1)} %shard_map.59.refs_0_), channel_id=1, source_target_pairs={{0,3},{1,4},{2,5},{3,6},{4,7},{5,0},{6,1},{7,2},{8,11},{9,12},{10,... | collective-permute-start | bytes 786440 | tf_op jit(solution)/shard_map/ppermute | solution.py:343
  86.9 29.9 %collective-permute-start.8 = (bf16[128,1024]{1,0:T(8,128)(2,1)S(1)}, bf16[128,1024]{1,0:T(8,128)(2,1)S(1)}, u32[]{:S(2)}, u32[]{:S(2)}) collective-permute-start(bf16[128,1024]{1,0:T(8,128)(2,1)S(1)} %shard_map.60.refs_0_), channel_id=1, source_target_pairs={{0,5},{1,6},{2,7},{3,0},{4,1},{5,2},{6,3},{7,4},{8,13},{9,14},{10,... | collective-permute-start | bytes 786440 | tf_op jit(solution)/shard_map/ppermute | solution.py:343
  94.4 22.4 %collective-permute-start.9 = (bf16[128,1024]{1,0:T(8,128)(2,1)S(1)}, bf16[128,1024]{1,0:T(8,128)(2,1)S(1)}, u32[]{:S(2)}, u32[]{:S(2)}) collective-permute-start(bf16[128,1024]{1,0:T(8,128)(2,1)S(1)} %shard_map.61.refs_0_), channel_id=1, source_target_pairs={{0,2},{1,3},{2,4},{3,5},{4,6},{5,7},{6,0},{7,1},{8,10},{9,11},{10,... | collective-permute-start | bytes 786440 | tf_op jit(solution)/shard_map/ppermute | solution.py:343
  104.2 19.0 %collective-permute-start.11 = (bf16[128,1024]{1,0:T(8,128)(2,1)S(1)}, bf16[128,1024]{1,0:T(8,128)(2,1)S(1)}, u32[]{:S(2)}, u32[]{:S(2)}) collective-permute-start(bf16[128,1024]{1,0:T(8,128)(2,1)S(1)} %shard_map.63.refs_0_), channel_id=1, source_target_pairs={{0,7},{1,0},{2,1},{3,2},{4,3},{5,4},{6,5},{7,6},{8,15},{9,8},{10,9... | collective-permute-start | bytes 786440 | tf_op jit(solution)/shard_map/ppermute | solution.py:343
  107.4 15.8 %collective-permute-start.10 = (bf16[128,1024]{1,0:T(8,128)(2,1)S(1)}, bf16[128,1024]{1,0:T(8,128)(2,1)S(1)}, u32[]{:S(2)}, u32[]{:S(2)}) collective-permute-start(bf16[128,1024]{1,0:T(8,128)(2,1)S(1)} %shard_map.62.refs_0_), channel_id=1, source_target_pairs={{0,1},{1,2},{2,3},{3,4},{4,5},{5,6},{6,7},{7,0},{8,9},{9,10},{10,1... | collective-permute-start | bytes 786440 | tf_op jit(solution)/shard_map/ppermute | solution.py:343
  109.5 13.7 %collective-permute-start.6 = (bf16[64,1024]{1,0:T(8,128)(2,1)S(1)}, bf16[64,1024]{1,0:T(8,128)(2,1)S(1)}, u32[]{:S(2)}, u32[]{:S(2)}) collective-permute-start(bf16[64,1024]{1,0:T(8,128)(2,1)S(1)} %slice.4), channel_id=1, source_target_pairs={{0,6},{1,7},{2,0},{3,1},{4,2},{5,3},{6,4},{7,5},{8,14},{9,15},{10,... | collective-permute-start | bytes 393224 | tf_op jit(solution)/shard_map/ppermute | solution.py:343

commit v5 on v4

--- a/solution.py
+++ b/solution.py
@@ -122,7 +122,7 @@
     )(verticals, slashes)
 
 
-def pool_kernel(blocks, own_ref, swapped_ref, two_ref, halfway_ref, onward_ref, columns_ref, pool_ref, sems):
+def pool_kernel(blocks, own_ref, swapped_ref, two_ref, halfway_ref, onward_ref, columns_ref, _, pool_ref, sems):
     odd = lax.rem(lax.axis_index("ctx"), 2)
     rows = blocks * BLK
 
@@ -157,17 +157,17 @@
         pool_ref[1, at, :] = jnp.zeros((BLK, HD), jnp.bfloat16)
 
 
-def make_pool(blocks, own, swapped, two_back, halfway, onward, columns):
+def make_pool(blocks, own, swapped, two_back, halfway, onward, columns, query):
     rows = (REACH + 2) * blocks * BLK + columns.shape[1]
     return pl.pallas_call(
         functools.partial(pool_kernel, blocks),
         out_shape=jax.ShapeDtypeStruct((2, rows, HD), jnp.bfloat16),
-        in_specs=[ANYWHERE] * 6,
+        in_specs=[ANYWHERE] * 6 + [IN_VMEM],
         out_specs=IN_VMEM,
         scratch_shapes=[pltpu.SemaphoreType.DMA((5,))],
         compiler_params=SMALL,
         cost_estimate=small_cost(2**22),
-    )(own, swapped, two_back, halfway, onward, columns)
+    )(own, swapped, two_back, halfway, onward, columns, query)
 
 
 def attend_kernel(offsets, blocks, slots_ref, pool_ref, query_ref, *refs):
@@ -325,16 +325,17 @@
     columns_of = [[y * ROW + g for y in range(lines)] for g in range(ROW)]
     share = add_up(exchange(picked.reshape(ROW, -1, HD), rows))
     share = add_up(exchange(spread(share, lines), columns_of))
-    columns = exchange(spread(share, ROW), rows).reshape(2, -1, HD)
-
+
+    share, key_value = lax.optimization_barrier((share, key_value))
     first, mixed, last = window_routes(stretches)
     two_back = lax.ppermute(key_value, "ctx", first)
     halfway = lax.ppermute(key_value, "ctx", mixed)
     swapped = lax.ppermute(two_back, "ctx", [(s, s ^ 1) for s in range(stretches)])
     onward = lax.ppermute(halfway, "ctx", last)
 
+    columns = exchange(spread(share, ROW), rows).reshape(2, -1, HD)
     slots = plan(blocks, verticals, slashes)
-    pool = make_pool(blocks, key_value, swapped, two_back, halfway, onward, columns)
+    pool = make_pool(blocks, key_value, swapped, two_back, halfway, onward, columns, query_states)
 
     def attend(offsets, after):
         return attend_call(tuple(n % planes for n in offsets), blocks, slots, pool, query_states, after)

time: 126 us -> 136 us (1.079)
  blocking collectives: 14 us -> 29.4 us
  starting transfers between devices: 59.8 us -> 54.4 us
  local copies, waits for them, and re-layouts: 2.76 us -> 0.81 us
    all_to_all x1 -> x2, blocking collectives: 14 us -> 29.4 us  [exchange(): lax.all_to_all(parts, 'ctx', split_axis=0, concat_axis=0, axis_index_grou...]
    all_to_all x2 -> x1, starting transfers between devices: 12 us -> 3.75 us  [exchange(): lax.all_to_all(parts, 'ctx', split_axis=0, concat_axis=0, axis_index_grou...]
    ppermute x1, waiting for transfers between devices: 0.01 us -> 6.87 us  [shards(): two_back = lax.ppermute(key_value, 'ctx', first)]
    all_to_all x2 -> x1, waiting for transfers between devices: 10.7 us -> 4.69 us  [exchange(): lax.all_to_all(parts, 'ctx', split_axis=0, concat_axis=0, axis_index_grou...]
    ppermute x1, starting transfers between devices: 3.24 us -> 5.46 us  [shards(): lax.ppermute(two_back, 'ctx', [(s, s ^ 1) for s in range(stretches)])]
    ppermute x1, starting transfers between devices: 5.23 us -> 7.1 us  [shards(): halfway = lax.ppermute(key_value, 'ctx', mixed)]
    ppermute x1, starting transfers between devices: 4.08 us -> 2.21 us  [shards(): two_back = lax.ppermute(key_value, 'ctx', first)]
  transfers between devices with their start and end apart: 14 -> 13, of which waited for: 3 -> 3; matrix products, arithmetic and copies ran while one was open for 1% -> 1% of each run, Pallas kernels for 17% -> 16%
where the time goes in v5:
time: 136 us; the launch traced here: 135 us
  starting transfers between devices  54.4 us (40%)
  Pallas kernels  31.6 us (23%)
  blocking collectives  29.4 us (22%)
  waiting for transfers between devices  18 us (13%)
    ppermute x8, starting transfers between devices, send(): lax.ppermute(block, 'kvh', [(s, (s + offset) % planes) for s in range(pla...  34.3 us
    all_to_all x2, blocking collectives, exchange(): lax.all_to_all(parts, 'ctx', split_axis=0, concat_axis=0, axis_index_grou...  29.4 us
    pallas_call x7, Pallas kernels, attend_call(): pl.pallas_call(functools.partial(attend_kernel, offsets, blocks), out_sha...  24.7 us
    ppermute x1, starting transfers between devices, shards(): halfway = lax.ppermute(key_value, 'ctx', mixed)  7.1 us
    ppermute x1, waiting for transfers between devices, shards(): two_back = lax.ppermute(key_value, 'ctx', first)  6.87 us
    ppermute x8, waiting for transfers between devices, send(): lax.ppermute(block, 'kvh', [(s, (s + offset) % planes) for s in range(pla...  6.44 us
    ppermute x1, starting transfers between devices, shards(): lax.ppermute(two_back, 'ctx', [(s, s ^ 1) for s in range(stretches)])  5.46 us
    all_to_all x1, waiting for transfers between devices, exchange(): lax.all_to_all(parts, 'ctx', split_axis=0, concat_axis=0, axis_index_grou...  4.69 us
  transfers between devices with their start and end apart: 13, of which 3 were waited for; matrix products, arithmetic and copies ran while one was open for 1% of the time, Pallas kernels for 16%

profile of v5, /device:TPU:1, one launch (start us, length us, event | category | flops | bytes accessed | tf_op | source)
XLA Modules:
  0.0 134.7 jit_solution(5150862127495439115)
XLA Ops:
  0.0 2.2 %shard_map.56 = (bf16[2,1024,128]{2,1,0:T(8,128)(2,1)}, bf16[2,512,128]{2,1,0:T(8,128)(2,1)}) custom-call(s32[1,4]{1,0:T(1,128)} %verticals_ref.3, bf16[1024,128]{1,0:T(8,128)(2,1)} %keys_ref.1, bf16[1024,128]{1,0:T(8,128)(2,1)} %values_ref.1), custom_call_target="tpu_custom_call" | custom-call | bytes 1048576 | tf_op jit(solution)/shard_map/pallas_call | solution.py:68
  2.2 0.0 copy-start.1
  2.3 16.8 %all_to_all.15 = bf16[8,128,128]{2,1,0:T(8,128)(2,1)S(1)} all-to-all(bf16[8,128,128]{2,1,0:T(8,128)(2,1)} %bitcast.3), channel_id=1, replica_groups={{0,8,16,24,32,40,48,56},{64,72,80,88,96,104,112,120},{128,136,144,152,1..., dimensions={0} | all-to-all | bytes 524288 | tf_op jit(solution)/shard_map/all_to_all | solution.py:306
  19.2 12.6 %all_to_all.16 = bf16[8,128,128]{2,1,0:T(8,128)(2,1)S(1)} all-to-all(bf16[8,128,128]{2,1,0:T(8,128)(2,1)S(1)} %broadcast_in_dim.4), channel_id=1, replica_groups={{0,64,128,192,256,320,384,448},{8,72,136,200,264,328,392,456},{16,80,14..., dimensions={0} | all-to-all | bytes 524288 | tf_op jit(solution)/shard_map/all_to_all | solution.py:306
  31.8 2.2 %collective-permute-start = (bf16[2,1024,128]{2,1,0:T(8,128)(2,1)}, bf16[2,1024,128]{2,1,0:T(8,128)(2,1)S(1)}, u32[]{:S(2)}, u32[]{:S(2)}) collective-permute-start(bf16[2,1024,128]{2,1,0:T(8,128)(2,1)} %get-tuple-element.13.own_ref), channel_id=1, source_target_pairs={{0,16},{8,24},{16,32},{24,40},{32,48},{40,56},{48,64},{56,72},{64,... | collective-permute-start | bytes 1572872 | tf_op jit(solution)/shard_map/ppermute | solution.py:331
  34.0 7.1 %collective-permute-start.2 = (bf16[2,1024,128]{2,1,0:T(8,128)(2,1)}, bf16[2,1024,128]{2,1,0:T(8,128)(2,1)}, u32[]{:S(2)}, u32[]{:S(2)}) collective-permute-start(bf16[2,1024,128]{2,1,0:T(8,128)(2,1)} %get-tuple-element.13.own_ref), channel_id=1, source_target_pairs={{0,8},{8,48},{16,24},{24,0},{32,40},{40,80},{48,56},{56,32},{64,72... | collective-permute-start | bytes 1572872 | tf_op jit(solution)/shard_map/ppermute | solution.py:332
  41.1 6.9 %collective-permute-done.two_ref = bf16[2,1024,128]{2,1,0:T(8,128)(2,1)S(1)} collective-permute-done((bf16[2,1024,128]{2,1,0:T(8,128)(2,1)}, bf16[2,1024,128]{2,1,0:T(8,128)(2,1)S(1)}, u32[]{:S(2)}, u32[]{:S(2)}) %collective-permute-start) | collective-permute-done | bytes 524320 | tf_op jit(solution)/shard_map/ppermute | solution.py:331
  48.0 5.5 %collective-permute-start.1 = (bf16[2,1024,128]{2,1,0:T(8,128)(2,1)S(1)}, bf16[2,1024,128]{2,1,0:T(8,128)(2,1)}, u32[]{:S(2)}, u32[]{:S(2)}) collective-permute-start(bf16[2,1024,128]{2,1,0:T(8,128)(2,1)S(1)} %collective-permute-done.two_ref), channel_id=1, source_target_pairs={{0,8},{8,0},{16,24},{24,16},{32,40},{40,32},{48,56},{56,48},{64,72... | collective-permute-start | bytes 1572872 | tf_op jit(solution)/shard_map/ppermute | solution.py:333
  53.5 0.0 collective-permute-done.2.halfway_ref
  53.5 1.5 %collective-permute-start.3 = (bf16[2,1024,128]{2,1,0:T(8,128)(2,1)}, bf16[2,1024,128]{2,1,0:T(8,128)(2,1)}, u32[]{:S(2)}, u32[]{:S(2)}) collective-permute-start(bf16[2,1024,128]{2,1,0:T(8,128)(2,1)} %collective-permute-done.2.halfway_ref), channel_id=1, source_target_pairs={{48,32},{0,48},{80,64},{32,80},{112,96},{64,112},{144,128},{96,144... | collective-permute-start | bytes 1572872 | tf_op jit(solution)/shard_map/ppermute | solution.py:334
  55.0 0.8 broadcast_in_dim.5
  55.7 3.8 %all-to-all-start.2 = ((bf16[8,128,128]{2,1,0:T(8,128)(2,1)}), bf16[8,128,128]{2,1,0:T(8,128)(2,1)S(1)}, u32[]{:S(2)}, u32[]{:S(2)}) async-start(bf16[8,128,128]{2,1,0:T(8,128)(2,1)} %broadcast_in_dim.5), calls=%async_computation.2 | async-start | bytes 524288 | tf_op jit(solution)/shard_map/all_to_all | solution.py:306
  59.5 1.9 %shard_map.55.slots_ref = s32[104]{0:T(128)S(1)} custom-call(s32[1,4]{1,0:T(1,128)S(1)} %copy-done.2, s32[1,8]{1,0:T(1,128)S(1)} %copy-done.3), custom_call_target="tpu_custom_call" | custom-call | bytes 1048576 | tf_op jit(solution)/shard_map/pallas_call | solution.py:115
  61.4 4.7 %all-to-all-done.2 = bf16[8,128,128]{2,1,0:T(8,128)(2,1)S(1)} async-done(((bf16[8,128,128]{2,1,0:T(8,128)(2,1)}), bf16[8,128,128]{2,1,0:T(8,128)(2,1)S(1)}, u32[]{:S(2)}, u32[]{:S(2)}) %all-to-all-start.2) | async-done | bytes 262176 | tf_op jit(solution)/shard_map/all_to_all | solution.py:306
  66.2 1.3 shard_map.57.pool_ref
  67.5 5.4 %shard_map.58 = (bf16[64,1024]{1,0:T(8,128)(2,1)S(1)}, bf16[192,1024]{1,0:T(8,128)(2,1)S(1)}) custom-call(s32[104]{0:T(128)S(1)} %shard_map.55.slots_ref, bf16[2,5632,128]{2,1,0:T(8,128)(2,1)S(1)} %shard_map.57.pool_ref, bf16[1024,1024]{1,0:T(8,128)(2,1)S(1)} %copy-done), custom_call_target="tpu_custom_call" | custom-call | flops 1744830464 | bytes 2097152 | tf_op jit(solution)/shard_map/pallas_call | solution.py:243
  73.0 10.4 %collective-permute-start.5 = (bf16[192,1024]{1,0:T(8,128)(2,1)S(1)}, bf16[192,1024]{1,0:T(8,128)(2,1)S(1)}, u32[]{:S(2)}, u32[]{:S(2)}) collective-permute-start(bf16[192,1024]{1,0:T(8,128)(2,1)S(1)} %get-tuple-element.16), channel_id=1, source_target_pairs={{0,6},{1,7},{2,0},{3,1},{4,2},{5,3},{6,4},{7,5},{8,14},{9,15},{10,... | collective-permute-start | bytes 1179656 | tf_op jit(solution)/shard_map/ppermute | solution.py:344
  83.4 1.9 %collective-permute-start.4 = (bf16[64,1024]{1,0:T(8,128)(2,1)S(1)}, bf16[64,1024]{1,0:T(8,128)(2,1)S(1)}, u32[]{:S(2)}, u32[]{:S(2)}) collective-permute-start(bf16[64,1024]{1,0:T(8,128)(2,1)S(1)} %get-tuple-element.15.refs_0_), channel_id=1, source_target_pairs={{0,4},{1,5},{2,6},{3,7},{4,0},{5,1},{6,2},{7,3},{8,12},{9,13},{10,... | collective-permute-start | bytes 393224 | tf_op jit(solution)/shard_map/ppermute | solution.py:344
  85.3 3.2 %shard_map.59.refs_0_ = bf16[128,1024]{1,0:T(8,128)(2,1)S(1)} custom-call(s32[104]{0:T(128)S(1)} %shard_map.55.slots_ref, bf16[2,5632,128]{2,1,0:T(8,128)(2,1)S(1)} %shard_map.57.pool_ref, bf16[1024,1024]{1,0:T(8,128)(2,1)S(1)} %copy-done, bf16[64,1024]{1,0:T(8,128)(2,1)S(1)} %get-tuple-element.15.refs_0_), custom_call_target="tpu_custom_call" | custom-call | flops 872415232 | bytes 1048576 | tf_op jit(solution)/shard_map/pallas_call | solution.py:243
  88.5 5.1 %collective-permute-start.7 = (bf16[128,1024]{1,0:T(8,128)(2,1)S(1)}, bf16[128,1024]{1,0:T(8,128)(2,1)S(1)}, u32[]{:S(2)}, u32[]{:S(2)}) collective-permute-start(bf16[128,1024]{1,0:T(8,128)(2,1)S(1)} %shard_map.59.refs_0_), channel_id=1, source_target_pairs={{0,3},{1,4},{2,5},{3,6},{4,7},{5,0},{6,1},{7,2},{8,11},{9,12},{10,... | collective-permute-start | bytes 786440 | tf_op jit(solution)/shard_map/ppermute | solution.py:344
  93.7 3.2 %shard_map.60.refs_0_ = bf16[128,1024]{1,0:T(8,128)(2,1)S(1)} custom-call(s32[104]{0:T(128)S(1)} %shard_map.55.slots_ref, bf16[2,5632,128]{2,1,0:T(8,128)(2,1)S(1)} %shard_map.57.pool_ref, bf16[1024,1024]{1,0:T(8,128)(2,1)S(1)} %copy-done, bf16[128,1024]{1,0:T(8,128)(2,1)S(1)} %shard_map.59.refs_0_), custom_call_target="tpu_custom_call" | custom-call | flops 872415232 | bytes 1048576 | tf_op jit(solution)/shard_map/pallas_call | solution.py:243
  96.9 4.2 %collective-permute-start.8 = (bf16[128,1024]{1,0:T(8,128)(2,1)S(1)}, bf16[128,1024]{1,0:T(8,128)(2,1)S(1)}, u32[]{:S(2)}, u32[]{:S(2)}) collective-permute-start(bf16[128,1024]{1,0:T(8,128)(2,1)S(1)} %shard_map.60.refs_0_), channel_id=1, source_target_pairs={{0,5},{1,6},{2,7},{3,0},{4,1},{5,2},{6,3},{7,4},{8,13},{9,14},{10,... | collective-permute-start | bytes 786440 | tf_op jit(solution)/shard_map/ppermute | solution.py:344
  101.1 3.2 %shard_map.61.refs_0_ = bf16[128,1024]{1,0:T(8,128)(2,1)S(1)} custom-call(s32[104]{0:T(128)S(1)} %shard_map.55.slots_ref, bf16[2,5632,128]{2,1,0:T(8,128)(2,1)S(1)} %shard_map.57.pool_ref, bf16[1024,1024]{1,0:T(8,128)(2,1)S(1)} %copy-done, bf16[128,1024]{1,0:T(8,128)(2,1)S(1)} %shard_map.60.refs_0_), custom_call_target="tpu_custom_call" | custom-call | flops 872415232 | bytes 1048576 | tf_op jit(solution)/shard_map/pallas_call | solution.py:243
  104.3 3.4 %collective-permute-start.9 = (bf16[128,1024]{1,0:T(8,128)(2,1)S(1)}, bf16[128,1024]{1,0:T(8,128)(2,1)S(1)}, u32[]{:S(2)}, u32[]{:S(2)}) collective-permute-start(bf16[128,1024]{1,0:T(8,128)(2,1)S(1)} %shard_map.61.refs_0_), channel_id=1, source_target_pairs={{0,2},{1,3},{2,4},{3,5},{4,6},{5,7},{6,0},{7,1},{8,10},{9,11},{10,... | collective-permute-start | bytes 786440 | tf_op jit(solution)/shard_map/ppermute | solution.py:344
  107.7 3.2 %shard_map.62.refs_0_ = bf16[128,1024]{1,0:T(8,128)(2,1)S(1)} custom-call(s32[104]{0:T(128)S(1)} %shard_map.55.slots_ref, bf16[2,5632,128]{2,1,0:T(8,128)(2,1)S(1)} %shard_map.57.pool_ref, bf16[1024,1024]{1,0:T(8,128)(2,1)S(1)} %copy-done, bf16[128,1024]{1,0:T(8,128)(2,1)S(1)} %shard_map.61.refs_0_, bf16[192,1024]{1,0:T(8,128)(2,1)S(1)} %collective-permute-done.5.refs_1_.refs_2_), custom_call_target="tpu_custom_call" | custom-call | flops 872415232 | bytes 1048576 | tf_op jit(solution)/shard_map/pallas_call | solution.py:243
  110.9 3.2 %shard_map.63.refs_0_ = bf16[128,1024]{1,0:T(8,128)(2,1)S(1)} custom-call(s32[104]{0:T(128)S(1)} %shard_map.55.slots_ref, bf16[2,5632,128]{2,1,0:T(8,128)(2,1)S(1)} %shard_map.57.pool_ref, bf16[1024,1024]{1,0:T(8,128)(2,1)S(1)} %copy-done, bf16[128,1024]{1,0:T(8,128)(2,1)S(1)} %shard_map.62.refs_0_, bf16[64,1024]{1,0:T(8,128)(2,1)S(1)} %collective-permute-done.4.refs_1_.refs_0_), custom_call_target="tpu_custom_call" | custom-call | flops 872415232 | bytes 1048576 | tf_op jit(solution)/shard_map/pallas_call | solution.py:243
  114.2 3.2 %collective-permute-start.11 = (bf16[128,1024]{1,0:T(8,128)(2,1)S(1)}, bf16[128,1024]{1,0:T(8,128)(2,1)S(1)}, u32[]{:S(2)}, u32[]{:S(2)}) collective-permute-start(bf16[128,1024]{1,0:T(8,128)(2,1)S(1)} %shard_map.63.refs_0_), channel_id=1, source_target_pairs={{0,7},{1,0},{2,1},{3,2},{4,3},{5,4},{6,5},{7,6},{8,15},{9,8},{10,9... | collective-permute-start | bytes 786440 | tf_op jit(solution)/shard_map/ppermute | solution.py:344
  117.3 2.1 %collective-permute-start.10 = (bf16[128,1024]{1,0:T(8,128)(2,1)S(1)}, bf16[128,1024]{1,0:T(8,128)(2,1)S(1)}, u32[]{:S(2)}, u32[]{:S(2)}) collective-permute-start(bf16[128,1024]{1,0:T(8,128)(2,1)S(1)} %shard_map.62.refs_0_), channel_id=1, source_target_pairs={{0,1},{1,2},{2,3},{3,4},{4,5},{5,6},{6,7},{7,0},{8,9},{9,10},{10,1... | collective-permute-start | bytes 786440 | tf_op jit(solution)/shard_map/ppermute | solution.py:344
  119.5 4.0 %collective-permute-start.6 = (bf16[64,1024]{1,0:T(8,128)(2,1)S(1)}, bf16[64,1024]{1,0:T(8,128)(2,1)S(1)}, u32[]{:S(2)}, u32[]{:S(2)}) collective-permute-start(bf16[64,1024]{1,0:T(8,128)(2,1)S(1)} %slice.4), channel_id=1, source_target_pairs={{0,6},{1,7},{2,0},{3,1},{4,2},{5,3},{6,4},{7,5},{8,14},{9,15},{10,... | collective-permute-start | bytes 393224 | tf_op jit(solution)/shard_map/ppermute | solution.py:344
  123.5 3.2 %shard_map.64.refs_8_ = bf16[128,1024]{1,0:T(8,128)(2,1)S(1)} custom-call(s32[104]{0:T(128)S(1)} %shard_map.55.slots_ref, bf16[2,5632,128]{2,1,0:T(8,128)(2,1)S(1)} %shard_map.57.pool_ref, bf16[1024,1024]{1,0:T(8,128)(2,1)S(1)} %copy-done, bf16[128,1024]{1,0:T(8,128)(2,1)S(1)} %shard_map.63.refs_0_, bf16[128,1024]{1,0:T(8,128)(2,1)S(1)} %collective-permute-done.7.refs_1_.refs_3_), custom_call_target="tpu_custom_call" | custom-call | flops 872415232 | bytes 1048576 | tf_op jit(solution)/shard_map/pallas_call | solution.py:243
  126.8 6.4 %collective-permute-done.6.refs_1_ = bf16[64,1024]{1,0:T(8,128)(2,1)S(1)} collective-permute-done((bf16[64,1024]{1,0:T(8,128)(2,1)S(1)}, bf16[64,1024]{1,0:T(8,128)(2,1)S(1)}, u32[]{:S(2)}, u32[]{:S(2)}) %collective-permute-start.6) | collective-permute-done | bytes 131104 | tf_op jit(solution)/shard_map/ppermute | solution.py:344
  133.2 1.4 %shard_map.65 = bf16[128,8192]{1,0:T(8,128)(2,1)} custom-call(bf16[64,1024]{1,0:T(8,128)(2,1)S(1)} %collective-permute-done.4.refs_1_.refs_0_, bf16[64,1024]{1,0:T(8,128)(2,1)S(1)} %collective-permute-done.6.refs_1_, bf16[192,1024]{1,0:T(8,128)(2,1)S(1)} %collective-permute-done.5.refs_1_.refs_2_, ...), custom_call_target="tpu_custom_call" | custom-call | bytes 8388608 | tf_op jit(solution)/shard_map/pallas_call | solution.py:278
  (20 shorter events, 0.2 us)
Async XLA Ops:
  0.0 59.5 %copy-start.2 = (s32[1,4]{1,0:T(1,128)S(1)}, s32[1,4]{1,0:T(1,128)}, u32[]{:S(2)}) copy-start(s32[1,4]{1,0:T(1,128)} %verticals_ref.3) | copy-start | bytes 52
  0.0 59.5 %copy-start.3 = (s32[1,8]{1,0:T(1,128)S(1)}, s32[1,8]{1,0:T(1,128)}, u32[]{:S(2)}) copy-start(s32[1,8]{1,0:T(1,128)} %slashes_ref.1) | copy-start | bytes 100
  0.0 66.1 %copy-start = (bf16[1024,1024]{1,0:T(8,128)(2,1)S(1)}, bf16[1024,1024]{1,0:T(8,128)(2,1)}, u32[]{:S(2)}) copy-start(bf16[1024,1024]{1,0:T(8,128)(2,1)} %query_ref.13) | copy-start | bytes 6291460
  2.2 63.9 %copy-start.1 = (bf16[2,1024,128]{2,1,0:T(8,128)(2,1)S(1)}, bf16[2,1024,128]{2,1,0:T(8,128)(2,1)}, u32[]{:S(2)}) copy-start(bf16[2,1024,128]{2,1,0:T(8,128)(2,1)} %get-tuple-element.13.own_ref) | copy-start | bytes 1572868
  31.8 16.2 %collective-permute-start = (bf16[2,1024,128]{2,1,0:T(8,128)(2,1)}, bf16[2,1024,128]{2,1,0:T(8,128)(2,1)S(1)}, u32[]{:S(2)}, u32[]{:S(2)}) collective-permute-start(bf16[2,1024,128]{2,1,0:T(8,128)(2,1)} %get-tuple-element.13.own_ref), channel_id=1, source_target_pairs={{0,16},{8,24},{16,32},{24,40},{32,48},{40,56},{48,64},{56,72},{64,... | collective-permute-start | bytes 1572872 | tf_op jit(solution)/shard_map/ppermute | solution.py:331
  34.0 19.5 %collective-permute-start.2 = (bf16[2,1024,128]{2,1,0:T(8,128)(2,1)}, bf16[2,1024,128]{2,1,0:T(8,128)(2,1)}, u32[]{:S(2)}, u32[]{:S(2)}) collective-permute-start(bf16[2,1024,128]{2,1,0:T(8,128)(2,1)} %get-tuple-element.13.own_ref), channel_id=1, source_target_pairs={{0,8},{8,48},{16,24},{24,0},{32,40},{40,80},{48,56},{56,32},{64,72... | collective-permute-start | bytes 1572872 | tf_op jit(solution)/shard_map/ppermute | solution.py:332
  48.0 18.1 %collective-permute-start.1 = (bf16[2,1024,128]{2,1,0:T(8,128)(2,1)S(1)}, bf16[2,1024,128]{2,1,0:T(8,128)(2,1)}, u32[]{:S(2)}, u32[]{:S(2)}) collective-permute-start(bf16[2,1024,128]{2,1,0:T(8,128)(2,1)S(1)} %collective-permute-done.two_ref), channel_id=1, source_target_pairs={{0,8},{8,0},{16,24},{24,16},{32,40},{40,32},{48,56},{56,48},{64,72... | collective-permute-start | bytes 1572872 | tf_op jit(solution)/shard_map/ppermute | solution.py:333
  53.5 12.7 %collective-permute-start.3 = (bf16[2,1024,128]{2,1,0:T(8,128)(2,1)}, bf16[2,1024,128]{2,1,0:T(8,128)(2,1)}, u32[]{:S(2)}, u32[]{:S(2)}) collective-permute-start(bf16[2,1024,128]{2,1,0:T(8,128)(2,1)} %collective-permute-done.2.halfway_ref), channel_id=1, source_target_pairs={{48,32},{0,48},{80,64},{32,80},{112,96},{64,112},{144,128},{96,144... | collective-permute-start | bytes 1572872 | tf_op jit(solution)/shard_map/ppermute | solution.py:334
  55.7 10.4 %all-to-all-start.2 = ((bf16[8,128,128]{2,1,0:T(8,128)(2,1)}), bf16[8,128,128]{2,1,0:T(8,128)(2,1)S(1)}, u32[]{:S(2)}, u32[]{:S(2)}) async-start(bf16[8,128,128]{2,1,0:T(8,128)(2,1)} %broadcast_in_dim.5), calls=%async_computation.2 | async-start | bytes 524288 | tf_op jit(solution)/shard_map/all_to_all | solution.py:306
  73.0 34.7 %collective-permute-start.5 = (bf16[192,1024]{1,0:T(8,128)(2,1)S(1)}, bf16[192,1024]{1,0:T(8,128)(2,1)S(1)}, u32[]{:S(2)}, u32[]{:S(2)}) collective-permute-start(bf16[192,1024]{1,0:T(8,128)(2,1)S(1)} %get-tuple-element.16), channel_id=1, source_target_pairs={{0,6},{1,7},{2,0},{3,1},{4,2},{5,3},{6,4},{7,5},{8,14},{9,15},{10,... | collective-permute-start | bytes 1179656 | tf_op jit(solution)/shard_map/ppermute | solution.py:344
  83.4 27.6 %collective-permute-start.4 = (bf16[64,1024]{1,0:T(8,128)(2,1)S(1)}, bf16[64,1024]{1,0:T(8,128)(2,1)S(1)}, u32[]{:S(2)}, u32[]{:S(2)}) collective-permute-start(bf16[64,1024]{1,0:T(8,128)(2,1)S(1)} %get-tuple-element.15.refs_0_), channel_id=1, source_target_pairs={{0,4},{1,5},{2,6},{3,7},{4,0},{5,1},{6,2},{7,3},{8,12},{9,13},{10,... | collective-permute-start | bytes 393224 | tf_op jit(solution)/shard_map/ppermute | solution.py:344
  88.5 31.0 %collective-permute-start.7 = (bf16[128,1024]{1,0:T(8,128)(2,1)S(1)}, bf16[128,1024]{1,0:T(8,128)(2,1)S(1)}, u32[]{:S(2)}, u32[]{:S(2)}) collective-permute-start(bf16[128,1024]{1,0:T(8,128)(2,1)S(1)} %shard_map.59.refs_0_), channel_id=1, source_target_pairs={{0,3},{1,4},{2,5},{3,6},{4,7},{5,0},{6,1},{7,2},{8,11},{9,12},{10,... | collective-permute-start | bytes 786440 | tf_op jit(solution)/shard_map/ppermute | solution.py:344
  96.9 29.9 %collective-permute-start.8 = (bf16[128,1024]{1,0:T(8,128)(2,1)S(1)}, bf16[128,1024]{1,0:T(8,128)(2,1)S(1)}, u32[]{:S(2)}, u32[]{:S(2)}) collective-permute-start(bf16[128,1024]{1,0:T(8,128)(2,1)S(1)} %shard_map.60.refs_0_), channel_id=1, source_target_pairs={{0,5},{1,6},{2,7},{3,0},{4,1},{5,2},{6,3},{7,4},{8,13},{9,14},{10,... | collective-permute-start | bytes 786440 | tf_op jit(solution)/shard_map/ppermute | solution.py:344
  104.3 22.4 %collective-permute-start.9 = (bf16[128,1024]{1,0:T(8,128)(2,1)S(1)}, bf16[128,1024]{1,0:T(8,128)(2,1)S(1)}, u32[]{:S(2)}, u32[]{:S(2)}) collective-permute-start(bf16[128,1024]{1,0:T(8,128)(2,1)S(1)} %shard_map.61.refs_0_), channel_id=1, source_target_pairs={{0,2},{1,3},{2,4},{3,5},{4,6},{5,7},{6,0},{7,1},{8,10},{9,11},{10,... | collective-permute-start | bytes 786440 | tf_op jit(solution)/shard_map/ppermute | solution.py:344
  114.2 19.0 %collective-permute-start.11 = (bf16[128,1024]{1,0:T(8,128)(2,1)S(1)}, bf16[128,1024]{1,0:T(8,128)(2,1)S(1)}, u32[]{:S(2)}, u32[]{:S(2)}) collective-permute-start(bf16[128,1024]{1,0:T(8,128)(2,1)S(1)} %shard_map.63.refs_0_), channel_id=1, source_target_pairs={{0,7},{1,0},{2,1},{3,2},{4,3},{5,4},{6,5},{7,6},{8,15},{9,8},{10,9... | collective-permute-start | bytes 786440 | tf_op jit(solution)/shard_map/ppermute | solution.py:344
  117.3 15.9 %collective-permute-start.10 = (bf16[128,1024]{1,0:T(8,128)(2,1)S(1)}, bf16[128,1024]{1,0:T(8,128)(2,1)S(1)}, u32[]{:S(2)}, u32[]{:S(2)}) collective-permute-start(bf16[128,1024]{1,0:T(8,128)(2,1)S(1)} %shard_map.62.refs_0_), channel_id=1, source_target_pairs={{0,1},{1,2},{2,3},{3,4},{4,5},{5,6},{6,7},{7,0},{8,9},{9,10},{10,1... | collective-permute-start | bytes 786440 | tf_op jit(solution)/shard_map/ppermute | solution.py:344
  119.5 13.7 %collective-permute-start.6 = (bf16[64,1024]{1,0:T(8,128)(2,1)S(1)}, bf16[64,1024]{1,0:T(8,128)(2,1)S(1)}, u32[]{:S(2)}, u32[]{:S(2)}) collective-permute-start(bf16[64,1024]{1,0:T(8,128)(2,1)S(1)} %slice.4), channel_id=1, source_target_pairs={{0,6},{1,7},{2,0},{3,1},{4,2},{5,3},{6,4},{7,5},{8,14},{9,15},{10,... | collective-permute-start | bytes 393224 | tf_op jit(solution)/shard_map/ppermute | solution.py:344

commit v6 on v4

--- a/solution.py
+++ b/solution.py
@@ -325,14 +325,15 @@
     columns_of = [[y * ROW + g for y in range(lines)] for g in range(ROW)]
     share = add_up(exchange(picked.reshape(ROW, -1, HD), rows))
     share = add_up(exchange(spread(share, lines), columns_of))
-    columns = exchange(spread(share, ROW), rows).reshape(2, -1, HD)
 
     first, mixed, last = window_routes(stretches)
     two_back = lax.ppermute(key_value, "ctx", first)
     halfway = lax.ppermute(key_value, "ctx", mixed)
+    share, two_back = lax.optimization_barrier((share, two_back))
     swapped = lax.ppermute(two_back, "ctx", [(s, s ^ 1) for s in range(stretches)])
     onward = lax.ppermute(halfway, "ctx", last)
 
+    columns = exchange(spread(share, ROW), rows).reshape(2, -1, HD)
     slots = plan(blocks, verticals, slashes)
     pool = make_pool(blocks, key_value, swapped, two_back, halfway, onward, columns)
 
@@ -349,7 +350,7 @@
     lower = send(bundle[BLK:], BY_STEPS)
     pieces = [upper, lower, bundle]
     places = [(FAR_SIDE, 0, HALF), (FAR_SIDE, HALF, HALF), (BY_STEPS % planes, 0, BLK)]
-    arrived = {3: [bundle], 4: [upper]}
+    arrived = {3: [bundle], 4: [upper, lower]}
     for number, offset in enumerate(OFFSETS):
         (result,) = attend((offset,), after + arrived.get(number, []))
         after = [result]

time: 126 us -> 125 us (level)
  blocking collectives: 14 us -> 0 us
  waiting for transfers between devices: 17.1 us -> 28.9 us
  starting transfers between devices: 59.8 us -> 62 us
    all_to_all x1 -> x0, blocking collectives: 14 us -> none  [exchange(): lax.all_to_all(parts, 'ctx', split_axis=0, concat_axis=0, axis_index_grou...]
    all_to_all x2 -> x3, starting transfers between devices: 12 us -> 17.6 us  [exchange(): lax.all_to_all(parts, 'ctx', split_axis=0, concat_axis=0, axis_index_grou...]
    ppermute x1, waiting for transfers between devices: 0.01 us -> 5.01 us  [shards(): two_back = lax.ppermute(key_value, 'ctx', first)]
    all_to_all x2 -> x3, waiting for transfers between devices: 10.7 us -> 14.1 us  [exchange(): lax.all_to_all(parts, 'ctx', split_axis=0, concat_axis=0, axis_index_grou...]
    ppermute x8, waiting for transfers between devices: 6.4 us -> 9.44 us  [send(): lax.ppermute(block, 'kvh', [(s, (s + offset) % planes) for s in range(pla...]
    ppermute x1, starting transfers between devices: 4.08 us -> 1.92 us  [shards(): two_back = lax.ppermute(key_value, 'ctx', first)]
    ppermute x1, starting transfers between devices: 3.24 us -> 1.91 us  [shards(): lax.ppermute(two_back, 'ctx', [(s, s ^ 1) for s in range(stretches)])]
  transfers between devices with their start and end apart: 14 -> 15, of which waited for: 3 -> 6; matrix products, arithmetic and copies ran while one was open for 1% -> 1% of each run, Pallas kernels for 17% -> 17%
where the time goes in v6:
time: 125 us; the launch traced here: 124 us
  starting transfers between devices  62 us (50%)
  Pallas kernels  30.1 us (24%)
  waiting for transfers between devices  28.9 us (23%)
  local copies, waits for them, and re-layouts  2.78 us (2%)
    ppermute x8, starting transfers between devices, send(): lax.ppermute(block, 'kvh', [(s, (s + offset) % planes) for s in range(pla...  35.1 us
    pallas_call x7, Pallas kernels, attend_call(): pl.pallas_call(functools.partial(attend_kernel, offsets, blocks), out_sha...  24.4 us
    all_to_all x3, starting transfers between devices, exchange(): lax.all_to_all(parts, 'ctx', split_axis=0, concat_axis=0, axis_index_grou...  17.6 us
    all_to_all x3, waiting for transfers between devices, exchange(): lax.all_to_all(parts, 'ctx', split_axis=0, concat_axis=0, axis_index_grou...  14.1 us
    ppermute x8, waiting for transfers between devices, send(): lax.ppermute(block, 'kvh', [(s, (s + offset) % planes) for s in range(pla...  9.44 us
    ppermute x1, waiting for transfers between devices, shards(): two_back = lax.ppermute(key_value, 'ctx', first)  5.01 us
    ppermute x1, starting transfers between devices, shards(): halfway = lax.ppermute(key_value, 'ctx', mixed)  4.77 us
  transfers between devices with their start and end apart: 15, of which 6 were waited for; matrix products, arithmetic and copies ran while one was open for 1% of the time, Pallas kernels for 17%

profile of v6, /device:TPU:1, one launch (start us, length us, event | category | flops | bytes accessed | tf_op | source)
XLA Modules:
  0.0 124.2 jit_solution(14314770708844730200)
XLA Ops:
  0.0 2.1 %shard_map.56 = (bf16[2,1024,128]{2,1,0:T(8,128)(2,1)}, bf16[2,512,128]{2,1,0:T(8,128)(2,1)}) custom-call(s32[1,4]{1,0:T(1,128)} %verticals_ref.3, bf16[1024,128]{1,0:T(8,128)(2,1)} %keys_ref.1, bf16[1024,128]{1,0:T(8,128)(2,1)} %values_ref.1), custom_call_target="tpu_custom_call" | custom-call | bytes 1048576 | tf_op jit(solution)/shard_map/pallas_call | solution.py:68
  2.1 10.3 %all-to-all-start = ((bf16[8,128,128]{2,1,0:T(8,128)(2,1)}), bf16[8,128,128]{2,1,0:T(8,128)(2,1)S(1)}, u32[]{:S(2)}, u32[]{:S(2)}) async-start(bf16[8,128,128]{2,1,0:T(8,128)(2,1)} %bitcast.3), calls=%async_computation | async-start | bytes 524288 | tf_op jit(solution)/shard_map/all_to_all | solution.py:306
  12.5 4.8 %collective-permute-start.2 = (bf16[2,1024,128]{2,1,0:T(8,128)(2,1)}, bf16[2,1024,128]{2,1,0:T(8,128)(2,1)S(1)}, u32[]{:S(2)}, u32[]{:S(2)}) collective-permute-start(bf16[2,1024,128]{2,1,0:T(8,128)(2,1)} %get-tuple-element.11.own_ref), channel_id=1, source_target_pairs={{0,8},{8,48},{16,24},{24,0},{32,40},{40,80},{48,56},{56,32},{64,72... | collective-permute-start | bytes 1572872 | tf_op jit(solution)/shard_map/ppermute | solution.py:331
  17.2 1.9 %collective-permute-start = (bf16[2,1024,128]{2,1,0:T(8,128)(2,1)}, bf16[2,1024,128]{2,1,0:T(8,128)(2,1)S(1)}, u32[]{:S(2)}, u32[]{:S(2)}) collective-permute-start(bf16[2,1024,128]{2,1,0:T(8,128)(2,1)} %get-tuple-element.11.own_ref), channel_id=1, source_target_pairs={{0,16},{8,24},{16,32},{24,40},{32,48},{40,56},{48,64},{56,72},{64,... | collective-permute-start | bytes 1572872 | tf_op jit(solution)/shard_map/ppermute | solution.py:330
  19.2 0.7 broadcast_in_dim.4
  20.0 3.4 %all-to-all-start.1 = ((bf16[8,128,128]{2,1,0:T(8,128)(2,1)}), bf16[8,128,128]{2,1,0:T(8,128)(2,1)S(1)}, u32[]{:S(2)}, u32[]{:S(2)}) async-start(bf16[8,128,128]{2,1,0:T(8,128)(2,1)} %broadcast_in_dim.4), calls=%async_computation.1 | async-start | bytes 524288 | tf_op jit(solution)/shard_map/all_to_all | solution.py:306
  23.7 0.7 collective-permute-start.3
  24.3 9.6 %all-to-all-done.1 = bf16[8,128,128]{2,1,0:T(8,128)(2,1)S(1)} async-done(((bf16[8,128,128]{2,1,0:T(8,128)(2,1)}), bf16[8,128,128]{2,1,0:T(8,128)(2,1)S(1)}, u32[]{:S(2)}, u32[]{:S(2)}) %all-to-all-start.1) | async-done | bytes 262176 | tf_op jit(solution)/shard_map/all_to_all | solution.py:306
  34.0 5.0 %collective-permute-done.two_ref = bf16[2,1024,128]{2,1,0:T(8,128)(2,1)S(1)} collective-permute-done((bf16[2,1024,128]{2,1,0:T(8,128)(2,1)}, bf16[2,1024,128]{2,1,0:T(8,128)(2,1)S(1)}, u32[]{:S(2)}, u32[]{:S(2)}) %collective-permute-start) | collective-permute-done | bytes 524320 | tf_op jit(solution)/shard_map/ppermute | solution.py:330
  39.0 1.9 %collective-permute-start.1 = (bf16[2,1024,128]{2,1,0:T(8,128)(2,1)S(1)}, bf16[2,1024,128]{2,1,0:T(8,128)(2,1)S(1)}, u32[]{:S(2)}, u32[]{:S(2)}) collective-permute-start(bf16[2,1024,128]{2,1,0:T(8,128)(2,1)S(1)} %collective-permute-done.two_ref), channel_id=1, source_target_pairs={{0,8},{8,0},{16,24},{24,16},{32,40},{40,32},{48,56},{56,48},{64,72... | collective-permute-start | bytes 1572872 | tf_op jit(solution)/shard_map/ppermute | solution.py:333
  40.9 0.7 broadcast_in_dim.5
  41.6 3.8 %all-to-all-start.2 = ((bf16[8,128,128]{2,1,0:T(8,128)(2,1)}), bf16[8,128,128]{2,1,0:T(8,128)(2,1)S(1)}, u32[]{:S(2)}, u32[]{:S(2)}) async-start(bf16[8,128,128]{2,1,0:T(8,128)(2,1)} %broadcast_in_dim.5), calls=%async_computation.2 | async-start | bytes 524288 | tf_op jit(solution)/shard_map/all_to_all | solution.py:306
  45.4 1.9 %shard_map.55.slots_ref = s32[104]{0:T(128)S(1)} custom-call(s32[1,4]{1,0:T(1,128)S(1)} %copy-done.2, s32[1,8]{1,0:T(1,128)S(1)} %copy-done.3), custom_call_target="tpu_custom_call" | custom-call | bytes 1048576 | tf_op jit(solution)/shard_map/pallas_call | solution.py:115
  47.4 4.6 %all-to-all-done.2 = bf16[8,128,128]{2,1,0:T(8,128)(2,1)S(1)} async-done(((bf16[8,128,128]{2,1,0:T(8,128)(2,1)}), bf16[8,128,128]{2,1,0:T(8,128)(2,1)S(1)}, u32[]{:S(2)}, u32[]{:S(2)}) %all-to-all-start.2) | async-done | bytes 262176 | tf_op jit(solution)/shard_map/all_to_all | solution.py:306
  52.3 1.3 %copy-done = bf16[1024,1024]{1,0:T(8,128)(2,1)S(1)} copy-done((bf16[1024,1024]{1,0:T(8,128)(2,1)S(1)}, bf16[1024,1024]{1,0:T(8,128)(2,1)}, u32[]{:S(2)}) %copy-start) | copy-done | bytes 2097176
  53.6 5.4 %shard_map.58 = (bf16[64,1024]{1,0:T(8,128)(2,1)S(1)}, bf16[192,1024]{1,0:T(8,128)(2,1)S(1)}) custom-call(s32[104]{0:T(128)S(1)} %shard_map.55.slots_ref, bf16[2,5632,128]{2,1,0:T(8,128)(2,1)S(1)} %shard_map.57.pool_ref, bf16[1024,1024]{1,0:T(8,128)(2,1)S(1)} %copy-done), custom_call_target="tpu_custom_call" | custom-call | flops 1744830464 | bytes 2097152 | tf_op jit(solution)/shard_map/pallas_call | solution.py:243
  58.9 7.7 %collective-permute-start.5 = (bf16[192,1024]{1,0:T(8,128)(2,1)S(1)}, bf16[192,1024]{1,0:T(8,128)(2,1)S(1)}, u32[]{:S(2)}, u32[]{:S(2)}) collective-permute-start(bf16[192,1024]{1,0:T(8,128)(2,1)S(1)} %get-tuple-element.16), channel_id=1, source_target_pairs={{0,6},{1,7},{2,0},{3,1},{4,2},{5,3},{6,4},{7,5},{8,14},{9,15},{10,... | collective-permute-start | bytes 1179656 | tf_op jit(solution)/shard_map/ppermute | solution.py:344
  66.7 1.9 %collective-permute-start.4 = (bf16[64,1024]{1,0:T(8,128)(2,1)S(1)}, bf16[64,1024]{1,0:T(8,128)(2,1)S(1)}, u32[]{:S(2)}, u32[]{:S(2)}) collective-permute-start(bf16[64,1024]{1,0:T(8,128)(2,1)S(1)} %get-tuple-element.15.refs_0_), channel_id=1, source_target_pairs={{0,4},{1,5},{2,6},{3,7},{4,0},{5,1},{6,2},{7,3},{8,12},{9,13},{10,... | collective-permute-start | bytes 393224 | tf_op jit(solution)/shard_map/ppermute | solution.py:344
  68.6 3.2 %shard_map.59.refs_0_ = bf16[128,1024]{1,0:T(8,128)(2,1)S(1)} custom-call(s32[104]{0:T(128)S(1)} %shard_map.55.slots_ref, bf16[2,5632,128]{2,1,0:T(8,128)(2,1)S(1)} %shard_map.57.pool_ref, bf16[1024,1024]{1,0:T(8,128)(2,1)S(1)} %copy-done, bf16[64,1024]{1,0:T(8,128)(2,1)S(1)} %get-tuple-element.15.refs_0_), custom_call_target="tpu_custom_call" | custom-call | flops 872415232 | bytes 1048576 | tf_op jit(solution)/shard_map/pallas_call | solution.py:243
  71.8 5.1 %collective-permute-start.7 = (bf16[128,1024]{1,0:T(8,128)(2,1)S(1)}, bf16[128,1024]{1,0:T(8,128)(2,1)S(1)}, u32[]{:S(2)}, u32[]{:S(2)}) collective-permute-start(bf16[128,1024]{1,0:T(8,128)(2,1)S(1)} %shard_map.59.refs_0_), channel_id=1, source_target_pairs={{0,3},{1,4},{2,5},{3,6},{4,7},{5,0},{6,1},{7,2},{8,11},{9,12},{10,... | collective-permute-start | bytes 786440 | tf_op jit(solution)/shard_map/ppermute | solution.py:344
  77.0 3.2 %shard_map.60.refs_0_ = bf16[128,1024]{1,0:T(8,128)(2,1)S(1)} custom-call(s32[104]{0:T(128)S(1)} %shard_map.55.slots_ref, bf16[2,5632,128]{2,1,0:T(8,128)(2,1)S(1)} %shard_map.57.pool_ref, bf16[1024,1024]{1,0:T(8,128)(2,1)S(1)} %copy-done, bf16[128,1024]{1,0:T(8,128)(2,1)S(1)} %shard_map.59.refs_0_), custom_call_target="tpu_custom_call" | custom-call | flops 872415232 | bytes 1048576 | tf_op jit(solution)/shard_map/pallas_call | solution.py:243
  80.1 4.0 %collective-permute-start.8 = (bf16[128,1024]{1,0:T(8,128)(2,1)S(1)}, bf16[128,1024]{1,0:T(8,128)(2,1)S(1)}, u32[]{:S(2)}, u32[]{:S(2)}) collective-permute-start(bf16[128,1024]{1,0:T(8,128)(2,1)S(1)} %shard_map.60.refs_0_), channel_id=1, source_target_pairs={{0,5},{1,6},{2,7},{3,0},{4,1},{5,2},{6,3},{7,4},{8,13},{9,14},{10,... | collective-permute-start | bytes 786440 | tf_op jit(solution)/shard_map/ppermute | solution.py:344
  84.2 5.5 %collective-permute-start.6 = (bf16[64,1024]{1,0:T(8,128)(2,1)S(1)}, bf16[64,1024]{1,0:T(8,128)(2,1)S(1)}, u32[]{:S(2)}, u32[]{:S(2)}) collective-permute-start(bf16[64,1024]{1,0:T(8,128)(2,1)S(1)} %slice.4), channel_id=1, source_target_pairs={{0,6},{1,7},{2,0},{3,1},{4,2},{5,3},{6,4},{7,5},{8,14},{9,15},{10,... | collective-permute-start | bytes 393224 | tf_op jit(solution)/shard_map/ppermute | solution.py:344
  89.7 3.2 %shard_map.61.refs_0_ = bf16[128,1024]{1,0:T(8,128)(2,1)S(1)} custom-call(s32[104]{0:T(128)S(1)} %shard_map.55.slots_ref, bf16[2,5632,128]{2,1,0:T(8,128)(2,1)S(1)} %shard_map.57.pool_ref, bf16[1024,1024]{1,0:T(8,128)(2,1)S(1)} %copy-done, bf16[128,1024]{1,0:T(8,128)(2,1)S(1)} %shard_map.60.refs_0_), custom_call_target="tpu_custom_call" | custom-call | flops 872415232 | bytes 1048576 | tf_op jit(solution)/shard_map/pallas_call | solution.py:243
  92.9 1.9 %collective-permute-start.9 = (bf16[128,1024]{1,0:T(8,128)(2,1)S(1)}, bf16[128,1024]{1,0:T(8,128)(2,1)S(1)}, u32[]{:S(2)}, u32[]{:S(2)}) collective-permute-start(bf16[128,1024]{1,0:T(8,128)(2,1)S(1)} %shard_map.61.refs_0_), channel_id=1, source_target_pairs={{0,2},{1,3},{2,4},{3,5},{4,6},{5,7},{6,0},{7,1},{8,10},{9,11},{10,... | collective-permute-start | bytes 786440 | tf_op jit(solution)/shard_map/ppermute | solution.py:344
  94.8 3.2 %shard_map.62.refs_0_ = bf16[128,1024]{1,0:T(8,128)(2,1)S(1)} custom-call(s32[104]{0:T(128)S(1)} %shard_map.55.slots_ref, bf16[2,5632,128]{2,1,0:T(8,128)(2,1)S(1)} %shard_map.57.pool_ref, bf16[1024,1024]{1,0:T(8,128)(2,1)S(1)} %copy-done, bf16[128,1024]{1,0:T(8,128)(2,1)S(1)} %shard_map.61.refs_0_, bf16[192,1024]{1,0:T(8,128)(2,1)S(1)} %collective-permute-done.5.refs_1_.refs_2_), custom_call_target="tpu_custom_call" | custom-call | flops 872415232 | bytes 1048576 | tf_op jit(solution)/shard_map/pallas_call | solution.py:243
  98.0 3.9 %collective-permute-start.10 = (bf16[128,1024]{1,0:T(8,128)(2,1)S(1)}, bf16[128,1024]{1,0:T(8,128)(2,1)S(1)}, u32[]{:S(2)}, u32[]{:S(2)}) collective-permute-start(bf16[128,1024]{1,0:T(8,128)(2,1)S(1)} %shard_map.62.refs_0_), channel_id=1, source_target_pairs={{0,1},{1,2},{2,3},{3,4},{4,5},{5,6},{6,7},{7,0},{8,9},{9,10},{10,1... | collective-permute-start | bytes 786440 | tf_op jit(solution)/shard_map/ppermute | solution.py:344
  101.9 8.7 %collective-permute-done.6.refs_2_.refs_1_ = bf16[64,1024]{1,0:T(8,128)(2,1)S(1)} collective-permute-done((bf16[64,1024]{1,0:T(8,128)(2,1)S(1)}, bf16[64,1024]{1,0:T(8,128)(2,1)S(1)}, u32[]{:S(2)}, u32[]{:S(2)}) %collective-permute-start.6) | collective-permute-done | bytes 131104 | tf_op jit(solution)/shard_map/ppermute | solution.py:344
  110.6 3.2 %shard_map.63.refs_0_ = bf16[128,1024]{1,0:T(8,128)(2,1)S(1)} custom-call(s32[104]{0:T(128)S(1)} %shard_map.55.slots_ref, bf16[2,5632,128]{2,1,0:T(8,128)(2,1)S(1)} %shard_map.57.pool_ref, bf16[1024,1024]{1,0:T(8,128)(2,1)S(1)} %copy-done, bf16[128,1024]{1,0:T(8,128)(2,1)S(1)} %shard_map.62.refs_0_, ...), custom_call_target="tpu_custom_call" | custom-call | flops 872415232 | bytes 1048576 | tf_op jit(solution)/shard_map/pallas_call | solution.py:243
  113.8 5.0 %collective-permute-start.11 = (bf16[128,1024]{1,0:T(8,128)(2,1)S(1)}, bf16[128,1024]{1,0:T(8,128)(2,1)S(1)}, u32[]{:S(2)}, u32[]{:S(2)}) collective-permute-start(bf16[128,1024]{1,0:T(8,128)(2,1)S(1)} %shard_map.63.refs_0_), channel_id=1, source_target_pairs={{0,7},{1,0},{2,1},{3,2},{4,3},{5,4},{6,5},{7,6},{8,15},{9,8},{10,9... | collective-permute-start | bytes 786440 | tf_op jit(solution)/shard_map/ppermute | solution.py:344
  118.8 3.2 %shard_map.64.refs_8_ = bf16[128,1024]{1,0:T(8,128)(2,1)S(1)} custom-call(s32[104]{0:T(128)S(1)} %shard_map.55.slots_ref, bf16[2,5632,128]{2,1,0:T(8,128)(2,1)S(1)} %shard_map.57.pool_ref, bf16[1024,1024]{1,0:T(8,128)(2,1)S(1)} %copy-done, bf16[128,1024]{1,0:T(8,128)(2,1)S(1)} %shard_map.63.refs_0_, bf16[128,1024]{1,0:T(8,128)(2,1)S(1)} %collective-permute-done.7.refs_1_.refs_3_), custom_call_target="tpu_custom_call" | custom-call | flops 872415232 | bytes 1048576 | tf_op jit(solution)/shard_map/pallas_call | solution.py:243
  122.7 1.4 %shard_map.65 = bf16[128,8192]{1,0:T(8,128)(2,1)} custom-call(bf16[64,1024]{1,0:T(8,128)(2,1)S(1)} %collective-permute-done.4.refs_1_.refs_0_, bf16[64,1024]{1,0:T(8,128)(2,1)S(1)} %collective-permute-done.6.refs_2_.refs_1_, bf16[192,1024]{1,0:T(8,128)(2,1)S(1)} %collective-permute-done.5.refs_1_.refs_2_, ...), custom_call_target="tpu_custom_call" | custom-call | bytes 8388608 | tf_op jit(solution)/shard_map/pallas_call | solution.py:278
  (22 shorter events, 1.4 us)
Async XLA Ops:
  0.0 45.4 %copy-start.2 = (s32[1,4]{1,0:T(1,128)S(1)}, s32[1,4]{1,0:T(1,128)}, u32[]{:S(2)}) copy-start(s32[1,4]{1,0:T(1,128)} %verticals_ref.3) | copy-start | bytes 52
  0.0 45.4 %copy-start.3 = (s32[1,8]{1,0:T(1,128)S(1)}, s32[1,8]{1,0:T(1,128)}, u32[]{:S(2)}) copy-start(s32[1,8]{1,0:T(1,128)} %slashes_ref.1) | copy-start | bytes 100
  2.1 49.9 %copy-start.1 = (bf16[2,1024,128]{2,1,0:T(8,128)(2,1)S(1)}, bf16[2,1024,128]{2,1,0:T(8,128)(2,1)}, u32[]{:S(2)}) copy-start(bf16[2,1024,128]{2,1,0:T(8,128)(2,1)} %get-tuple-element.11.own_ref) | copy-start | bytes 1572868
  2.1 17.0 %all-to-all-start = ((bf16[8,128,128]{2,1,0:T(8,128)(2,1)}), bf16[8,128,128]{2,1,0:T(8,128)(2,1)S(1)}, u32[]{:S(2)}, u32[]{:S(2)}) async-start(bf16[8,128,128]{2,1,0:T(8,128)(2,1)} %bitcast.3), calls=%async_computation | async-start | bytes 524288 | tf_op jit(solution)/shard_map/all_to_all | solution.py:306
  12.5 11.2 %collective-permute-start.2 = (bf16[2,1024,128]{2,1,0:T(8,128)(2,1)}, bf16[2,1024,128]{2,1,0:T(8,128)(2,1)S(1)}, u32[]{:S(2)}, u32[]{:S(2)}) collective-permute-start(bf16[2,1024,128]{2,1,0:T(8,128)(2,1)} %get-tuple-element.11.own_ref), channel_id=1, source_target_pairs={{0,8},{8,48},{16,24},{24,0},{32,40},{40,80},{48,56},{56,32},{64,72... | collective-permute-start | bytes 1572872 | tf_op jit(solution)/shard_map/ppermute | solution.py:331
  17.2 21.7 %collective-permute-start = (bf16[2,1024,128]{2,1,0:T(8,128)(2,1)}, bf16[2,1024,128]{2,1,0:T(8,128)(2,1)S(1)}, u32[]{:S(2)}, u32[]{:S(2)}) collective-permute-start(bf16[2,1024,128]{2,1,0:T(8,128)(2,1)} %get-tuple-element.11.own_ref), channel_id=1, source_target_pairs={{0,16},{8,24},{16,32},{24,40},{32,48},{40,56},{48,64},{56,72},{64,... | collective-permute-start | bytes 1572872 | tf_op jit(solution)/shard_map/ppermute | solution.py:330
  20.0 14.0 %all-to-all-start.1 = ((bf16[8,128,128]{2,1,0:T(8,128)(2,1)}), bf16[8,128,128]{2,1,0:T(8,128)(2,1)S(1)}, u32[]{:S(2)}, u32[]{:S(2)}) async-start(bf16[8,128,128]{2,1,0:T(8,128)(2,1)} %broadcast_in_dim.4), calls=%async_computation.1 | async-start | bytes 524288 | tf_op jit(solution)/shard_map/all_to_all | solution.py:306
  23.7 28.3 %collective-permute-start.3 = (bf16[2,1024,128]{2,1,0:T(8,128)(2,1)S(1)}, bf16[2,1024,128]{2,1,0:T(8,128)(2,1)S(1)}, u32[]{:S(2)}, u32[]{:S(2)}) collective-permute-start(bf16[2,1024,128]{2,1,0:T(8,128)(2,1)S(1)} %collective-permute-done.2.halfway_ref), channel_id=1, source_target_pairs={{48,32},{0,48},{80,64},{32,80},{112,96},{64,112},{144,128},{96,144... | collective-permute-start | bytes 1572872 | tf_op jit(solution)/shard_map/ppermute | solution.py:334
  39.0 13.0 %collective-permute-start.1 = (bf16[2,1024,128]{2,1,0:T(8,128)(2,1)S(1)}, bf16[2,1024,128]{2,1,0:T(8,128)(2,1)S(1)}, u32[]{:S(2)}, u32[]{:S(2)}) collective-permute-start(bf16[2,1024,128]{2,1,0:T(8,128)(2,1)S(1)} %collective-permute-done.two_ref), channel_id=1, source_target_pairs={{0,8},{8,0},{16,24},{24,16},{32,40},{40,32},{48,56},{56,48},{64,72... | collective-permute-start | bytes 1572872 | tf_op jit(solution)/shard_map/ppermute | solution.py:333
  41.6 10.3 %all-to-all-start.2 = ((bf16[8,128,128]{2,1,0:T(8,128)(2,1)}), bf16[8,128,128]{2,1,0:T(8,128)(2,1)S(1)}, u32[]{:S(2)}, u32[]{:S(2)}) async-start(bf16[8,128,128]{2,1,0:T(8,128)(2,1)} %broadcast_in_dim.5), calls=%async_computation.2 | async-start | bytes 524288 | tf_op jit(solution)/shard_map/all_to_all | solution.py:306
  52.0 1.6 %copy-start = (bf16[1024,1024]{1,0:T(8,128)(2,1)S(1)}, bf16[1024,1024]{1,0:T(8,128)(2,1)}, u32[]{:S(2)}) copy-start(bf16[1024,1024]{1,0:T(8,128)(2,1)} %query_ref.13) | copy-start | bytes 6291460
  58.9 25.3 %collective-permute-start.5 = (bf16[192,1024]{1,0:T(8,128)(2,1)S(1)}, bf16[192,1024]{1,0:T(8,128)(2,1)S(1)}, u32[]{:S(2)}, u32[]{:S(2)}) collective-permute-start(bf16[192,1024]{1,0:T(8,128)(2,1)S(1)} %get-tuple-element.16), channel_id=1, source_target_pairs={{0,6},{1,7},{2,0},{3,1},{4,2},{5,3},{6,4},{7,5},{8,14},{9,15},{10,... | collective-permute-start | bytes 1179656 | tf_op jit(solution)/shard_map/ppermute | solution.py:344
  66.7 31.3 %collective-permute-start.4 = (bf16[64,1024]{1,0:T(8,128)(2,1)S(1)}, bf16[64,1024]{1,0:T(8,128)(2,1)S(1)}, u32[]{:S(2)}, u32[]{:S(2)}) collective-permute-start(bf16[64,1024]{1,0:T(8,128)(2,1)S(1)} %get-tuple-element.15.refs_0_), channel_id=1, source_target_pairs={{0,4},{1,5},{2,6},{3,7},{4,0},{5,1},{6,2},{7,3},{8,12},{9,13},{10,... | collective-permute-start | bytes 393224 | tf_op jit(solution)/shard_map/ppermute | solution.py:344
  71.8 47.0 %collective-permute-start.7 = (bf16[128,1024]{1,0:T(8,128)(2,1)S(1)}, bf16[128,1024]{1,0:T(8,128)(2,1)S(1)}, u32[]{:S(2)}, u32[]{:S(2)}) collective-permute-start(bf16[128,1024]{1,0:T(8,128)(2,1)S(1)} %shard_map.59.refs_0_), channel_id=1, source_target_pairs={{0,3},{1,4},{2,5},{3,6},{4,7},{5,0},{6,1},{7,2},{8,11},{9,12},{10,... | collective-permute-start | bytes 786440 | tf_op jit(solution)/shard_map/ppermute | solution.py:344
  80.1 41.9 %collective-permute-start.8 = (bf16[128,1024]{1,0:T(8,128)(2,1)S(1)}, bf16[128,1024]{1,0:T(8,128)(2,1)S(1)}, u32[]{:S(2)}, u32[]{:S(2)}) collective-permute-start(bf16[128,1024]{1,0:T(8,128)(2,1)S(1)} %shard_map.60.refs_0_), channel_id=1, source_target_pairs={{0,5},{1,6},{2,7},{3,0},{4,1},{5,2},{6,3},{7,4},{8,13},{9,14},{10,... | collective-permute-start | bytes 786440 | tf_op jit(solution)/shard_map/ppermute | solution.py:344
  84.2 26.4 %collective-permute-start.6 = (bf16[64,1024]{1,0:T(8,128)(2,1)S(1)}, bf16[64,1024]{1,0:T(8,128)(2,1)S(1)}, u32[]{:S(2)}, u32[]{:S(2)}) collective-permute-start(bf16[64,1024]{1,0:T(8,128)(2,1)S(1)} %slice.4), channel_id=1, source_target_pairs={{0,6},{1,7},{2,0},{3,1},{4,2},{5,3},{6,4},{7,5},{8,14},{9,15},{10,... | collective-permute-start | bytes 393224 | tf_op jit(solution)/shard_map/ppermute | solution.py:344
  92.9 29.1 %collective-permute-start.9 = (bf16[128,1024]{1,0:T(8,128)(2,1)S(1)}, bf16[128,1024]{1,0:T(8,128)(2,1)S(1)}, u32[]{:S(2)}, u32[]{:S(2)}) collective-permute-start(bf16[128,1024]{1,0:T(8,128)(2,1)S(1)} %shard_map.61.refs_0_), channel_id=1, source_target_pairs={{0,2},{1,3},{2,4},{3,5},{4,6},{5,7},{6,0},{7,1},{8,10},{9,11},{10,... | collective-permute-start | bytes 786440 | tf_op jit(solution)/shard_map/ppermute | solution.py:344
  98.0 24.0 %collective-permute-start.10 = (bf16[128,1024]{1,0:T(8,128)(2,1)S(1)}, bf16[128,1024]{1,0:T(8,128)(2,1)S(1)}, u32[]{:S(2)}, u32[]{:S(2)}) collective-permute-start(bf16[128,1024]{1,0:T(8,128)(2,1)S(1)} %shard_map.62.refs_0_), channel_id=1, source_target_pairs={{0,1},{1,2},{2,3},{3,4},{4,5},{5,6},{6,7},{7,0},{8,9},{9,10},{10,1... | collective-permute-start | bytes 786440 | tf_op jit(solution)/shard_map/ppermute | solution.py:344
  113.8 8.9 %collective-permute-start.11 = (bf16[128,1024]{1,0:T(8,128)(2,1)S(1)}, bf16[128,1024]{1,0:T(8,128)(2,1)S(1)}, u32[]{:S(2)}, u32[]{:S(2)}) collective-permute-start(bf16[128,1024]{1,0:T(8,128)(2,1)S(1)} %shard_map.63.refs_0_), channel_id=1, source_target_pairs={{0,7},{1,0},{2,1},{3,2},{4,3},{5,4},{6,5},{7,6},{8,15},{9,8},{10,9... | collective-permute-start | bytes 786440 | tf_op jit(solution)/shard_map/ppermute | solution.py:344

commit v7 on v6

--- a/solution.py
+++ b/solution.py
@@ -350,7 +350,7 @@
     lower = send(bundle[BLK:], BY_STEPS)
     pieces = [upper, lower, bundle]
     places = [(FAR_SIDE, 0, HALF), (FAR_SIDE, HALF, HALF), (BY_STEPS % planes, 0, BLK)]
-    arrived = {3: [bundle], 4: [upper, lower]}
+    arrived = {3: [bundle], 4: [upper]}
     for number, offset in enumerate(OFFSETS):
         (result,) = attend((offset,), after + arrived.get(number, []))
         after = [result]

time: 125 us -> 118 us (0.944)
  waiting for transfers between devices: 28.9 us -> 24.4 us
  starting transfers between devices: 62 us -> 58.6 us
    ppermute x8, waiting for transfers between devices: 9.44 us -> 4.95 us  [send(): lax.ppermute(block, 'kvh', [(s, (s + offset) % planes) for s in range(pla...]
    ppermute x8, starting transfers between devices: 35.1 us -> 31.7 us  [send(): lax.ppermute(block, 'kvh', [(s, (s + offset) % planes) for s in range(pla...]
  transfers between devices with their start and end apart: 15 -> 15, of which waited for: 6 -> 5; matrix products, arithmetic and copies ran while one was open for 1% -> 1% of each run, Pallas kernels for 17% -> 18%
where the time goes in v7:
time: 118 us; the launch traced here: 116 us
  starting transfers between devices  58.6 us (50%)
  Pallas kernels  30.1 us (26%)
  waiting for transfers between devices  24.4 us (21%)
  local copies, waits for them, and re-layouts  2.78 us (2%)
    ppermute x8, starting transfers between devices, send(): lax.ppermute(block, 'kvh', [(s, (s + offset) % planes) for s in range(pla...  31.7 us
    pallas_call x7, Pallas kernels, attend_call(): pl.pallas_call(functools.partial(attend_kernel, offsets, blocks), out_sha...  24.4 us
    all_to_all x3, starting transfers between devices, exchange(): lax.all_to_all(parts, 'ctx', split_axis=0, concat_axis=0, axis_index_grou...  17.6 us
    all_to_all x3, waiting for transfers between devices, exchange(): lax.all_to_all(parts, 'ctx', split_axis=0, concat_axis=0, axis_index_grou...  14.1 us
    ppermute x1, waiting for transfers between devices, shards(): two_back = lax.ppermute(key_value, 'ctx', first)  5.01 us
    ppermute x8, waiting for transfers between devices, send(): lax.ppermute(block, 'kvh', [(s, (s + offset) % planes) for s in range(pla...  4.95 us
    ppermute x1, starting transfers between devices, shards(): halfway = lax.ppermute(key_value, 'ctx', mixed)  4.77 us
  transfers between devices with their start and end apart: 15, of which 5 were waited for; matrix products, arithmetic and copies ran while one was open for 1% of the time, Pallas kernels for 18%

profile of v7, /device:TPU:1, one launch (start us, length us, event | category | flops | bytes accessed | tf_op | source)
XLA Modules:
  0.0 116.3 jit_solution(13578673668501494677)
XLA Ops:
  0.0 2.1 %shard_map.56 = (bf16[2,1024,128]{2,1,0:T(8,128)(2,1)}, bf16[2,512,128]{2,1,0:T(8,128)(2,1)}) custom-call(s32[1,4]{1,0:T(1,128)} %verticals_ref.3, bf16[1024,128]{1,0:T(8,128)(2,1)} %keys_ref.1, bf16[1024,128]{1,0:T(8,128)(2,1)} %values_ref.1), custom_call_target="tpu_custom_call" | custom-call | bytes 1048576 | tf_op jit(solution)/shard_map/pallas_call | solution.py:68
  2.1 10.3 %all-to-all-start = ((bf16[8,128,128]{2,1,0:T(8,128)(2,1)}), bf16[8,128,128]{2,1,0:T(8,128)(2,1)S(1)}, u32[]{:S(2)}, u32[]{:S(2)}) async-start(bf16[8,128,128]{2,1,0:T(8,128)(2,1)} %bitcast.3), calls=%async_computation | async-start | bytes 524288 | tf_op jit(solution)/shard_map/all_to_all | solution.py:306
  12.5 4.8 %collective-permute-start.2 = (bf16[2,1024,128]{2,1,0:T(8,128)(2,1)}, bf16[2,1024,128]{2,1,0:T(8,128)(2,1)S(1)}, u32[]{:S(2)}, u32[]{:S(2)}) collective-permute-start(bf16[2,1024,128]{2,1,0:T(8,128)(2,1)} %get-tuple-element.11.own_ref), channel_id=1, source_target_pairs={{0,8},{8,48},{16,24},{24,0},{32,40},{40,80},{48,56},{56,32},{64,72... | collective-permute-start | bytes 1572872 | tf_op jit(solution)/shard_map/ppermute | solution.py:331
  17.2 1.9 %collective-permute-start = (bf16[2,1024,128]{2,1,0:T(8,128)(2,1)}, bf16[2,1024,128]{2,1,0:T(8,128)(2,1)S(1)}, u32[]{:S(2)}, u32[]{:S(2)}) collective-permute-start(bf16[2,1024,128]{2,1,0:T(8,128)(2,1)} %get-tuple-element.11.own_ref), channel_id=1, source_target_pairs={{0,16},{8,24},{16,32},{24,40},{32,48},{40,56},{48,64},{56,72},{64,... | collective-permute-start | bytes 1572872 | tf_op jit(solution)/shard_map/ppermute | solution.py:330
  19.2 0.7 broadcast_in_dim.4
  20.0 3.4 %all-to-all-start.1 = ((bf16[8,128,128]{2,1,0:T(8,128)(2,1)}), bf16[8,128,128]{2,1,0:T(8,128)(2,1)S(1)}, u32[]{:S(2)}, u32[]{:S(2)}) async-start(bf16[8,128,128]{2,1,0:T(8,128)(2,1)} %broadcast_in_dim.4), calls=%async_computation.1 | async-start | bytes 524288 | tf_op jit(solution)/shard_map/all_to_all | solution.py:306
  23.7 0.7 collective-permute-start.3
  24.3 9.6 %all-to-all-done.1 = bf16[8,128,128]{2,1,0:T(8,128)(2,1)S(1)} async-done(((bf16[8,128,128]{2,1,0:T(8,128)(2,1)}), bf16[8,128,128]{2,1,0:T(8,128)(2,1)S(1)}, u32[]{:S(2)}, u32[]{:S(2)}) %all-to-all-start.1) | async-done | bytes 262176 | tf_op jit(solution)/shard_map/all_to_all | solution.py:306
  34.0 5.0 %collective-permute-done.two_ref = bf16[2,1024,128]{2,1,0:T(8,128)(2,1)S(1)} collective-permute-done((bf16[2,1024,128]{2,1,0:T(8,128)(2,1)}, bf16[2,1024,128]{2,1,0:T(8,128)(2,1)S(1)}, u32[]{:S(2)}, u32[]{:S(2)}) %collective-permute-start) | collective-permute-done | bytes 524320 | tf_op jit(solution)/shard_map/ppermute | solution.py:330
  39.0 1.9 %collective-permute-start.1 = (bf16[2,1024,128]{2,1,0:T(8,128)(2,1)S(1)}, bf16[2,1024,128]{2,1,0:T(8,128)(2,1)S(1)}, u32[]{:S(2)}, u32[]{:S(2)}) collective-permute-start(bf16[2,1024,128]{2,1,0:T(8,128)(2,1)S(1)} %collective-permute-done.two_ref), channel_id=1, source_target_pairs={{0,8},{8,0},{16,24},{24,16},{32,40},{40,32},{48,56},{56,48},{64,72... | collective-permute-start | bytes 1572872 | tf_op jit(solution)/shard_map/ppermute | solution.py:333
  40.9 0.7 broadcast_in_dim.5
  41.6 3.8 %all-to-all-start.2 = ((bf16[8,128,128]{2,1,0:T(8,128)(2,1)}), bf16[8,128,128]{2,1,0:T(8,128)(2,1)S(1)}, u32[]{:S(2)}, u32[]{:S(2)}) async-start(bf16[8,128,128]{2,1,0:T(8,128)(2,1)} %broadcast_in_dim.5), calls=%async_computation.2 | async-start | bytes 524288 | tf_op jit(solution)/shard_map/all_to_all | solution.py:306
  45.4 1.9 %shard_map.55.slots_ref = s32[104]{0:T(128)S(1)} custom-call(s32[1,4]{1,0:T(1,128)S(1)} %copy-done.2, s32[1,8]{1,0:T(1,128)S(1)} %copy-done.3), custom_call_target="tpu_custom_call" | custom-call | bytes 1048576 | tf_op jit(solution)/shard_map/pallas_call | solution.py:115
  47.4 4.6 %all-to-all-done.2 = bf16[8,128,128]{2,1,0:T(8,128)(2,1)S(1)} async-done(((bf16[8,128,128]{2,1,0:T(8,128)(2,1)}), bf16[8,128,128]{2,1,0:T(8,128)(2,1)S(1)}, u32[]{:S(2)}, u32[]{:S(2)}) %all-to-all-start.2) | async-done | bytes 262176 | tf_op jit(solution)/shard_map/all_to_all | solution.py:306
  52.3 1.3 %copy-done = bf16[1024,1024]{1,0:T(8,128)(2,1)S(1)} copy-done((bf16[1024,1024]{1,0:T(8,128)(2,1)S(1)}, bf16[1024,1024]{1,0:T(8,128)(2,1)}, u32[]{:S(2)}) %copy-start) | copy-done | bytes 2097176
  53.6 5.4 %shard_map.58 = (bf16[64,1024]{1,0:T(8,128)(2,1)S(1)}, bf16[192,1024]{1,0:T(8,128)(2,1)S(1)}) custom-call(s32[104]{0:T(128)S(1)} %shard_map.55.slots_ref, bf16[2,5632,128]{2,1,0:T(8,128)(2,1)S(1)} %shard_map.57.pool_ref, bf16[1024,1024]{1,0:T(8,128)(2,1)S(1)} %copy-done), custom_call_target="tpu_custom_call" | custom-call | flops 1744830464 | bytes 2097152 | tf_op jit(solution)/shard_map/pallas_call | solution.py:243
  58.9 7.8 %collective-permute-start.5 = (bf16[192,1024]{1,0:T(8,128)(2,1)S(1)}, bf16[192,1024]{1,0:T(8,128)(2,1)S(1)}, u32[]{:S(2)}, u32[]{:S(2)}) collective-permute-start(bf16[192,1024]{1,0:T(8,128)(2,1)S(1)} %get-tuple-element.16), channel_id=1, source_target_pairs={{0,6},{1,7},{2,0},{3,1},{4,2},{5,3},{6,4},{7,5},{8,14},{9,15},{10,... | collective-permute-start | bytes 1179656 | tf_op jit(solution)/shard_map/ppermute | solution.py:344
  66.7 1.9 %collective-permute-start.4 = (bf16[64,1024]{1,0:T(8,128)(2,1)S(1)}, bf16[64,1024]{1,0:T(8,128)(2,1)S(1)}, u32[]{:S(2)}, u32[]{:S(2)}) collective-permute-start(bf16[64,1024]{1,0:T(8,128)(2,1)S(1)} %get-tuple-element.15.refs_0_), channel_id=1, source_target_pairs={{0,4},{1,5},{2,6},{3,7},{4,0},{5,1},{6,2},{7,3},{8,12},{9,13},{10,... | collective-permute-start | bytes 393224 | tf_op jit(solution)/shard_map/ppermute | solution.py:344
  68.6 3.2 %shard_map.59.refs_0_ = bf16[128,1024]{1,0:T(8,128)(2,1)S(1)} custom-call(s32[104]{0:T(128)S(1)} %shard_map.55.slots_ref, bf16[2,5632,128]{2,1,0:T(8,128)(2,1)S(1)} %shard_map.57.pool_ref, bf16[1024,1024]{1,0:T(8,128)(2,1)S(1)} %copy-done, bf16[64,1024]{1,0:T(8,128)(2,1)S(1)} %get-tuple-element.15.refs_0_), custom_call_target="tpu_custom_call" | custom-call | flops 872415232 | bytes 1048576 | tf_op jit(solution)/shard_map/pallas_call | solution.py:243
  71.8 5.1 %collective-permute-start.7 = (bf16[128,1024]{1,0:T(8,128)(2,1)S(1)}, bf16[128,1024]{1,0:T(8,128)(2,1)S(1)}, u32[]{:S(2)}, u32[]{:S(2)}) collective-permute-start(bf16[128,1024]{1,0:T(8,128)(2,1)S(1)} %shard_map.59.refs_0_), channel_id=1, source_target_pairs={{0,3},{1,4},{2,5},{3,6},{4,7},{5,0},{6,1},{7,2},{8,11},{9,12},{10,... | collective-permute-start | bytes 786440 | tf_op jit(solution)/shard_map/ppermute | solution.py:344
  77.0 3.2 %shard_map.60.refs_0_ = bf16[128,1024]{1,0:T(8,128)(2,1)S(1)} custom-call(s32[104]{0:T(128)S(1)} %shard_map.55.slots_ref, bf16[2,5632,128]{2,1,0:T(8,128)(2,1)S(1)} %shard_map.57.pool_ref, bf16[1024,1024]{1,0:T(8,128)(2,1)S(1)} %copy-done, bf16[128,1024]{1,0:T(8,128)(2,1)S(1)} %shard_map.59.refs_0_), custom_call_target="tpu_custom_call" | custom-call | flops 872415232 | bytes 1048576 | tf_op jit(solution)/shard_map/pallas_call | solution.py:243
  80.1 4.2 %collective-permute-start.8 = (bf16[128,1024]{1,0:T(8,128)(2,1)S(1)}, bf16[128,1024]{1,0:T(8,128)(2,1)S(1)}, u32[]{:S(2)}, u32[]{:S(2)}) collective-permute-start(bf16[128,1024]{1,0:T(8,128)(2,1)S(1)} %shard_map.60.refs_0_), channel_id=1, source_target_pairs={{0,5},{1,6},{2,7},{3,0},{4,1},{5,2},{6,3},{7,4},{8,13},{9,14},{10,... | collective-permute-start | bytes 786440 | tf_op jit(solution)/shard_map/ppermute | solution.py:344
  84.4 3.2 %shard_map.61.refs_0_ = bf16[128,1024]{1,0:T(8,128)(2,1)S(1)} custom-call(s32[104]{0:T(128)S(1)} %shard_map.55.slots_ref, bf16[2,5632,128]{2,1,0:T(8,128)(2,1)S(1)} %shard_map.57.pool_ref, bf16[1024,1024]{1,0:T(8,128)(2,1)S(1)} %copy-done, bf16[128,1024]{1,0:T(8,128)(2,1)S(1)} %shard_map.60.refs_0_), custom_call_target="tpu_custom_call" | custom-call | flops 872415232 | bytes 1048576 | tf_op jit(solution)/shard_map/pallas_call | solution.py:243
  87.6 3.3 %collective-permute-start.9 = (bf16[128,1024]{1,0:T(8,128)(2,1)S(1)}, bf16[128,1024]{1,0:T(8,128)(2,1)S(1)}, u32[]{:S(2)}, u32[]{:S(2)}) collective-permute-start(bf16[128,1024]{1,0:T(8,128)(2,1)S(1)} %shard_map.61.refs_0_), channel_id=1, source_target_pairs={{0,2},{1,3},{2,4},{3,5},{4,6},{5,7},{6,0},{7,1},{8,10},{9,11},{10,... | collective-permute-start | bytes 786440 | tf_op jit(solution)/shard_map/ppermute | solution.py:344
  90.9 3.2 %shard_map.62.refs_0_ = bf16[128,1024]{1,0:T(8,128)(2,1)S(1)} custom-call(s32[104]{0:T(128)S(1)} %shard_map.55.slots_ref, bf16[2,5632,128]{2,1,0:T(8,128)(2,1)S(1)} %shard_map.57.pool_ref, bf16[1024,1024]{1,0:T(8,128)(2,1)S(1)} %copy-done, bf16[128,1024]{1,0:T(8,128)(2,1)S(1)} %shard_map.61.refs_0_, bf16[192,1024]{1,0:T(8,128)(2,1)S(1)} %collective-permute-done.5.refs_1_.refs_2_), custom_call_target="tpu_custom_call" | custom-call | flops 872415232 | bytes 1048576 | tf_op jit(solution)/shard_map/pallas_call | solution.py:243
  94.1 3.2 %shard_map.63.refs_0_ = bf16[128,1024]{1,0:T(8,128)(2,1)S(1)} custom-call(s32[104]{0:T(128)S(1)} %shard_map.55.slots_ref, bf16[2,5632,128]{2,1,0:T(8,128)(2,1)S(1)} %shard_map.57.pool_ref, bf16[1024,1024]{1,0:T(8,128)(2,1)S(1)} %copy-done, bf16[128,1024]{1,0:T(8,128)(2,1)S(1)} %shard_map.62.refs_0_, bf16[64,1024]{1,0:T(8,128)(2,1)S(1)} %collective-permute-done.4.refs_1_.refs_0_), custom_call_target="tpu_custom_call" | custom-call | flops 872415232 | bytes 1048576 | tf_op jit(solution)/shard_map/pallas_call | solution.py:243
  97.2 3.2 %collective-permute-start.11 = (bf16[128,1024]{1,0:T(8,128)(2,1)S(1)}, bf16[128,1024]{1,0:T(8,128)(2,1)S(1)}, u32[]{:S(2)}, u32[]{:S(2)}) collective-permute-start(bf16[128,1024]{1,0:T(8,128)(2,1)S(1)} %shard_map.63.refs_0_), channel_id=1, source_target_pairs={{0,7},{1,0},{2,1},{3,2},{4,3},{5,4},{6,5},{7,6},{8,15},{9,8},{10,9... | collective-permute-start | bytes 786440 | tf_op jit(solution)/shard_map/ppermute | solution.py:344
  100.4 2.1 %collective-permute-start.10 = (bf16[128,1024]{1,0:T(8,128)(2,1)S(1)}, bf16[128,1024]{1,0:T(8,128)(2,1)S(1)}, u32[]{:S(2)}, u32[]{:S(2)}) collective-permute-start(bf16[128,1024]{1,0:T(8,128)(2,1)S(1)} %shard_map.62.refs_0_), channel_id=1, source_target_pairs={{0,1},{1,2},{2,3},{3,4},{4,5},{5,6},{6,7},{7,0},{8,9},{9,10},{10,1... | collective-permute-start | bytes 786440 | tf_op jit(solution)/shard_map/ppermute | solution.py:344
  102.6 4.1 %collective-permute-start.6 = (bf16[64,1024]{1,0:T(8,128)(2,1)S(1)}, bf16[64,1024]{1,0:T(8,128)(2,1)S(1)}, u32[]{:S(2)}, u32[]{:S(2)}) collective-permute-start(bf16[64,1024]{1,0:T(8,128)(2,1)S(1)} %slice.4), channel_id=1, source_target_pairs={{0,6},{1,7},{2,0},{3,1},{4,2},{5,3},{6,4},{7,5},{8,14},{9,15},{10,... | collective-permute-start | bytes 393224 | tf_op jit(solution)/shard_map/ppermute | solution.py:344
  106.6 3.2 %shard_map.64.refs_8_ = bf16[128,1024]{1,0:T(8,128)(2,1)S(1)} custom-call(s32[104]{0:T(128)S(1)} %shard_map.55.slots_ref, bf16[2,5632,128]{2,1,0:T(8,128)(2,1)S(1)} %shard_map.57.pool_ref, bf16[1024,1024]{1,0:T(8,128)(2,1)S(1)} %copy-done, bf16[128,1024]{1,0:T(8,128)(2,1)S(1)} %shard_map.63.refs_0_, bf16[128,1024]{1,0:T(8,128)(2,1)S(1)} %collective-permute-done.7.refs_1_.refs_3_), custom_call_target="tpu_custom_call" | custom-call | flops 872415232 | bytes 1048576 | tf_op jit(solution)/shard_map/pallas_call | solution.py:243
  109.8 4.9 %collective-permute-done.6.refs_1_ = bf16[64,1024]{1,0:T(8,128)(2,1)S(1)} collective-permute-done((bf16[64,1024]{1,0:T(8,128)(2,1)S(1)}, bf16[64,1024]{1,0:T(8,128)(2,1)S(1)}, u32[]{:S(2)}, u32[]{:S(2)}) %collective-permute-start.6) | collective-permute-done | bytes 131104 | tf_op jit(solution)/shard_map/ppermute | solution.py:344
  114.8 1.4 %shard_map.65 = bf16[128,8192]{1,0:T(8,128)(2,1)} custom-call(bf16[64,1024]{1,0:T(8,128)(2,1)S(1)} %collective-permute-done.4.refs_1_.refs_0_, bf16[64,1024]{1,0:T(8,128)(2,1)S(1)} %collective-permute-done.6.refs_1_, bf16[192,1024]{1,0:T(8,128)(2,1)S(1)} %collective-permute-done.5.refs_1_.refs_2_, ...), custom_call_target="tpu_custom_call" | custom-call | bytes 8388608 | tf_op jit(solution)/shard_map/pallas_call | solution.py:278
  (22 shorter events, 0.7 us)
Async XLA Ops:
  0.0 45.4 %copy-start.2 = (s32[1,4]{1,0:T(1,128)S(1)}, s32[1,4]{1,0:T(1,128)}, u32[]{:S(2)}) copy-start(s32[1,4]{1,0:T(1,128)} %verticals_ref.3) | copy-start | bytes 52
  0.0 45.4 %copy-start.3 = (s32[1,8]{1,0:T(1,128)S(1)}, s32[1,8]{1,0:T(1,128)}, u32[]{:S(2)}) copy-start(s32[1,8]{1,0:T(1,128)} %slashes_ref.1) | copy-start | bytes 100
  2.1 49.9 %copy-start.1 = (bf16[2,1024,128]{2,1,0:T(8,128)(2,1)S(1)}, bf16[2,1024,128]{2,1,0:T(8,128)(2,1)}, u32[]{:S(2)}) copy-start(bf16[2,1024,128]{2,1,0:T(8,128)(2,1)} %get-tuple-element.11.own_ref) | copy-start | bytes 1572868
  2.1 17.0 %all-to-all-start = ((bf16[8,128,128]{2,1,0:T(8,128)(2,1)}), bf16[8,128,128]{2,1,0:T(8,128)(2,1)S(1)}, u32[]{:S(2)}, u32[]{:S(2)}) async-start(bf16[8,128,128]{2,1,0:T(8,128)(2,1)} %bitcast.3), calls=%async_computation | async-start | bytes 524288 | tf_op jit(solution)/shard_map/all_to_all | solution.py:306
  12.5 11.2 %collective-permute-start.2 = (bf16[2,1024,128]{2,1,0:T(8,128)(2,1)}, bf16[2,1024,128]{2,1,0:T(8,128)(2,1)S(1)}, u32[]{:S(2)}, u32[]{:S(2)}) collective-permute-start(bf16[2,1024,128]{2,1,0:T(8,128)(2,1)} %get-tuple-element.11.own_ref), channel_id=1, source_target_pairs={{0,8},{8,48},{16,24},{24,0},{32,40},{40,80},{48,56},{56,32},{64,72... | collective-permute-start | bytes 1572872 | tf_op jit(solution)/shard_map/ppermute | solution.py:331
  17.2 21.7 %collective-permute-start = (bf16[2,1024,128]{2,1,0:T(8,128)(2,1)}, bf16[2,1024,128]{2,1,0:T(8,128)(2,1)S(1)}, u32[]{:S(2)}, u32[]{:S(2)}) collective-permute-start(bf16[2,1024,128]{2,1,0:T(8,128)(2,1)} %get-tuple-element.11.own_ref), channel_id=1, source_target_pairs={{0,16},{8,24},{16,32},{24,40},{32,48},{40,56},{48,64},{56,72},{64,... | collective-permute-start | bytes 1572872 | tf_op jit(solution)/shard_map/ppermute | solution.py:330
  20.0 14.0 %all-to-all-start.1 = ((bf16[8,128,128]{2,1,0:T(8,128)(2,1)}), bf16[8,128,128]{2,1,0:T(8,128)(2,1)S(1)}, u32[]{:S(2)}, u32[]{:S(2)}) async-start(bf16[8,128,128]{2,1,0:T(8,128)(2,1)} %broadcast_in_dim.4), calls=%async_computation.1 | async-start | bytes 524288 | tf_op jit(solution)/shard_map/all_to_all | solution.py:306
  23.7 28.3 %collective-permute-start.3 = (bf16[2,1024,128]{2,1,0:T(8,128)(2,1)S(1)}, bf16[2,1024,128]{2,1,0:T(8,128)(2,1)S(1)}, u32[]{:S(2)}, u32[]{:S(2)}) collective-permute-start(bf16[2,1024,128]{2,1,0:T(8,128)(2,1)S(1)} %collective-permute-done.2.halfway_ref), channel_id=1, source_target_pairs={{48,32},{0,48},{80,64},{32,80},{112,96},{64,112},{144,128},{96,144... | collective-permute-start | bytes 1572872 | tf_op jit(solution)/shard_map/ppermute | solution.py:334
  39.0 13.0 %collective-permute-start.1 = (bf16[2,1024,128]{2,1,0:T(8,128)(2,1)S(1)}, bf16[2,1024,128]{2,1,0:T(8,128)(2,1)S(1)}, u32[]{:S(2)}, u32[]{:S(2)}) collective-permute-start(bf16[2,1024,128]{2,1,0:T(8,128)(2,1)S(1)} %collective-permute-done.two_ref), channel_id=1, source_target_pairs={{0,8},{8,0},{16,24},{24,16},{32,40},{40,32},{48,56},{56,48},{64,72... | collective-permute-start | bytes 1572872 | tf_op jit(solution)/shard_map/ppermute | solution.py:333
  41.6 10.3 %all-to-all-start.2 = ((bf16[8,128,128]{2,1,0:T(8,128)(2,1)}), bf16[8,128,128]{2,1,0:T(8,128)(2,1)S(1)}, u32[]{:S(2)}, u32[]{:S(2)}) async-start(bf16[8,128,128]{2,1,0:T(8,128)(2,1)} %broadcast_in_dim.5), calls=%async_computation.2 | async-start | bytes 524288 | tf_op jit(solution)/shard_map/all_to_all | solution.py:306
  52.0 1.6 %copy-start = (bf16[1024,1024]{1,0:T(8,128)(2,1)S(1)}, bf16[1024,1024]{1,0:T(8,128)(2,1)}, u32[]{:S(2)}) copy-start(bf16[1024,1024]{1,0:T(8,128)(2,1)} %query_ref.13) | copy-start | bytes 6291460
  58.9 31.9 %collective-permute-start.5 = (bf16[192,1024]{1,0:T(8,128)(2,1)S(1)}, bf16[192,1024]{1,0:T(8,128)(2,1)S(1)}, u32[]{:S(2)}, u32[]{:S(2)}) collective-permute-start(bf16[192,1024]{1,0:T(8,128)(2,1)S(1)} %get-tuple-element.16), channel_id=1, source_target_pairs={{0,6},{1,7},{2,0},{3,1},{4,2},{5,3},{6,4},{7,5},{8,14},{9,15},{10,... | collective-permute-start | bytes 1179656 | tf_op jit(solution)/shard_map/ppermute | solution.py:344
  66.7 27.4 %collective-permute-start.4 = (bf16[64,1024]{1,0:T(8,128)(2,1)S(1)}, bf16[64,1024]{1,0:T(8,128)(2,1)S(1)}, u32[]{:S(2)}, u32[]{:S(2)}) collective-permute-start(bf16[64,1024]{1,0:T(8,128)(2,1)S(1)} %get-tuple-element.15.refs_0_), channel_id=1, source_target_pairs={{0,4},{1,5},{2,6},{3,7},{4,0},{5,1},{6,2},{7,3},{8,12},{9,13},{10,... | collective-permute-start | bytes 393224 | tf_op jit(solution)/shard_map/ppermute | solution.py:344
  71.8 30.8 %collective-permute-start.7 = (bf16[128,1024]{1,0:T(8,128)(2,1)S(1)}, bf16[128,1024]{1,0:T(8,128)(2,1)S(1)}, u32[]{:S(2)}, u32[]{:S(2)}) collective-permute-start(bf16[128,1024]{1,0:T(8,128)(2,1)S(1)} %shard_map.59.refs_0_), channel_id=1, source_target_pairs={{0,3},{1,4},{2,5},{3,6},{4,7},{5,0},{6,1},{7,2},{8,11},{9,12},{10,... | collective-permute-start | bytes 786440 | tf_op jit(solution)/shard_map/ppermute | solution.py:344
  80.1 29.7 %collective-permute-start.8 = (bf16[128,1024]{1,0:T(8,128)(2,1)S(1)}, bf16[128,1024]{1,0:T(8,128)(2,1)S(1)}, u32[]{:S(2)}, u32[]{:S(2)}) collective-permute-start(bf16[128,1024]{1,0:T(8,128)(2,1)S(1)} %shard_map.60.refs_0_), channel_id=1, source_target_pairs={{0,5},{1,6},{2,7},{3,0},{4,1},{5,2},{6,3},{7,4},{8,13},{9,14},{10,... | collective-permute-start | bytes 786440 | tf_op jit(solution)/shard_map/ppermute | solution.py:344
  87.6 22.3 %collective-permute-start.9 = (bf16[128,1024]{1,0:T(8,128)(2,1)S(1)}, bf16[128,1024]{1,0:T(8,128)(2,1)S(1)}, u32[]{:S(2)}, u32[]{:S(2)}) collective-permute-start(bf16[128,1024]{1,0:T(8,128)(2,1)S(1)} %shard_map.61.refs_0_), channel_id=1, source_target_pairs={{0,2},{1,3},{2,4},{3,5},{4,6},{5,7},{6,0},{7,1},{8,10},{9,11},{10,... | collective-permute-start | bytes 786440 | tf_op jit(solution)/shard_map/ppermute | solution.py:344
  97.2 17.5 %collective-permute-start.11 = (bf16[128,1024]{1,0:T(8,128)(2,1)S(1)}, bf16[128,1024]{1,0:T(8,128)(2,1)S(1)}, u32[]{:S(2)}, u32[]{:S(2)}) collective-permute-start(bf16[128,1024]{1,0:T(8,128)(2,1)S(1)} %shard_map.63.refs_0_), channel_id=1, source_target_pairs={{0,7},{1,0},{2,1},{3,2},{4,3},{5,4},{6,5},{7,6},{8,15},{9,8},{10,9... | collective-permute-start | bytes 786440 | tf_op jit(solution)/shard_map/ppermute | solution.py:344
  100.4 14.4 %collective-permute-start.10 = (bf16[128,1024]{1,0:T(8,128)(2,1)S(1)}, bf16[128,1024]{1,0:T(8,128)(2,1)S(1)}, u32[]{:S(2)}, u32[]{:S(2)}) collective-permute-start(bf16[128,1024]{1,0:T(8,128)(2,1)S(1)} %shard_map.62.refs_0_), channel_id=1, source_target_pairs={{0,1},{1,2},{2,3},{3,4},{4,5},{5,6},{6,7},{7,0},{8,9},{9,10},{10,1... | collective-permute-start | bytes 786440 | tf_op jit(solution)/shard_map/ppermute | solution.py:344
  102.6 12.2 %collective-permute-start.6 = (bf16[64,1024]{1,0:T(8,128)(2,1)S(1)}, bf16[64,1024]{1,0:T(8,128)(2,1)S(1)}, u32[]{:S(2)}, u32[]{:S(2)}) collective-permute-start(bf16[64,1024]{1,0:T(8,128)(2,1)S(1)} %slice.4), channel_id=1, source_target_pairs={{0,6},{1,7},{2,0},{3,1},{4,2},{5,3},{6,4},{7,5},{8,14},{9,15},{10,... | collective-permute-start | bytes 393224 | tf_op jit(solution)/shard_map/ppermute | solution.py:344
